TPU v7x, 128 devices: a whole 4x4x4 slice. The times are simulated.
128 devices in a mesh: seq: 16 (over z_hi, y, core), tensor: 8 (over x, z_lo).
Axes of the slice: x: 4, y: 4, z: 4 (z_hi: 2, z_lo: 2; z = z_hi * 2 + z_lo), core: 2. Of those that a mesh axis runs over, the one named last changes fastest.
Arguments:
- query_states: bfloat16 [16384, 8192], P('seq', 'tensor'), may hold values from -6 to 6
- key_states: bfloat16 [16384, 1024], P('seq', 'tensor'), may hold values from -6 to 6
- value_states: bfloat16 [16384, 1024], P('seq', 'tensor'), may hold values from -6 to 6
- grad_output: bfloat16 [16384, 8192], P('seq', 'tensor'), may hold values from -6 to 6
- normed_layer_input: bfloat16 [16384, 8192], P('seq', 'tensor'), may hold values from -6 to 6
- query_down: bfloat16 [16, 8192], P(None, 'tensor'), may hold values from -0.0625 to 0.0625
- query_up: bfloat16 [16, 8192], P(None, 'tensor'), may hold values from -1.5 to 1.5
- value_down: bfloat16 [16, 8192], P(None, 'tensor'), may hold values from -0.0625 to 0.0625
- value_up: bfloat16 [16, 1024], P(None, 'tensor'), may hold values from -1.5 to 1.5
Outputs:
- query_gradient: bfloat16 [16384, 8192], P('seq', 'tensor')
- grad_key: bfloat16 [16384, 1024], P('seq', 'tensor')
- value_gradient: bfloat16 [16384, 1024], P('seq', 'tensor')
- query_down_gradient: float32 [16, 8192], P(None, 'tensor')
- query_up_gradient: float32 [16, 8192], P(None, 'tensor')
- value_down_gradient: float32 [16, 8192], P(None, 'tensor')
- value_up_gradient: float32 [16, 1024], P(None, 'tensor')
All inputs are finite; a program needn't handle non-finite values.
Results may differ from a plain program's by a relative error of at most 0.012.
Values may be sent and summed in bfloat16 or wider, within the bound.
No kernel may reach another device: no remote copies, remote signals or barrier semaphores. Data moves between devices by JAX's collectives and lax.ppermute only.
A program may use at most 192 MiB of HBM per device.

v0:
```python
import math

import jax
import jax.numpy as jnp
from jax import lax
from jax.sharding import PartitionSpec as P

HEADS = 64
KV = 8
HD = 128


adapter_scale = 2.0
masked = -1e30


def shifted(value, axis, steps):
    count = lax.axis_size(axis)
    pairs = [(source, (source + steps) % count) for source in range(count)]
    return lax.ppermute(value, axis, pairs)


def attend_back(queries, key_rows, value_rows, cotangent):
    factor = 1.0 / math.sqrt(queries.shape[-1])
    scores = (
        jnp.einsum("qjhe,kje->jhqk", queries, key_rows, preferred_element_type=jnp.float32) * factor
    )
    query_pos = jnp.arange(queries.shape[0])
    key_pos = jnp.arange(key_rows.shape[0])
    allowed = query_pos[:, None] >= key_pos[None, :]
    scores = jnp.where(allowed, scores, masked)
    highest = jnp.max(scores, axis=-1, keepdims=True)
    weights = jnp.exp(scores - highest)
    chances = weights / jnp.sum(weights, axis=-1, keepdims=True)
    chances_low = chances.astype(jnp.bfloat16)
    attended = jnp.einsum(
        "jhqk,kje->qjhe", chances_low, value_rows, preferred_element_type=jnp.float32
    )
    delta = jnp.einsum("qjhe,qjhe->jhq", cotangent.astype(jnp.float32), attended)
    dprob = jnp.einsum("qjhe,kje->jhqk", cotangent, value_rows, preferred_element_type=jnp.float32)
    dscore = (chances * (dprob - delta[..., None])).astype(jnp.bfloat16)
    grad_q = (
        jnp.einsum("jhqk,kje->qjhe", dscore, key_rows, preferred_element_type=jnp.float32) * factor
    )
    grad_k = (
        jnp.einsum("jhqk,qjhe->kje", dscore, queries, preferred_element_type=jnp.float32) * factor
    )
    grad_v = jnp.einsum(
        "jhqk,qjhe->kje", chances_low, cotangent, preferred_element_type=jnp.float32
    )
    return (grad_q, grad_k, grad_v)


def on_device(
    query_states,
    key_states,
    value_states,
    grad_output,
    normed_layer_input,
    query_down,
    query_up,
    value_down,
    value_up,
):
    length = query_states.shape[0]
    midpoint = length // 2
    kv_local = key_states.shape[1] // HD
    group_heads = HEADS // KV
    steady = group_heads // 2
    query_heads = query_states.reshape(length, kv_local, group_heads, HD)
    cot_heads = grad_output.reshape(length, kv_local, group_heads, HD)
    key_heads = key_states.reshape(length, kv_local, HD)
    value_heads = value_states.reshape(length, kv_local, HD)
    query_reduced, value_reduced = lax.psum(
        (
            jnp.dot(normed_layer_input, query_down.T, preferred_element_type=jnp.float32),
            jnp.dot(normed_layer_input, value_down.T, preferred_element_type=jnp.float32),
        ),
        "tensor",
    )
    query_reduced = query_reduced.astype(jnp.bfloat16)
    value_reduced = value_reduced.astype(jnp.bfloat16)
    grad_q_plain, grad_k_plain, grad_v_plain = attend_back(
        query_heads[:, :, :steady], key_heads, value_heads, cot_heads[:, :, :steady]
    )
    moved_query = query_heads[:, :, steady:]
    moved_cot = cot_heads[:, :, steady:]
    incoming = shifted(
        (
            moved_query[:midpoint],
            key_heads[:midpoint],
            value_heads[:midpoint],
            moved_cot[:midpoint],
        ),
        "seq",
        -1,
    )
    group_query = jnp.concatenate([moved_query[midpoint:], incoming[0]], axis=0)
    group_keys = jnp.concatenate([key_heads[midpoint:], incoming[1]], axis=0)
    group_values = jnp.concatenate([value_heads[midpoint:], incoming[2]], axis=0)
    group_cot = jnp.concatenate([moved_cot[midpoint:], incoming[3]], axis=0)
    grad_q_roll, grad_k_roll, grad_v_roll = attend_back(
        group_query, group_keys, group_values, group_cot
    )
    returned = shifted(
        (grad_q_roll[midpoint:], grad_k_roll[midpoint:], grad_v_roll[midpoint:]), "seq", 1
    )
    grad_q_moved = jnp.concatenate([returned[0], grad_q_roll[:midpoint]], axis=0).astype(
        jnp.bfloat16
    )
    grad_k_moved = jnp.concatenate([returned[1], grad_k_roll[:midpoint]], axis=0)
    grad_v_moved = jnp.concatenate([returned[2], grad_v_roll[:midpoint]], axis=0)
    query_gradient = jnp.concatenate(
        [grad_q_plain.astype(jnp.bfloat16), grad_q_moved], axis=2
    ).reshape(length, kv_local * group_heads * HD)
    grad_key = (grad_k_plain + grad_k_moved).reshape(length, kv_local * HD).astype(jnp.bfloat16)
    value_gradient = (
        (grad_v_plain + grad_v_moved).reshape(length, kv_local * HD).astype(jnp.bfloat16)
    )
    partial_query_up = adapter_scale * jnp.dot(
        query_reduced.T, query_gradient, preferred_element_type=jnp.float32
    )
    partial_value_up = adapter_scale * jnp.dot(
        value_reduced.T, value_gradient, preferred_element_type=jnp.float32
    )
    query_backward, value_backward = lax.psum(
        (
            jnp.dot(query_gradient, query_up.T, preferred_element_type=jnp.float32),
            jnp.dot(value_gradient, value_up.T, preferred_element_type=jnp.float32),
        ),
        "tensor",
    )
    query_backward = query_backward.astype(jnp.bfloat16)
    value_backward = value_backward.astype(jnp.bfloat16)
    partial_query_down = adapter_scale * jnp.dot(
        query_backward.T, normed_layer_input, preferred_element_type=jnp.float32
    )
    partial_value_down = adapter_scale * jnp.dot(
        value_backward.T, normed_layer_input, preferred_element_type=jnp.float32
    )
    query_down_gradient, query_up_gradient, value_down_gradient, value_up_gradient = lax.psum(
        (partial_query_down, partial_query_up, partial_value_down, partial_value_up), "seq"
    )
    return (
        query_gradient,
        grad_key,
        value_gradient,
        query_down_gradient,
        query_up_gradient,
        value_down_gradient,
        value_up_gradient,
    )


def solution(mesh):
    return jax.shard_map(
        on_device,
        mesh=mesh,
        in_specs=(
            P("seq", "tensor"),
            P("seq", "tensor"),
            P("seq", "tensor"),
            P("seq", "tensor"),
            P("seq", "tensor"),
            P(None, "tensor"),
            P(None, "tensor"),
            P(None, "tensor"),
            P(None, "tensor"),
        ),
        out_specs=(
            P("seq", "tensor"),
            P("seq", "tensor"),
            P("seq", "tensor"),
            P(None, "tensor"),
            P(None, "tensor"),
            P(None, "tensor"),
            P(None, "tensor"),
        ),
        check_vma=False,
    )
```

profile of v0, /device:TPU:1, one launch (start us, length us, event | category | flops | bytes accessed | tf_op | source)
XLA Modules:
  0.0 408.5 jit_solution(1872639672412643408)
XLA Ops:
  7.2 0.0 copy-start
  7.2 0.0 all-reduce.5.cloned.1.call-start
  7.2 4.1 %copy.30 = bf16[1024,1024]{0,1:T(8,128)(2,1)} copy(bf16[1024,1024]{1,0:T(8,128)(2,1)} %param.9) | data formatting | bytes 4194304 | tf_op args[0]
  11.3 2.1 fusion.98
  13.4 1.0 copy.85
  14.4 1.4 collective-permute-start.1
  15.8 1.6 slice_bitcast_fusion.8
  17.5 5.8 %collective-permute-start = (bf16[512,1,128]{2,0,1:T(8,128)(2,1)}, bf16[512,1,128]{2,0,1:T(8,128)(2,1)}, u32[]{:S(2)}, u32[]{:S(2)}) collective-permute-start(bf16[512,1,128]{2,0,1:T(8,128)(2,1)} %get-tuple-element.41), channel_id=1, source_target_pairs={{0,120},{8,0},{16,8},{24,16},{32,24},{40,32},{48,40},{56,48},{64,5... | collective-permute-start | bytes 393224 | tf_op jit(solution)/shard_map/ppermute | solution.py:20
  23.3 3.9 copy.32
  27.3 2.1 fusion.99
  29.4 1.0 copy.87
  30.4 0.7 collective-permute-start.3
  31.0 0.7 slice_bitcast_fusion.6
  31.8 0.2 collective-permute-start.2
  32.0 0.3 iota_compare_fusion
  32.3 0.0 copy-start.20
  32.3 0.0 copy-start.2
  32.3 10.9 %fusion.8 = (f32[4,1024]{1,0:T(4,128)}, f32[1024,1024,4]{1,0,2:T(8,128)}) fusion(pred[1024,1024]{0,1:T(8,128)(4,1)S(1)} %iota_compare_fusion, bf16[1024,1,8,128]{0,3,2,1:T(8,128)(2,1)} %bitcast.278, bf16[1024,128]{1,0:T(8,128)(2,1)} %param.10), kind=kOutput, calls=%fused_computation.14 | convolution fusion | flops 1086320640 | bytes 19152896 | tf_op jit(solution)/shard_map/qjhe,kje->jhqk/dot_general | solution.py:26
  43.2 1.5 fusion.104
  44.7 1.5 fusion.106
  46.1 1.1 slice.88
  47.2 2.1 copy.84
  49.3 2.1 copy.86
  51.3 2.8 copy.83
  54.1 14.1 %fusion.5 = (f32[4,1024]{1,0:T(4,128)S(1)}, f32[4,1024]{1,0:T(4,128)S(1)}, f32[1024,1024,4]{1,0,2:T(8,128)}) fusion(f32[1024,1024,4]{1,0,2:T(8,128)} %get-tuple-element.45, f32[4,1024]{1,0:T(4,128)} %get-tuple-element.44, pred[1024,1024]{0,1:T(8,128)(4,1)S(1)} %iota_compare_fusion, bf16[512,1,4,128]{3,0,2,1:T(8,128)(2,1)} %collective-permute-done.1, ...), kind=kOutput, calls=%fused_computation.11 | convolution fusion | flops 1105715200 | bytes 35962880 | tf_op jit(solution)/shard_map/qjhe,kje->jhqk/dot_general | solution.py:26
  68.2 0.0 copy-start.28
  68.2 8.5 %fusion.7 = f32[4,1024]{1,0:T(4,128)S(1)} fusion(f32[1024,1024,4]{1,0,2:T(8,128)} %get-tuple-element.46, f32[4,1024]{1,0:T(4,128)S(1)} %get-tuple-element.22, pred[1024,1024]{0,1:T(8,128)(4,1)S(1)} %iota_compare_fusion), kind=kLoop, calls=%fused_computation.13 | loop fusion | flops 16773120 | bytes 17858560 | tf_op jit(solution)/shard_map/reduce_sum | solution.py:34
  76.8 2.1 copy-done.1
  78.9 0.0 copy-done.7
  78.9 5.5 %fusion.44 = f32[1024,1,128]{2,0,1:T(8,128)S(1)} fusion(bf16[512,1,4,128]{3,0,2,1:T(8,128)(2,1)} %collective-permute-done.3, bf16[512,1,4,128]{3,0,2,1:T(8,128)(2,1)S(1)} %copy-done.7, f32[4,1024]{1,0:T(4,128)S(1)} %fusion.7, f32[4,1024]{1,0:T(4,128)S(1)} %get-tuple-element.22, f32[1024,1024,4]{1,0,2:T(8,128)S(1)} %copy-done.1, ...), kind=kOutput, calls=%fused_computation.44 | convolution fusion | flops 1096810496 | bytes 19431424 | tf_op jit(solution)/shard_map/jhqk,qjhe->kje/dot_general | solution.py:48
  84.5 0.8 fusion.101
  85.3 1.6 collective-permute-start.6
  86.9 9.0 %multiply_reduce_fusion = f32[4,1024]{1,0:T(4,128)S(1)} fusion(bf16[1024,1,4,128]{3,0,2,1:T(8,128)(2,1)S(1)} %copy-done.11, bf16[1024,128]{1,0:T(8,128)(2,1)S(1)} %copy-done.16, f32[4,1024]{1,0:T(4,128)S(1)} %get-tuple-element.21, f32[4,1024]{1,0:T(4,128)S(1)} %copy-done.26, f32[1024,1024,4]{1,0,2:T(8,128)} %get-tuple-element.45, ...), kind=kOutput, calls=%fused_computation.38 | convolution fusion | flops 1096282112 | bytes 19185664 | tf_op jit(solution)/shard_map/jhqk,kje->qjhe/dot_general | solution.py:36
  95.9 11.6 %fusion.3 = bf16[1,4,1024,1024]{2,3,1,0:T(8,128)(2,1)} fusion(f32[4,1024]{1,0:T(4,128)S(1)} %multiply_reduce_fusion, f32[4,1024]{1,0:T(4,128)S(1)} %get-tuple-element.21, f32[4,1024]{1,0:T(4,128)S(1)} %copy-done.26, f32[1024,1024,4]{1,0,2:T(8,128)} %get-tuple-element.45, pred[1024,1024]{0,1:T(8,128)(4,1)S(1)} %iota_compare_fusion, ...), kind=kOutput, calls=%fused_computation.6 | convolution fusion | flops 1103101952 | bytes 27574272 | tf_op jit(solution)/shard_map/qjhe,kje->jhqk/dot_general | solution.py:40
  107.4 6.9 %fusion.35 = bf16[1024,1,4,128]{0,3,2,1:T(8,128)(2,1)} fusion(bf16[1,4,1024,1024]{2,3,1,0:T(8,128)(2,1)} %fusion.3, bf16[1024,128]{1,0:T(8,128)(2,1)S(1)} %copy-done.17), kind=kOutput, calls=%fused_computation.41 | convolution fusion | flops 1074790400 | bytes 9699328 | tf_op jit(solution)/shard_map/jhqk,kje->qjhe/dot_general | solution.py:43
  114.3 2.5 bitcast_convert_fusion
  116.8 2.9 copy.68
  119.8 8.9 %fusion.16 = f32[128,4,1024]{2,0,1:T(8,128)S(1)} fusion(bf16[512,1,128]{2,0,1:T(8,128)(2,1)} %collective-permute-done.2, bf16[512,1,128]{2,0,1:T(8,128)(2,1)S(1)} %copy-done.19, f32[4,1024]{1,0:T(4,128)S(1)} %copy-done.24, f32[4,1024]{1,0:T(4,128)S(1)} %get-tuple-element.22, f32[1024,1024,4]{1,0,2:T(8,128)} %get-tuple-element.46, ...), kind=kOutput, calls=%fused_computation.22 | convolution fusion | flops 1095237632 | bytes 20217856 | tf_op jit(solution)/shard_map/jhqk,kje->qjhe/dot_general | solution.py:36
  128.7 0.5 fusion.28
  129.2 10.6 %fusion.1 = bf16[1,4,1024,1024]{2,3,1,0:T(8,128)(2,1)S(1)} fusion(f32[4,1024]{1,0:T(4,128)S(1)} %fusion.28, f32[4,1024]{1,0:T(4,128)S(1)} %copy-done.24, f32[4,1024]{1,0:T(4,128)S(1)} %get-tuple-element.22, f32[1024,1024,4]{1,0,2:T(8,128)} %get-tuple-element.46, pred[1024,1024]{0,1:T(8,128)(4,1)S(1)} %iota_compare_fusion, ...), kind=kOutput, calls=%fused_computation.2 | convolution fusion | flops 1105723392 | bytes 27574272 | tf_op jit(solution)/shard_map/qjhe,kje->jhqk/dot_general | solution.py:40
  139.8 2.3 multiply_bitcast_fusion
  142.1 0.0 copy-start.18
  142.1 0.0 copy-start.27
  142.1 0.1 fusion.100
  142.2 0.1 collective-permute-start.4
  142.3 3.5 fusion.53
  145.9 0.1 collective-permute-start.5
  146.0 8.6 %fusion.70 = bf16[1024,128]{1,0:T(8,128)(2,1)S(1)} fusion(f32[512,1,128]{2,0,1:T(8,128)S(1)} %copy-done.18, f32[512,1,128]{2,0,1:T(8,128)} %collective-permute-done.6, bf16[1024,1,8,128]{0,3,2,1:T(8,128)(2,1)S(1)} %bitcast.276, f32[4,1024]{1,0:T(4,128)S(1)} %copy-done.29, f32[4,1024]{1,0:T(4,128)S(1)} %copy-done.27, ...), kind=kOutput, calls=%fused_computation.69 | convolution fusion | flops 1095106560 | bytes 19693568 | tf_op jit(solution)/shard_map/jhqk,qjhe->kje/dot_general | solution.py:48
  154.7 0.2 fusion.105
  155.0 3.0 fusion.71
  158.0 1.6 maximum_maximum_fusion
  159.6 3.9 copy.51
  163.5 3.1 fusion.103
  166.7 84.3 %all-reduce.6 = (bf16[1024,16]{1,0:T(8,128)(2,1)}, bf16[1024,16]{1,0:T(8,128)(2,1)}, bf16[1024,16]{1,0:T(8,128)(2,1)}, bf16[1024,16]{1,0:T(8,128)(2,1)}) all-reduce(f32[1024,16]{1,0:T(8,128)} %fusion.103, f32[1024,16]{1,0:T(8,128)S(1)} %copy-done.9, f32[1024,16]{1,0:T(8,128)S(1)} %fusion.105, ...), channel_id=1, replica_groups=mesh['seq'=16,'tensor'=8] {'tensor'}, use_global_device_ids=true, to_apply=%region_4.5 | all-reduce | flops 65536 | bytes 393216 | tf_op jit(solution)/shard_map/psum | solution.py:126
  250.9 3.0 convolution_multiply_fusion.1
  253.9 2.0 convolution_multiply_fusion
  255.9 2.0 convolution_multiply_fusion.2
  257.9 0.0 all-reduce.5.cloned.1.call-update
  257.9 1.2 convolution_multiply_fusion.3
  259.1 43.9 %psum.63 = f32[16,128]{1,0:T(8,128)} all-reduce(f32[16,128]{1,0:T(8,128)S(1)} %convolution_multiply_fusion.3), channel_id=1, replica_groups=mesh['seq'=16,'tensor'=8] {'seq'}, use_global_device_ids=true, to_apply=%region_11.12 | all-reduce | flops 2048 | bytes 16384 | tf_op jit(solution)/shard_map/psum | solution.py:141
  303.0 94.0 %all-reduce.5.cloned.1.call-done = (f32[16,1024]{1,0:T(8,128)}, f32[16,1024]{1,0:T(8,128)}, f32[16,1024]{1,0:T(8,128)}) async-done(((f32[16,1024]{1,0:T(8,128)}, f32[16,1024]{1,0:T(8,128)}, f32[16,1024]{1,0:T(8,128)}), (f32[16,1024]{1,0:T(8,128)}, f32[16,1024]{1,0:T(8,128)}, f32[16,1024]{1,0:T(8,128)})) %all-reduce.5.cloned.1.call-update) | async-done | bytes 196624 | tf_op jit(solution)/shard_map/psum | solution.py:141
  397.0 1.5 copy.99
  398.5 1.5 copy.100
  400.0 1.5 copy.101
  (65 shorter events, 0.2 us)
Async XLA Ops:
  7.2 36.0 %copy-start = (bf16[1024,1024]{1,0:T(8,128)(2,1)S(1)}, bf16[1024,1024]{1,0:T(8,128)(2,1)}, u32[]{:S(2)}) copy-start(bf16[1024,1024]{1,0:T(8,128)(2,1)} %param.13) | copy-start | bytes 6291460
  7.2 23.9 %copy-start.16 = (bf16[1024,128]{1,0:T(8,128)(2,1)S(1)}, bf16[1024,128]{1,0:T(8,128)(2,1)}, u32[]{:S(2)}) copy-start(bf16[1024,128]{1,0:T(8,128)(2,1)} %param.11) | copy-start | bytes 786436
  7.2 389.8 %all-reduce.5.cloned.1.call-start = ((), (), s32[]{:S(2)}) async-start(), calls=%async_computation | async-start | bytes 393216 | tf_op jit(solution)/shard_map/psum | solution.py:141
  14.4 39.7 %collective-permute-start.1 = (bf16[512,1,4,128]{3,0,2,1:T(8,128)(2,1)}, bf16[512,1,4,128]{3,0,2,1:T(8,128)(2,1)}, u32[]{:S(2)}, u32[]{:S(2)}) collective-permute-start(bf16[512,1,4,128]{3,0,2,1:T(8,128)(2,1)} %copy.85), channel_id=1, source_target_pairs={{0,120},{8,0},{16,8},{24,16},{32,24},{40,32},{48,40},{56,48},{64,5... | collective-permute-start | bytes 1572872 | tf_op jit(solution)/shard_map/ppermute | solution.py:20
  17.5 36.6 %copy-start.13 = (bf16[512,1,128]{2,0,1:T(8,128)(2,1)}, bf16[512,1,128]{2,0,1:T(8,128)(2,1)S(1)}, u32[]{:S(2)}) copy-start(bf16[512,1,128]{2,0,1:T(8,128)(2,1)S(1)} %get-tuple-element.40) | copy-start | bytes 393220
  17.5 36.6 %collective-permute-start = (bf16[512,1,128]{2,0,1:T(8,128)(2,1)}, bf16[512,1,128]{2,0,1:T(8,128)(2,1)}, u32[]{:S(2)}, u32[]{:S(2)}) collective-permute-start(bf16[512,1,128]{2,0,1:T(8,128)(2,1)} %get-tuple-element.41), channel_id=1, source_target_pairs={{0,120},{8,0},{16,8},{24,16},{32,24},{40,32},{48,40},{56,48},{64,5... | collective-permute-start | bytes 393224 | tf_op jit(solution)/shard_map/ppermute | solution.py:20
  30.4 46.4 %collective-permute-start.3 = (bf16[512,1,4,128]{3,0,2,1:T(8,128)(2,1)}, bf16[512,1,4,128]{3,0,2,1:T(8,128)(2,1)}, u32[]{:S(2)}, u32[]{:S(2)}) collective-permute-start(bf16[512,1,4,128]{3,0,2,1:T(8,128)(2,1)} %copy.87), channel_id=1, source_target_pairs={{0,120},{8,0},{16,8},{24,16},{32,24},{40,32},{48,40},{56,48},{64,5... | collective-permute-start | bytes 1572872 | tf_op jit(solution)/shard_map/ppermute | solution.py:20
  31.8 88.0 %collective-permute-start.2 = (bf16[512,1,128]{2,0,1:T(8,128)(2,1)}, bf16[512,1,128]{2,0,1:T(8,128)(2,1)}, u32[]{:S(2)}, u32[]{:S(2)}) collective-permute-start(bf16[512,1,128]{2,0,1:T(8,128)(2,1)} %get-tuple-element.43), channel_id=1, source_target_pairs={{0,120},{8,0},{16,8},{24,16},{32,24},{40,32},{48,40},{56,48},{64,5... | collective-permute-start | bytes 393224 | tf_op jit(solution)/shard_map/ppermute | solution.py:20
  32.3 10.9 %copy-start.20 = (bf16[16,1024]{1,0:T(8,128)(2,1)S(1)}, bf16[16,1024]{1,0:T(8,128)(2,1)}, u32[]{:S(2)}) copy-start(bf16[16,1024]{1,0:T(8,128)(2,1)} %param.14) | copy-start | bytes 98308
  32.3 12.4 %copy-start.21 = (bf16[16,1024]{1,0:T(8,128)(2,1)S(1)}, bf16[16,1024]{1,0:T(8,128)(2,1)}, u32[]{:S(2)}) copy-start(bf16[16,1024]{1,0:T(8,128)(2,1)} %param.16) | copy-start | bytes 98308
  32.3 13.8 %copy-start.2 = (bf16[1024,1024]{0,1:T(8,128)(2,1)S(1)}, bf16[1024,1024]{0,1:T(8,128)(2,1)}, u32[]{:S(2)}) copy-start(bf16[1024,1024]{0,1:T(8,128)(2,1)} %copy.32) | copy-start | bytes 6291460
  68.2 27.7 %copy-start.28 = (f32[4,1024]{1,0:T(4,128)}, f32[4,1024]{1,0:T(4,128)S(1)}, u32[]{:S(2)}) copy-start(f32[4,1024]{1,0:T(4,128)S(1)} %get-tuple-element.21) | copy-start | bytes 49156
  68.2 10.7 %copy-start.1 = (f32[1024,1024,4]{1,0,2:T(8,128)S(1)}, f32[1024,1024,4]{1,0,2:T(8,128)}, u32[]{:S(2)}) copy-start(f32[1024,1024,4]{1,0,2:T(8,128)} %get-tuple-element.46) | copy-start | bytes 50331652
  68.2 10.7 %copy-start.7 = (bf16[512,1,4,128]{3,0,2,1:T(8,128)(2,1)S(1)}, bf16[512,1,4,128]{3,0,2,1:T(8,128)(2,1)}, u32[]{:S(2)}) copy-start(bf16[512,1,4,128]{3,0,2,1:T(8,128)(2,1)} %copy.86) | copy-start | bytes 1572868
  76.8 7.7 %copy-start.23 = (f32[4,1024]{1,0:T(4,128)}, f32[4,1024]{1,0:T(4,128)S(1)}, u32[]{:S(2)}) copy-start(f32[4,1024]{1,0:T(4,128)S(1)} %fusion.7) | copy-start | bytes 49156
  76.8 10.1 %copy-start.11 = (bf16[1024,1,4,128]{3,0,2,1:T(8,128)(2,1)S(1)}, bf16[1024,1,4,128]{3,0,2,1:T(8,128)(2,1)}, u32[]{:S(2)}) copy-start(bf16[1024,1,4,128]{3,0,2,1:T(8,128)(2,1)} %copy.83) | copy-start | bytes 3145732
  76.8 10.1 %copy-start.26 = (f32[4,1024]{1,0:T(4,128)S(1)}, f32[4,1024]{1,0:T(4,128)}, u32[]{:S(2)}) copy-start(f32[4,1024]{1,0:T(4,128)} %get-tuple-element.44) | copy-start | bytes 49156
  85.3 60.7 %collective-permute-start.6 = (f32[512,1,128]{2,0,1:T(8,128)}, f32[512,1,128]{2,0,1:T(8,128)}, u32[]{:S(2)}, u32[]{:S(2)}) collective-permute-start(f32[512,1,128]{2,0,1:T(8,128)} %get-tuple-element.36), channel_id=1, source_target_pairs={{0,8},{8,16},{16,24},{24,32},{32,40},{40,48},{48,56},{56,64},{64,7... | collective-permute-start | bytes 786440 | tf_op jit(solution)/shard_map/ppermute | solution.py:20
  86.9 9.0 %copy-start.3 = (bf16[1024,1024]{0,1:T(8,128)(2,1)S(1)}, bf16[1024,1024]{0,1:T(8,128)(2,1)}, u32[]{:S(2)}) copy-start(bf16[1024,1024]{0,1:T(8,128)(2,1)} %copy.32) | copy-start | bytes 6291460
  95.8 11.6 %copy-start.17 = (bf16[1024,128]{1,0:T(8,128)(2,1)S(1)}, bf16[1024,128]{1,0:T(8,128)(2,1)}, u32[]{:S(2)}) copy-start(bf16[1024,128]{1,0:T(8,128)(2,1)} %param.10) | copy-start | bytes 786436
  107.4 12.3 %copy-start.19 = (bf16[512,1,128]{2,0,1:T(8,128)(2,1)S(1)}, bf16[512,1,128]{2,0,1:T(8,128)(2,1)}, u32[]{:S(2)}) copy-start(bf16[512,1,128]{2,0,1:T(8,128)(2,1)} %get-tuple-element.42) | copy-start | bytes 393220
  107.4 12.3 %copy-start.24 = (f32[4,1024]{1,0:T(4,128)S(1)}, f32[4,1024]{1,0:T(4,128)}, u32[]{:S(2)}) copy-start(f32[4,1024]{1,0:T(4,128)} %copy-done.23) | copy-start | bytes 49156
  119.7 8.9 %copy-start.5 = (f32[4,1024,128]{1,2,0:T(8,128)S(1)}, f32[4,1024,128]{1,2,0:T(8,128)}, u32[]{:S(2)}) copy-start(f32[4,1024,128]{1,2,0:T(8,128)} %copy.68) | copy-start | bytes 6291460
  119.8 9.4 %copy-start.8 = (bf16[512,1,4,128]{3,0,2,1:T(8,128)(2,1)S(1)}, bf16[512,1,4,128]{3,0,2,1:T(8,128)(2,1)}, u32[]{:S(2)}) copy-start(bf16[512,1,4,128]{3,0,2,1:T(8,128)(2,1)} %copy.86) | copy-start | bytes 1572868
  129.2 10.6 %copy-start.14 = (bf16[512,1,128]{2,0,1:T(8,128)(2,1)S(1)}, bf16[512,1,128]{2,0,1:T(8,128)(2,1)}, u32[]{:S(2)}) copy-start(bf16[512,1,128]{2,0,1:T(8,128)(2,1)} %copy-done.13) | copy-start | bytes 393220
  139.7 2.5 copy-start.15
  142.0 3.9 copy-start.4
  142.1 3.9 copy-start.18
  142.1 3.9 copy-start.27
  142.1 3.9 copy-start.29
  142.2 15.8 %collective-permute-start.4 = (bf16[512,1,4,128]{0,3,2,1:T(8,128)(2,1)S(1)}, bf16[512,1,4,128]{0,3,2,1:T(8,128)(2,1)S(1)}, u32[]{:S(2)}, u32[]{:S(2)}) collective-permute-start(bf16[512,1,4,128]{0,3,2,1:T(8,128)(2,1)S(1)} %get-tuple-element.34), channel_id=1, source_target_pairs={{0,8},{8,16},{16,24},{24,32},{32,40},{40,48},{48,56},{56,64},{64,7... | collective-permute-start | bytes 1572872 | tf_op jit(solution)/shard_map/ppermute | solution.py:20
  142.3 12.6 %slice-start = ((s8[8388608]{0:T(1024)(128)(4,1)}), s8[4194304]{0:T(1024)(128)(4,1)S(1)}, s32[]{:S(2)}) async-start(s8[8388608]{0:T(1024)(128)(4,1)} %bitcast.280), calls=%async_computation.1 | async-start | bytes 8388608
  145.9 9.0 %collective-permute-start.5 = (f32[512,1,128]{2,0,1:T(8,128)S(1)}, f32[512,1,128]{2,0,1:T(8,128)S(1)}, u32[]{:S(2)}, u32[]{:S(2)}) collective-permute-start(f32[512,1,128]{2,0,1:T(8,128)S(1)} %get-tuple-element.38), channel_id=1, source_target_pairs={{0,8},{8,16},{16,24},{24,32},{32,40},{40,48},{48,56},{56,64},{64,7... | collective-permute-start | bytes 786440 | tf_op jit(solution)/shard_map/ppermute | solution.py:20
  146.0 8.7 %copy-start.25 = (bf16[16,128]{1,0:T(8,128)(2,1)S(1)}, bf16[16,128]{1,0:T(8,128)(2,1)}, u32[]{:S(2)}) copy-start(bf16[16,128]{1,0:T(8,128)(2,1)} %param.17) | copy-start | bytes 12292
  146.0 8.9 %copy-start.6 = (bf16[1024,1024]{0,1:T(8,128)(2,1)S(1)}, bf16[1024,1024]{0,1:T(8,128)(2,1)}, u32[]{:S(2)}) copy-start(bf16[1024,1024]{0,1:T(8,128)(2,1)} %copy.30) | copy-start | bytes 6291460
  146.0 8.9 %slice-start.1 = ((s8[8388608]{0:T(1024)(128)(4,1)}), s8[4194304]{0:T(1024)(128)(4,1)S(1)}, s32[]{:S(2)}) async-start(s8[8388608]{0:T(1024)(128)(4,1)} %bitcast.280), calls=%async_computation.2 | async-start | bytes 8388608
  154.7 103.2 %copy-start.10 = (bf16[1024,128]{1,0:T(8,128)(2,1)}, bf16[1024,128]{1,0:T(8,128)(2,1)S(1)}, u32[]{:S(2)}) copy-start(bf16[1024,128]{1,0:T(8,128)(2,1)S(1)} %fusion.70) | copy-start | bytes 786436
  154.7 3.3 copy-start.12
  154.9 8.6 %copy-start.22 = (bf16[16,1024]{1,0:T(8,128)(2,1)S(1)}, bf16[16,1024]{1,0:T(8,128)(2,1)}, u32[]{:S(2)}) copy-start(bf16[16,1024]{1,0:T(8,128)(2,1)} %param.15) | copy-start | bytes 98308
  158.0 8.7 %copy-start.9 = (f32[1024,16]{1,0:T(8,128)S(1)}, f32[1024,16]{1,0:T(8,128)}, u32[]{:S(2)}) copy-start(f32[1024,16]{1,0:T(8,128)} %fusion.104) | copy-start | bytes 196612
Sparse Core Ops, SparseCore 0:
  258.0 138.9 all-reduce.4
where the time goes:
time: 416 us; the launch traced here: 409 us
  blocking collectives  128 us (31%)
  matrix products  109 us (26%)
  waiting for transfers between devices  94.1 us (23%)
  local copies, waits for them, and re-layouts  39 us (9%)
  between operations  14.8 us (4%)
  other arithmetic  13.4 us (3%)
  starting transfers between devices  9.91 us (2%)
    psum x1, waiting for transfers between devices, on_device(): lax.psum((partial_query_down, partial_query_up, partial_value_down, parti...  94 us
    psum x1, blocking collectives, on_device(): lax.psum((jnp.dot(query_gradient, query_up.T, preferred_element_type=jnp....  84.3 us
    psum x1, blocking collectives, on_device(): lax.psum((partial_query_down, partial_query_up, partial_value_down, parti...  43.9 us
    unnamed x76, local copies, waits for them, and re-layouts  30.4 us
    dot_general x2, matrix products, attend_back(): jnp.einsum('qjhe,kje->jhqk', queries, key_rows, preferred_element_type=jn...  24.9 us
    dot_general x2, matrix products, attend_back(): jnp.einsum('qjhe,kje->jhqk', cotangent, value_rows, preferred_element_typ...  22.1 us
    dot_general x2, matrix products, attend_back(): jnp.einsum('jhqk,kje->qjhe', chances_low, value_rows, preferred_element_t...  17.9 us
    dot_general x2, matrix products, attend_back(): jnp.einsum('jhqk,qjhe->kje', chances_low, cotangent, preferred_element_ty...  14.1 us
  transfers between devices with their start and end apart: 8, of which 1 were waited for; matrix products, arithmetic and copies ran while one was open for 32% of the time, Pallas kernels for 0%

commit v1 on v0

v1 whole, which is shorter than its diff:
```python
import functools
import math

import jax
import jax.numpy as jnp
from jax import lax
from jax.experimental import pallas as pl
from jax.experimental.pallas import tpu as pltpu
from jax.sharding import PartitionSpec as P

HD = 128
RANK = 16
GROUP_HEADS = 8
STEADY = 4
ROWS = 1024
HALF = 512
WIDTH = 1024
SCALE = 1.0 / math.sqrt(HD)
LOG2E = 1.4426950408889634
F32 = jnp.float32
BF16 = jnp.bfloat16
NT = (((1,), (1,)), ((), ()))
PARAMS = pltpu.CompilerParams(vmem_limit_bytes=56 * 2**20)


def job(q, do, keys, values, keys_t):
    size, length = q.shape[0], keys.shape[0]
    s = lax.dot_general(keys, q, NT, preferred_element_type=F32)
    dp = lax.dot_general(values, do, NT, preferred_element_type=F32)
    row = lax.broadcasted_iota(jnp.int32, (size, size), 0)
    col = lax.broadcasted_iota(jnp.int32, (size, size), 1)
    own = jnp.where(row <= col, s[length - size :], -1e30)
    s = jnp.concatenate([s[: length - size], own], 0) if length > size else own
    high = jnp.max(s, axis=0, keepdims=True)
    e = jnp.exp2((s - high) * (SCALE * LOG2E))
    p = e * (1.0 / jnp.sum(e, axis=0, keepdims=True))
    delta = jnp.sum(p * dp, axis=0, keepdims=True)
    ds = (p * (dp - delta)).astype(BF16)
    dv = jnp.dot(p.astype(BF16), do, preferred_element_type=F32)
    dk = jnp.dot(ds, q, preferred_element_type=F32) * SCALE
    dq_t = (jnp.dot(keys_t, ds, preferred_element_type=F32) * SCALE).astype(BF16)
    return dq_t, dk, dv


def plain_kernel(q_ref, do_ref, k_ref, v_ref, up_ref, dq_ref, dk_ref, dv_ref, bq_ref, kt_ref):
    @pl.when(pl.program_id(0) == 0)
    def _():
        kt_ref[...] = k_ref[...].T
        dk_ref[...] = jnp.zeros_like(dk_ref)
        dv_ref[...] = jnp.zeros_like(dv_ref)
        bq_ref[...] = jnp.zeros_like(bq_ref)

    for at in (0, HALF):
        mine, end = slice(at, at + HALF), at + HALF
        dq_t, dk, dv = job(q_ref[mine], do_ref[mine], k_ref[:end], v_ref[:end], kt_ref[:, :end])
        dq_ref[mine] = dq_t.T
        dk_ref[:end] += dk
        dv_ref[:end] += dv
        bq_ref[:, mine] += jnp.dot(up_ref[...], dq_t, preferred_element_type=F32)


def cross_kernel(
    q_ref, do_ref, k_ref, v_ref, kv_ref, up_ref, _, dk_in, dv_in, bq_in,
    dq_ref, dk_ref, dv_ref, bq_ref, back_ref, kt_ref, keys_ref, values_ref, dkx_ref, dvx_ref,
):
    step = pl.program_id(0)

    @pl.when(step == 0)
    def _():
        keys_ref[:HALF] = kv_ref[:, :HD]
        values_ref[:HALF] = kv_ref[:, HD:]
        keys_ref[HALF:] = k_ref[:HALF]
        values_ref[HALF:] = v_ref[:HALF]
        kt_ref[...] = keys_ref[...].T
        dk_ref[...] = dk_in[...]
        dv_ref[...] = dv_in[...]
        bq_ref[...] = bq_in[...]
        dkx_ref[...] = jnp.zeros_like(dkx_ref)
        dvx_ref[...] = jnp.zeros_like(dvx_ref)

    dq_t, dk, dv = job(q_ref[...], do_ref[...], keys_ref[...], values_ref[...], kt_ref[...])
    dq_ref[...] = dq_t.T
    dkx_ref[...] += dk[:HALF]
    dvx_ref[...] += dv[:HALF]
    dk_ref[:HALF] += dk[HALF:]
    dv_ref[:HALF] += dv[HALF:]
    bq_ref[:, :HALF] += jnp.dot(up_ref[...], dq_t, preferred_element_type=F32)

    @pl.when(step == pl.num_programs(0) - 1)
    def _():
        back_ref[:, :HD] = dkx_ref[...].astype(BF16)
        back_ref[:, HD:] = dvx_ref[...].astype(BF16)


def late_kernel(
    q_ref, do_ref, k_ref, v_ref, up_ref, _, dk_in, dv_in, bq_in, dq_ref, dk_ref, dv_ref, bq_ref, kt_ref
):
    @pl.when(pl.program_id(0) == 0)
    def _():
        kt_ref[...] = k_ref[...].T
        dk_ref[...] = dk_in[...]
        dv_ref[...] = dv_in[...]
        bq_ref[...] = bq_in[...]

    dq_t, dk, dv = job(q_ref[...], do_ref[...], k_ref[...], v_ref[...], kt_ref[...])
    dq_ref[...] = dq_t.T
    dk_ref[HALF:] += dk
    dv_ref[HALF:] += dv
    bq_ref[:, HALF:] += jnp.dot(up_ref[...], dq_t, preferred_element_type=F32)


def low_kernel(x_ref, qd_ref, vd_ref, low_ref):
    low_ref[:RANK] = lax.dot_general(qd_ref[...], x_ref[...], NT, preferred_element_type=F32).astype(BF16)
    low_ref[RANK:] = lax.dot_general(vd_ref[...], x_ref[...], NT, preferred_element_type=F32).astype(BF16)


def close_kernel(dk_ref, dv_ref, back_ref, bq_ref, low_ref, up_ref, gk_ref, gv_ref, share_ref):
    gk_ref[:HALF] = dk_ref[:HALF].astype(BF16)
    gk_ref[HALF:] = (dk_ref[HALF:] + back_ref[:, :HD].astype(F32)).astype(BF16)
    gv_ref[:HALF] = dv_ref[:HALF].astype(BF16)
    gv_ref[HALF:] = (dv_ref[HALF:] + back_ref[:, HD:].astype(F32)).astype(BF16)
    bv = lax.dot_general(up_ref[...], gv_ref[...], NT, preferred_element_type=F32).astype(BF16)
    bq = bq_ref[...].astype(BF16)
    for peer in range(share_ref.shape[0]):
        share_ref[peer, : 2 * RANK] = low_ref[...]
        share_ref[peer, 2 * RANK : 3 * RANK] = bq
        share_ref[peer, 3 * RANK :] = bv


def weights_kernel(all_ref, x_ref, dq_ref, gv_ref, out_ref):
    total = all_ref[0].astype(F32)
    for peer in range(1, all_ref.shape[0]):
        total = total + all_ref[peer].astype(F32)
    total = total.astype(BF16)
    down = 2.0 * jnp.dot(total[2 * RANK :], x_ref[...], preferred_element_type=F32)
    up_q = 2.0 * jnp.dot(total[:RANK], dq_ref[...], preferred_element_type=F32)
    up_v = 2.0 * jnp.dot(total[RANK : 2 * RANK], gv_ref[...], preferred_element_type=F32)
    for part in range(2):
        columns = slice(part * HALF, (part + 1) * HALF)
        out_ref[part, : 2 * RANK] = down[:, columns]
        out_ref[part, 2 * RANK : 3 * RANK] = up_q[:, columns]
        out_ref[part, 3 * RANK :, :HD] = up_v[part * 8 : (part + 1) * 8]
        out_ref[part, 3 * RANK :, HD:] = jnp.zeros((8, HALF - HD), F32)


def whole(shape):
    return pl.BlockSpec(shape, lambda h: (0,) * len(shape))


def struct(shape, dtype):
    return jax.ShapeDtypeStruct(shape, dtype)


def on_device(query, key, value, cotangent, x, q_down, q_up, v_down, v_up):
    seq, tensor = lax.axis_size("seq"), lax.axis_size("tensor")
    sums_spec = [whole((ROWS, HD)), whole((ROWS, HD)), whole((RANK, ROWS))]
    sums_shape = [struct((ROWS, HD), F32), struct((ROWS, HD), F32), struct((RANK, ROWS), F32)]

    kv = lax.ppermute(
        jnp.concatenate([key[HALF:], value[HALF:]], axis=1),
        "seq",
        [(s, (s + 1) % seq) for s in range(seq)],
    )
    low = pl.pallas_call(
        low_kernel, out_shape=struct((2 * RANK, ROWS), BF16), compiler_params=PARAMS, name="low"
    )(x, q_down, v_down)
    column = lambda h: (0, h)
    dq, dk, dv, bq = pl.pallas_call(
        plain_kernel,
        grid=(STEADY,),
        in_specs=[pl.BlockSpec((ROWS, HD), column)] * 2
        + [whole((ROWS, HD))] * 2
        + [pl.BlockSpec((RANK, HD), column)],
        out_specs=[pl.BlockSpec((ROWS, HD), column)] + sums_spec,
        out_shape=[struct((ROWS, WIDTH), BF16)] + sums_shape,
        scratch_shapes=[pltpu.VMEM((HD, ROWS), BF16)],
        compiler_params=PARAMS,
        name="plain",
    )(query, cotangent, key, value, q_up)
    first = lambda h: (0, STEADY + h)
    dq, dk, dv, bq, back = pl.pallas_call(
        cross_kernel,
        grid=(GROUP_HEADS - STEADY,),
        in_specs=[pl.BlockSpec((HALF, HD), first)] * 2
        + [whole((ROWS, HD))] * 2
        + [whole((HALF, 2 * HD)), pl.BlockSpec((RANK, HD), first), pl.BlockSpec(memory_space=pl.ANY)]
        + sums_spec,
        out_specs=[pl.BlockSpec((HALF, HD), first)] + sums_spec + [whole((HALF, 2 * HD))],
        out_shape=[struct((ROWS, WIDTH), BF16)] + sums_shape + [struct((HALF, 2 * HD), BF16)],
        scratch_shapes=[
            pltpu.VMEM((HD, ROWS), BF16),
            pltpu.VMEM((ROWS, HD), BF16),
            pltpu.VMEM((ROWS, HD), BF16),
            pltpu.VMEM((HALF, HD), F32),
            pltpu.VMEM((HALF, HD), F32),
        ],
        input_output_aliases={6: 0},
        compiler_params=PARAMS,
        name="cross",
    )(query, cotangent, key, value, kv, q_up, dq, dk, dv, bq)
    back = lax.ppermute(back, "seq", [(s, (s - 1) % seq) for s in range(seq)])
    second = lambda h: (1, STEADY + h)
    dq, dk, dv, bq = pl.pallas_call(
        late_kernel,
        grid=(GROUP_HEADS - STEADY,),
        in_specs=[pl.BlockSpec((HALF, HD), second)] * 2
        + [pl.BlockSpec((HALF, HD), lambda h: (1, 0))] * 2
        + [pl.BlockSpec((RANK, HD), first), pl.BlockSpec(memory_space=pl.ANY)]
        + sums_spec,
        out_specs=[pl.BlockSpec((HALF, HD), second)] + sums_spec,
        out_shape=[struct((ROWS, WIDTH), BF16)] + sums_shape,
        scratch_shapes=[pltpu.VMEM((HD, HALF), BF16)],
        input_output_aliases={5: 0},
        compiler_params=PARAMS,
        name="late",
    )(query, cotangent, key, value, q_up, dq, dk, dv, bq)
    grad_key, grad_value, share = pl.pallas_call(
        close_kernel,
        out_shape=[
            struct((ROWS, HD), BF16),
            struct((ROWS, HD), BF16),
            struct((tensor, 4 * RANK, ROWS), BF16),
        ],
        compiler_params=PARAMS,
        name="close",
    )(dk, dv, back, bq, low, v_up)
    gathered = lax.all_to_all(share, "tensor", 0, 0)
    halves = pl.pallas_call(
        weights_kernel,
        out_shape=struct((2, 3 * RANK + 8, HALF), F32),
        compiler_params=PARAMS,
        name="weights",
    )(gathered, x, dq, grad_value)

    place = lax.axis_index("seq")
    core = lax.rem(place, 2)
    swap = [(s, s ^ 1) for s in range(seq)]
    mine = lax.dynamic_index_in_dim(halves, core, 0, False)
    theirs = lax.dynamic_index_in_dim(halves, 1 - core, 0, False)
    part = (mine + lax.ppermute(theirs, "seq", swap)).astype(BF16)
    chips = seq // 2
    parts = lax.all_to_all(
        jnp.broadcast_to(part[None], (chips,) + part.shape),
        "seq",
        0,
        0,
        axis_index_groups=[[2 * i + c for i in range(chips)] for c in range(2)],
    )
    total = jnp.sum(parts.astype(F32), axis=0)
    other = lax.ppermute(total, "seq", swap)
    left = jnp.where(core == 0, total, other)
    right = jnp.where(core == 0, other, total)
    both = jnp.concatenate([left[: 3 * RANK], right[: 3 * RANK]], axis=1)
    up_v = jnp.concatenate([left[3 * RANK :, :HD], right[3 * RANK :, :HD]], axis=0)
    return (
        dq,
        grad_key,
        grad_value,
        both[:RANK],
        both[2 * RANK :],
        both[RANK : 2 * RANK],
        up_v,
    )


def solution(mesh):
    rows, copied = P("seq", "tensor"), P(None, "tensor")
    return jax.shard_map(
        on_device,
        mesh=mesh,
        in_specs=(rows,) * 5 + (copied,) * 4,
        out_specs=(rows,) * 3 + (copied,) * 4,
        check_vma=False,
    )
```

time: 416 us -> 96 us (0.23); the launches traced: 409 us -> 95.6 us
  blocking collectives: 128 us -> 17.1 us
  matrix products: 109 us -> 0 us
  waiting for transfers between devices: 94.1 us -> 13.6 us
  Pallas kernels: 0 us -> 41.9 us
  local copies, waits for them, and re-layouts: 39 us -> 5.14 us
  between operations: 14.8 us -> 0.74 us
  other arithmetic: 13.4 us -> 2.3 us
  starting transfers between devices: 9.91 us -> 14.8 us
    psum x2 -> x0, blocking collectives: 128 us -> none  [the longest x1 84.3 us: on_device(): lax.psum((jnp.dot(query_gradient, query_up.T, preferred_element_type=jnp....]
    dot_general x20 -> x0, matrix products: 109 us -> none  [the longest x2 24.9 us: attend_back(): jnp.einsum('qjhe,kje->jhqk', queries, key_rows, preferred_element_type=jn...]
    psum x1 -> x0, waiting for transfers between devices: 94 us -> none  [on_device(): lax.psum((partial_query_down, partial_query_up, partial_value_down, parti...]
    pallas_call x0 -> x6, Pallas kernels: none -> 41.9 us  [the longest x1 14.2 us: on_device(): pl.pallas_call(plain_kernel, grid=(STEADY,), in_specs=[pl.BlockSpec((ROWS...]
    unnamed x76 -> x6, local copies, waits for them, and re-layouts: 30.4 us -> 2.35 us
    all_to_all x0 -> x1, blocking collectives: none -> 17.1 us  [on_device(): lax.all_to_all(jnp.broadcast_to(part[None], (chips,) + part.shape), 'seq'...]
    all_to_all x0 -> x1, waiting for transfers between devices: none -> 11.6 us  [on_device(): gathered = lax.all_to_all(share, 'tensor', 0, 0)]
    reduce_sum x1, other arithmetic: 8.54 us -> 0.06 us  [on_device(): total = jnp.sum(parts.astype(F32), axis=0)]
  transfers between devices with their start and end apart: 8 -> 5, of which waited for: 1 -> 3; matrix products, arithmetic and copies ran while one was open for 32% -> 0% of each run, Pallas kernels for 0% -> 26%
where the time goes in v1:
time: 96 us; the launch traced here: 95.6 us
  Pallas kernels  41.9 us (44%)
  blocking collectives  17.1 us (18%)
  starting transfers between devices  14.8 us (15%)
  waiting for transfers between devices  13.6 us (14%)
  local copies, waits for them, and re-layouts  5.14 us (5%)
  other arithmetic  2.3 us (2%)
    all_to_all x1, blocking collectives, on_device(): lax.all_to_all(jnp.broadcast_to(part[None], (chips,) + part.shape), 'seq'...  17.1 us
    pallas_call x1, Pallas kernels, on_device(): pl.pallas_call(plain_kernel, grid=(STEADY,), in_specs=[pl.BlockSpec((ROWS...  14.2 us
    all_to_all x1, waiting for transfers between devices, on_device(): gathered = lax.all_to_all(share, 'tensor', 0, 0)  11.6 us
    pallas_call x1, Pallas kernels, on_device(): pl.pallas_call(cross_kernel, grid=(GROUP_HEADS - STEADY,), in_specs=[pl.B...  11 us
    pallas_call x1, Pallas kernels, on_device(): pl.pallas_call(late_kernel, grid=(GROUP_HEADS - STEADY,), in_specs=[pl.Bl...  6.72 us
    all_to_all x1, starting transfers between devices, on_device(): gathered = lax.all_to_all(share, 'tensor', 0, 0)  5.38 us
    ppermute x1, starting transfers between devices, on_device(): part = (mine + lax.ppermute(theirs, 'seq', swap)).astype(BF16)  4.97 us
    pallas_call x1, Pallas kernels, on_device(): pl.pallas_call(weights_kernel, out_shape=struct((2, 3 * RANK + 8, HALF),...  4.02 us
  transfers between devices with their start and end apart: 5, of which 3 were waited for; matrix products, arithmetic and copies ran while one was open for 0% of the time, Pallas kernels for 26%

profile of v1, /device:TPU:1, one launch (start us, length us, event | category | flops | bytes accessed | tf_op | source)
XLA Modules:
  0.0 95.6 jit_solution(17331183056042640182)
XLA Ops:
  0.6 0.9 slice.27
  1.6 0.9 slice.28
  2.5 2.8 %collective-permute-start = (bf16[512,256]{1,0:T(8,128)(2,1)S(1)}, bf16[512,256]{1,0:T(8,128)(2,1)S(1)}, u32[]{:S(2)}, u32[]{:S(2)}) collective-permute-start(bf16[512,256]{1,0:T(8,128)(2,1)S(1)} %pad_maximum_fusion), channel_id=1, source_target_pairs={{0,8},{8,16},{16,24},{24,32},{32,40},{40,48},{48,56},{56,64},{64,7... | collective-permute-start | bytes 786440 | tf_op jit(solution)/shard_map/ppermute | solution.py:159
  5.3 14.2 %plain.1 = (bf16[1024,1024]{1,0:T(8,128)(2,1)}, f32[1024,128]{1,0:T(8,128)}, f32[1024,128]{1,0:T(8,128)}, f32[16,1024]{1,0:T(8,128)}) custom-call(bf16[1024,1024]{1,0:T(8,128)(2,1)} %q_ref.5, bf16[1024,1024]{1,0:T(8,128)(2,1)} %do_ref.5, bf16[1024,128]{1,0:T(8,128)(2,1)} %k_ref.5, bf16[1024,128]{1,0:T(8,128)(2,1)} %v_ref.5, bf16[16,1024]{1,0:T(8,128)(2,1)} %up_ref.6), custom_call_target="tpu_custom_call" | custom-call | tf_op jit(solution)/shard_map/plain/pallas_call | solution.py:168
  19.5 0.0 collective-permute-done.kv_ref
  19.5 0.0 copy-start.1
  19.5 0.7 copy-done.1
  20.2 11.0 %cross.1 = (bf16[1024,1024]{1,0:T(8,128)(2,1)}, f32[1024,128]{1,0:T(8,128)}, f32[1024,128]{1,0:T(8,128)}, f32[16,1024]{1,0:T(8,128)}, bf16[512,256]{1,0:T(8,128)(2,1)}) custom-call(bf16[1024,1024]{1,0:T(8,128)(2,1)} %q_ref.5, bf16[1024,1024]{1,0:T(8,128)(2,1)} %do_ref.5, bf16[1024,128]{1,0:T(8,128)(2,1)} %k_ref.5, ...), custom_call_target="tpu_custom_call", output_to_operand_aliasing={{0}: (6, {})} | custom-call | tf_op jit(solution)/shard_map/cross/pallas_call | solution.py:181
  31.2 0.1 collective-permute-start.1
  31.3 3.4 %low.1.low_ref = bf16[32,1024]{1,0:T(8,128)(2,1)} custom-call(bf16[1024,1024]{1,0:T(8,128)(2,1)} %x_ref.3, bf16[16,1024]{1,0:T(8,128)(2,1)} %qd_ref.1, bf16[16,1024]{1,0:T(8,128)(2,1)} %vd_ref.1), custom_call_target="tpu_custom_call" | custom-call | tf_op jit(solution)/shard_map/low/pallas_call | solution.py:164
  34.7 6.7 %late.1 = (bf16[1024,1024]{1,0:T(8,128)(2,1)}, f32[1024,128]{1,0:T(8,128)}, f32[1024,128]{1,0:T(8,128)}, f32[16,1024]{1,0:T(8,128)}) custom-call(bf16[1024,1024]{1,0:T(8,128)(2,1)} %q_ref.5, bf16[1024,1024]{1,0:T(8,128)(2,1)} %do_ref.5, bf16[1024,128]{1,0:T(8,128)(2,1)} %k_ref.5, bf16[1024,128]{1,0:T(8,128)(2,1)} %v_ref.5, ...), custom_call_target="tpu_custom_call", output_to_operand_aliasing={{0}: (5, {})} | custom-call | tf_op jit(solution)/shard_map/late/pallas_call | solution.py:203
  41.4 0.0 collective-permute-done.1.back_ref
  41.4 0.0 copy-start.2
  41.4 0.7 copy-done.2
  42.1 2.5 %close.1 = (bf16[1024,128]{1,0:T(8,128)(2,1)}, bf16[1024,128]{1,0:T(8,128)(2,1)}, bf16[8,64,1024]{2,1,0:T(8,128)(2,1)}) custom-call(f32[1024,128]{1,0:T(8,128)} %get-tuple-element.32.dk_ref, f32[1024,128]{1,0:T(8,128)} %get-tuple-element.33.dv_ref, bf16[512,256]{1,0:T(8,128)(2,1)} %copy-done.2, f32[16,1024]{1,0:T(8,128)} %get-tuple-element.35.bq_ref, ...), custom_call_target="tpu_custom_call" | custom-call | tf_op jit(solution)/shard_map/close/pallas_call | solution.py:217
  44.7 5.4 %all-to-all-start = ((bf16[8,64,1024]{2,1,0:T(8,128)(2,1)}), bf16[8,64,1024]{2,1,0:T(8,128)(2,1)S(1)}, u32[]{:S(2)}, u32[]{:S(2)}) async-start(bf16[8,64,1024]{2,1,0:T(8,128)(2,1)} %get-tuple-element.38), calls=%async_computation | async-start | bytes 2097152 | tf_op jit(solution)/shard_map/all_to_all | solution.py:227
  50.0 11.6 %all-to-all-done.all_ref = bf16[8,64,1024]{2,1,0:T(8,128)(2,1)S(1)} async-done(((bf16[8,64,1024]{2,1,0:T(8,128)(2,1)}), bf16[8,64,1024]{2,1,0:T(8,128)(2,1)S(1)}, u32[]{:S(2)}, u32[]{:S(2)}) %all-to-all-start) | async-done | bytes 1048608 | tf_op jit(solution)/shard_map/all_to_all | solution.py:227
  61.7 0.0 copy-start
  61.7 1.0 %copy-done = bf16[8,64,1024]{2,1,0:T(8,128)(2,1)} copy-done((bf16[8,64,1024]{2,1,0:T(8,128)(2,1)}, bf16[8,64,1024]{2,1,0:T(8,128)(2,1)S(1)}, u32[]{:S(2)}) %copy-start) | copy-done | bytes 1048600
  62.7 4.0 %weights.1 = f32[2,56,512]{2,1,0:T(8,128)} custom-call(bf16[8,64,1024]{2,1,0:T(8,128)(2,1)} %copy-done, bf16[1024,1024]{1,0:T(8,128)(2,1)} %x_ref.3, bf16[1024,1024]{1,0:T(8,128)(2,1)} %get-tuple-element.16.dq_ref, bf16[1024,128]{1,0:T(8,128)(2,1)} %get-tuple-element.18.gv_ref), custom_call_target="tpu_custom_call" | custom-call | tf_op jit(solution)/shard_map/weights/pallas_call | solution.py:228
  66.7 0.9 dynamic-slice_bitcast_fusion
  67.6 5.0 %collective-permute-start.2 = (f32[56,512]{1,0:T(8,128)S(1)}, f32[56,512]{1,0:T(8,128)S(1)}, u32[]{:S(2)}, u32[]{:S(2)}) collective-permute-start(f32[56,512]{1,0:T(8,128)S(1)} %dynamic-slice_bitcast_fusion), channel_id=1, source_target_pairs={{0,8},{8,0},{16,24},{24,16},{32,40},{40,32},{48,56},{56,48},{64,72... | collective-permute-start | bytes 344072 | tf_op jit(solution)/shard_map/ppermute | solution.py:240
  72.6 1.0 %collective-permute-done.2 = f32[56,512]{1,0:T(8,128)S(1)} collective-permute-done((f32[56,512]{1,0:T(8,128)S(1)}, f32[56,512]{1,0:T(8,128)S(1)}, u32[]{:S(2)}, u32[]{:S(2)}) %collective-permute-start.2) | collective-permute-done | bytes 114720 | tf_op jit(solution)/shard_map/ppermute | solution.py:240
  73.5 0.9 fusion
  74.5 17.1 %all_to_all.10 = bf16[8,56,512]{2,1,0:T(8,128)(2,1)S(1)} all-to-all(bf16[8,56,512]{2,1,0:T(8,128)(2,1)S(1)} %broadcast_in_dim.2), channel_id=1, replica_groups={{0,16,32,48,64,80,96,112},{8,24,40,56,72,88,104,120},{1,17,33,49,65,81,..., dimensions={0} | all-to-all | bytes 917504 | tf_op jit(solution)/shard_map/all_to_all | solution.py:242
  91.6 0.1 convert_reduce_fusion
  91.6 1.6 %collective-permute-start.3 = (f32[56,512]{1,0:T(8,128)S(1)}, f32[56,512]{1,0:T(8,128)S(1)}, u32[]{:S(2)}, u32[]{:S(2)}) collective-permute-start(f32[56,512]{1,0:T(8,128)S(1)} %convert_reduce_fusion), channel_id=1, source_target_pairs={{0,8},{8,0},{16,24},{24,16},{32,40},{40,32},{48,56},{56,48},{64,72... | collective-permute-start | bytes 344072 | tf_op jit(solution)/shard_map/ppermute | solution.py:250
  93.3 1.0 %collective-permute-done.3 = f32[56,512]{1,0:T(8,128)S(1)} collective-permute-done((f32[56,512]{1,0:T(8,128)S(1)}, f32[56,512]{1,0:T(8,128)S(1)}, u32[]{:S(2)}, u32[]{:S(2)}) %collective-permute-start.3) | collective-permute-done | bytes 114720 | tf_op jit(solution)/shard_map/ppermute | solution.py:250
  94.3 0.6 pad_maximum_fusion.2
  94.9 0.7 pad_maximum_fusion.1
  (7 shorter events, 0.1 us)
Async XLA Ops:
  2.5 17.0 %collective-permute-start = (bf16[512,256]{1,0:T(8,128)(2,1)S(1)}, bf16[512,256]{1,0:T(8,128)(2,1)S(1)}, u32[]{:S(2)}, u32[]{:S(2)}) collective-permute-start(bf16[512,256]{1,0:T(8,128)(2,1)S(1)} %pad_maximum_fusion), channel_id=1, source_target_pairs={{0,8},{8,16},{16,24},{24,32},{32,40},{40,48},{48,56},{56,64},{64,7... | collective-permute-start | bytes 786440 | tf_op jit(solution)/shard_map/ppermute | solution.py:159
  19.5 0.7 copy-start.1
  31.2 10.2 %collective-permute-start.1 = (bf16[512,256]{1,0:T(8,128)(2,1)}, bf16[512,256]{1,0:T(8,128)(2,1)S(1)}, u32[]{:S(2)}, u32[]{:S(2)}) collective-permute-start(bf16[512,256]{1,0:T(8,128)(2,1)} %get-tuple-element.34), channel_id=1, source_target_pairs={{0,120},{8,0},{16,8},{24,16},{32,24},{40,32},{48,40},{56,48},{64,5... | collective-permute-start | bytes 786440 | tf_op jit(solution)/shard_map/ppermute | solution.py:201
  41.4 0.7 copy-start.2
  44.7 17.0 %all-to-all-start = ((bf16[8,64,1024]{2,1,0:T(8,128)(2,1)}), bf16[8,64,1024]{2,1,0:T(8,128)(2,1)S(1)}, u32[]{:S(2)}, u32[]{:S(2)}) async-start(bf16[8,64,1024]{2,1,0:T(8,128)(2,1)} %get-tuple-element.38), calls=%async_computation | async-start | bytes 2097152 | tf_op jit(solution)/shard_map/all_to_all | solution.py:227
  61.7 1.0 %copy-start = (bf16[8,64,1024]{2,1,0:T(8,128)(2,1)}, bf16[8,64,1024]{2,1,0:T(8,128)(2,1)S(1)}, u32[]{:S(2)}) copy-start(bf16[8,64,1024]{2,1,0:T(8,128)(2,1)S(1)} %all-to-all-done.all_ref) | copy-start | bytes 3145732
  67.6 5.9 %collective-permute-start.2 = (f32[56,512]{1,0:T(8,128)S(1)}, f32[56,512]{1,0:T(8,128)S(1)}, u32[]{:S(2)}, u32[]{:S(2)}) collective-permute-start(f32[56,512]{1,0:T(8,128)S(1)} %dynamic-slice_bitcast_fusion), channel_id=1, source_target_pairs={{0,8},{8,0},{16,24},{24,16},{32,40},{40,32},{48,56},{56,48},{64,72... | collective-permute-start | bytes 344072 | tf_op jit(solution)/shard_map/ppermute | solution.py:240
  91.6 2.6 %collective-permute-start.3 = (f32[56,512]{1,0:T(8,128)S(1)}, f32[56,512]{1,0:T(8,128)S(1)}, u32[]{:S(2)}, u32[]{:S(2)}) collective-permute-start(f32[56,512]{1,0:T(8,128)S(1)} %convert_reduce_fusion), channel_id=1, source_target_pairs={{0,8},{8,0},{16,24},{24,16},{32,40},{40,32},{48,56},{56,48},{64,72... | collective-permute-start | bytes 344072 | tf_op jit(solution)/shard_map/ppermute | solution.py:250

commit v2 on v1

v2 whole, which is shorter than its diff:
```python
import math

import jax
import jax.numpy as jnp
from jax import lax
from jax.experimental import pallas as pl
from jax.experimental.pallas import tpu as pltpu
from jax.sharding import PartitionSpec as P

HD = 128
RANK = 16
STEADY = 4
ROWS = 1024
HALF = 512
WIDTH = 1024
BLOCK = 256
SCALE = 1.0 / math.sqrt(HD)
FOLDED = SCALE * 1.4426950408889634
F32 = jnp.float32
BF16 = jnp.bfloat16
NT = (((1,), (1,)), ((), ()))
LARGE = pltpu.CompilerParams(vmem_limit_bytes=48 * 2**20)
SMALL = pltpu.CompilerParams(vmem_limit_bytes=24 * 2**20)


def products(q, do, keys_twice, values):
    scaled = q.astype(F32) * FOLDED
    big = scaled.astype(BF16)
    rest = (scaled - big.astype(F32)).astype(BF16)
    s = lax.dot_general(keys_twice, jnp.concatenate([big, rest], 1), NT, preferred_element_type=F32)
    dp = lax.dot_general(values, do, NT, preferred_element_type=F32)
    return s, dp


def softmax_back(s, dp):
    length, size = s.shape
    row = lax.broadcasted_iota(jnp.int32, (size, size), 0)
    col = lax.broadcasted_iota(jnp.int32, (size, size), 1)
    own = jnp.where(row <= col, s[length - size :], -1e30)
    s = jnp.concatenate([s[: length - size], own], 0) if length > size else own
    e = jnp.exp2(s - jnp.max(s, axis=0, keepdims=True))
    r = 1.0 / jnp.sum(e, axis=0, keepdims=True)
    delta = jnp.sum(e * dp, axis=0, keepdims=True) * r
    p = e * r
    return p.astype(BF16), (p * (dp - delta)).astype(BF16)


def sweep(jobs, q_ref, do_ref, up_ref, twice, values, keys_t, dq_ref, bq_ref, add):
    tile = lambda ref, head, at: ref[at : at + BLOCK, head * HD : (head + 1) * HD]
    begin = lambda head, at, ks: products(tile(q_ref, head, at), tile(do_ref, head, at), twice[ks], values[ks])

    def finish(head, at, ks, p, ds):
        q, do = tile(q_ref, head, at), tile(do_ref, head, at)
        dq_t = (jnp.dot(keys_t[:, ks], ds, preferred_element_type=F32) * SCALE).astype(BF16)
        dq_ref[at : at + BLOCK, head * HD : (head + 1) * HD] = dq_t.T
        bq_ref[:, at : at + BLOCK] += jnp.dot(
            up_ref[:, head * HD : (head + 1) * HD], dq_t, preferred_element_type=F32
        )
        add(
            ks,
            jnp.dot(ds, q, preferred_element_type=F32),
            jnp.dot(p, do, preferred_element_type=F32),
        )

    ready, softened = begin(*jobs[0]), None
    for n in range(len(jobs) + 1):
        coming = begin(*jobs[n + 1]) if n + 1 < len(jobs) else None
        now = softmax_back(*ready) if n < len(jobs) else None
        if n > 0:
            finish(*jobs[n - 1], *softened)
        ready, softened = coming, now


def first_last():
    step = pl.program_id(0)
    return step == 0, step == pl.num_programs(0) - 1


def plain_kernel(
    q_ref, do_ref, k_ref, v_ref, up_ref, x_ref, qd_ref, vd_ref,
    dq_ref, dk_ref, dv_ref, bq_ref, low_ref, twice_ref, kt_ref,
):
    first, last = first_last()

    @pl.when(first)
    def _():
        twice_ref[:, :HD] = k_ref[...]
        twice_ref[:, HD:] = k_ref[...]
        kt_ref[...] = k_ref[...].T
        dk_ref[...] = jnp.zeros_like(dk_ref)
        dv_ref[...] = jnp.zeros_like(dv_ref)
        bq_ref[...] = jnp.zeros_like(bq_ref)

    low_ref[:RANK] = lax.dot_general(qd_ref[...], x_ref[...], NT, preferred_element_type=F32).astype(BF16)
    low_ref[RANK:] = lax.dot_general(vd_ref[...], x_ref[...], NT, preferred_element_type=F32).astype(BF16)

    def add(ks, dk, dv):
        dk_ref[ks] += dk
        dv_ref[ks] += dv

    jobs = [(head, at, slice(0, at + BLOCK)) for head in range(2) for at in range(0, ROWS, BLOCK)]
    sweep(jobs, q_ref, do_ref, up_ref, twice_ref, v_ref, kt_ref, dq_ref, bq_ref, add)

    @pl.when(last)
    def _():
        dk_ref[...] = dk_ref[...] * SCALE


def cross_kernel(
    q_ref, do_ref, k_ref, v_ref, kv_ref, up_ref, _,
    dq_ref, dk_ref, dv_ref, bq_ref, back_ref, twice_ref, values_ref, kt_ref, dkx_ref, dvx_ref,
):
    first, last = first_last()

    @pl.when(first)
    def _():
        for part in (slice(0, HD), slice(HD, 2 * HD)):
            twice_ref[:HALF, part] = kv_ref[:, :HD]
            twice_ref[HALF:, part] = k_ref[...]
        values_ref[:HALF] = kv_ref[:, HD:]
        values_ref[HALF:] = v_ref[...]
        kt_ref[:, :HALF] = kv_ref[:, :HD].T
        kt_ref[:, HALF:] = k_ref[...].T
        dkx_ref[...] = jnp.zeros_like(dkx_ref)
        dvx_ref[...] = jnp.zeros_like(dvx_ref)
        bq_ref[...] = jnp.zeros_like(bq_ref)

    def add(ks, dk, dv):
        dkx_ref[ks] += dk
        dvx_ref[ks] += dv

    jobs = [(head, at, slice(0, HALF + at + BLOCK)) for head in range(2) for at in range(0, HALF, BLOCK)]
    sweep(jobs, q_ref, do_ref, up_ref, twice_ref, values_ref, kt_ref, dq_ref, bq_ref, add)

    @pl.when(last)
    def _():
        back_ref[:, :HD] = (dkx_ref[:HALF] * SCALE).astype(BF16)
        back_ref[:, HD:] = dvx_ref[:HALF].astype(BF16)
        dk_ref[...] = dkx_ref[HALF:] * SCALE
        dv_ref[...] = dvx_ref[HALF:]


def late_kernel(
    q_ref, do_ref, k_ref, v_ref, up_ref, _, dq_ref, dk_ref, dv_ref, bq_ref, twice_ref, kt_ref
):
    twice_ref[:, :HD] = k_ref[...]
    twice_ref[:, HD:] = k_ref[...]
    kt_ref[...] = k_ref[...].T
    dk_ref[...] = jnp.zeros_like(dk_ref)
    dv_ref[...] = jnp.zeros_like(dv_ref)
    bq_ref[...] = jnp.zeros_like(bq_ref)

    def add(ks, dk, dv):
        dk_ref[ks] += dk
        dv_ref[ks] += dv

    jobs = [(head, at, slice(0, at + BLOCK)) for head in range(4) for at in range(0, HALF, BLOCK)]
    sweep(jobs, q_ref, do_ref, up_ref, twice_ref, v_ref, kt_ref, dq_ref, bq_ref, add)
    dk_ref[...] = dk_ref[...] * SCALE


def pack_kernel(k_ref, v_ref, kv_ref):
    kv_ref[:, :HD] = k_ref[...]
    kv_ref[:, HD:] = v_ref[...]


def close_kernel(
    dk_ref, dv_ref, dkb_ref, dvb_ref, dkc_ref, dvc_ref, back_ref, bq_ref, bqb_ref, bqc_ref, low_ref, up_ref,
    gk_ref, gv_ref, share_ref,
):
    gk_ref[:HALF] = (dk_ref[:HALF] + dkb_ref[...]).astype(BF16)
    gk_ref[HALF:] = (dk_ref[HALF:] + dkc_ref[...] + back_ref[:, :HD].astype(F32)).astype(BF16)
    gv_ref[:HALF] = (dv_ref[:HALF] + dvb_ref[...]).astype(BF16)
    gv_ref[HALF:] = (dv_ref[HALF:] + dvc_ref[...] + back_ref[:, HD:].astype(F32)).astype(BF16)
    bv = lax.dot_general(up_ref[...], gv_ref[...], NT, preferred_element_type=F32).astype(BF16)
    bq_low = (bq_ref[:, :HALF] + bqb_ref[...]).astype(BF16)
    bq_high = (bq_ref[:, HALF:] + bqc_ref[...]).astype(BF16)
    for peer in range(share_ref.shape[0]):
        share_ref[peer, : 2 * RANK] = low_ref[...]
        share_ref[peer, 2 * RANK : 3 * RANK, :HALF] = bq_low
        share_ref[peer, 2 * RANK : 3 * RANK, HALF:] = bq_high
        share_ref[peer, 3 * RANK :] = bv


def weights_kernel(all_ref, x_ref, dq_ref, gv_ref, keep_ref, give_ref, down_ref, upq_ref, upv_ref):
    first, last = first_last()

    @pl.when(first)
    def _():
        down_ref[...] = jnp.zeros_like(down_ref)
        upq_ref[...] = jnp.zeros_like(upq_ref)
        upv_ref[...] = jnp.zeros_like(upv_ref)

    total = all_ref[0].astype(F32)
    for peer in range(1, all_ref.shape[0]):
        total = total + all_ref[peer].astype(F32)
    total = total.astype(BF16)
    down_ref[...] += jnp.dot(total[2 * RANK :], x_ref[...], preferred_element_type=F32)
    upq_ref[...] += jnp.dot(total[:RANK], dq_ref[...], preferred_element_type=F32)
    upv_ref[...] += jnp.dot(total[RANK : 2 * RANK], gv_ref[...], preferred_element_type=F32)

    @pl.when(last)
    def _():
        even = lax.rem(lax.axis_index("seq"), 2) == 0
        for ref, left in ((keep_ref, even), (give_ref, jnp.logical_not(even))):
            pick = lambda a, b: 2.0 * jnp.where(left, a, b)
            ref[: 2 * RANK] = pick(down_ref[:, :HALF], down_ref[:, HALF:])
            ref[2 * RANK : 3 * RANK] = pick(upq_ref[:, :HALF], upq_ref[:, HALF:])
            ref[3 * RANK :, :HD] = pick(upv_ref[:8], upv_ref[8:])
            ref[3 * RANK :, HD:] = jnp.zeros((8, HALF - HD), F32)


def place_kernel(mine_ref, other_ref, qd_ref, qu_ref, vd_ref, vu_ref):
    even = lax.rem(lax.axis_index("seq"), 2) == 0
    left = jnp.where(even, mine_ref[...], other_ref[...])
    right = jnp.where(even, other_ref[...], mine_ref[...])
    for ref, at in ((qd_ref, 0), (vd_ref, RANK), (qu_ref, 2 * RANK)):
        ref[:, :HALF] = left[at : at + RANK]
        ref[:, HALF:] = right[at : at + RANK]
    vu_ref[:8] = left[3 * RANK :, :HD]
    vu_ref[8:] = right[3 * RANK :, :HD]


def whole(*shape):
    return pl.BlockSpec(shape, lambda h: (0,) * len(shape))


def struct(*shape, dtype=F32):
    return jax.ShapeDtypeStruct(shape, dtype)


def on_device(query, key, value, cotangent, x, q_down, q_up, v_down, v_up):
    seq, tensor = lax.axis_size("seq"), lax.axis_size("tensor")
    untouched = pl.BlockSpec(memory_space=pl.ANY)
    top, bottom = pl.BlockSpec((HALF, HD), lambda h: (0, 0)), pl.BlockSpec((HALF, HD), lambda h: (1, 0))

    kv = pl.pallas_call(
        pack_kernel,
        grid=(1,),
        in_specs=[bottom, bottom],
        out_specs=whole(HALF, 2 * HD),
        out_shape=struct(HALF, 2 * HD, dtype=BF16),
        compiler_params=SMALL,
        name="pack",
    )(key, value)
    kv = lax.ppermute(kv, "seq", [(s, (s + 1) % seq) for s in range(seq)])

    pair = lambda h: (0, h)
    dq, dk, dv, bq, low = pl.pallas_call(
        plain_kernel,
        grid=(2,),
        in_specs=[pl.BlockSpec((ROWS, 2 * HD), pair)] * 2
        + [whole(ROWS, HD)] * 2
        + [pl.BlockSpec((RANK, 2 * HD), pair), pl.BlockSpec((HALF, WIDTH), lambda h: (h, 0))]
        + [whole(RANK, WIDTH)] * 2,
        out_specs=[pl.BlockSpec((ROWS, 2 * HD), pair), whole(ROWS, HD), whole(ROWS, HD), whole(RANK, ROWS)]
        + [pl.BlockSpec((2 * RANK, HALF), pair)],
        out_shape=[
            struct(ROWS, WIDTH, dtype=BF16),
            struct(ROWS, HD),
            struct(ROWS, HD),
            struct(RANK, ROWS),
            struct(2 * RANK, ROWS, dtype=BF16),
        ],
        scratch_shapes=[pltpu.VMEM((ROWS, 2 * HD), BF16), pltpu.VMEM((HD, ROWS), BF16)],
        compiler_params=LARGE,
        name="plain",
    )(query, cotangent, key, value, q_up, x, q_down, v_down)

    rolled = lambda h: (0, 2 + h)
    dq, dk_b, dv_b, bq_b, back = pl.pallas_call(
        cross_kernel,
        grid=(2,),
        in_specs=[pl.BlockSpec((HALF, 2 * HD), rolled)] * 2
        + [top, top, whole(HALF, 2 * HD), pl.BlockSpec((RANK, 2 * HD), rolled), untouched],
        out_specs=[pl.BlockSpec((HALF, 2 * HD), rolled), whole(HALF, HD), whole(HALF, HD)]
        + [whole(RANK, HALF), whole(HALF, 2 * HD)],
        out_shape=[
            struct(ROWS, WIDTH, dtype=BF16),
            struct(HALF, HD),
            struct(HALF, HD),
            struct(RANK, HALF),
            struct(HALF, 2 * HD, dtype=BF16),
        ],
        scratch_shapes=[
            pltpu.VMEM((ROWS, 2 * HD), BF16),
            pltpu.VMEM((ROWS, HD), BF16),
            pltpu.VMEM((HD, ROWS), BF16),
            pltpu.VMEM((ROWS, HD), F32),
            pltpu.VMEM((ROWS, HD), F32),
        ],
        input_output_aliases={6: 0},
        compiler_params=LARGE,
        name="cross",
    )(query, cotangent, key, value, kv, q_up, dq)
    back = lax.ppermute(back, "seq", [(s, (s - 1) % seq) for s in range(seq)])

    corner = pl.BlockSpec((HALF, 4 * HD), lambda h: (1, 1))
    dq, dk_c, dv_c, bq_c = pl.pallas_call(
        late_kernel,
        grid=(1,),
        in_specs=[corner, corner, bottom, bottom, pl.BlockSpec((RANK, 4 * HD), lambda h: (0, 1)), untouched],
        out_specs=[corner, whole(HALF, HD), whole(HALF, HD), whole(RANK, HALF)],
        out_shape=[struct(ROWS, WIDTH, dtype=BF16), struct(HALF, HD), struct(HALF, HD), struct(RANK, HALF)],
        scratch_shapes=[pltpu.VMEM((HALF, 2 * HD), BF16), pltpu.VMEM((HD, HALF), BF16)],
        input_output_aliases={5: 0},
        compiler_params=LARGE,
        name="late",
    )(query, cotangent, key, value, q_up, dq)

    grad_key, grad_value, share = pl.pallas_call(
        close_kernel,
        out_shape=[
            struct(ROWS, HD, dtype=BF16),
            struct(ROWS, HD, dtype=BF16),
            struct(tensor, 4 * RANK, ROWS, dtype=BF16),
        ],
        compiler_params=SMALL,
        name="close",
    )(dk, dv, dk_b, dv_b, dk_c, dv_c, back, bq, bq_b, bq_c, low, v_up)
    gathered = lax.all_to_all(share, "tensor", 0, 0)

    down = lambda h: (h, 0)
    part_rows = 3 * RANK + 8
    keep, give = pl.pallas_call(
        weights_kernel,
        grid=(ROWS // BLOCK,),
        in_specs=[
            pl.BlockSpec((tensor, 4 * RANK, BLOCK), lambda h: (0, 0, h)),
            pl.BlockSpec((BLOCK, WIDTH), down),
            pl.BlockSpec((BLOCK, WIDTH), down),
            pl.BlockSpec((BLOCK, HD), down),
        ],
        out_specs=[whole(part_rows, HALF)] * 2,
        out_shape=[struct(part_rows, HALF)] * 2,
        scratch_shapes=[
            pltpu.VMEM((2 * RANK, WIDTH), F32),
            pltpu.VMEM((RANK, WIDTH), F32),
            pltpu.VMEM((RANK, HD), F32),
        ],
        compiler_params=SMALL,
        name="weights",
    )(gathered, x, dq, grad_value)

    swap = [(s, s ^ 1) for s in range(seq)]
    part = (keep + lax.ppermute(give, "seq", swap)).astype(BF16)
    chips = seq // 2
    parts = lax.all_to_all(
        jnp.broadcast_to(part[None], (chips,) + part.shape),
        "seq",
        0,
        0,
        axis_index_groups=[[2 * i + c for i in range(chips)] for c in range(2)],
    )
    total = jnp.sum(parts.astype(F32), axis=0)
    other = lax.ppermute(total, "seq", swap)
    q_down_grad, q_up_grad, v_down_grad, v_up_grad = pl.pallas_call(
        place_kernel,
        out_shape=[struct(RANK, WIDTH)] * 3 + [struct(RANK, HD)],
        compiler_params=SMALL,
        name="place",
    )(total, other)
    return dq, grad_key, grad_value, q_down_grad, q_up_grad, v_down_grad, v_up_grad


def solution(mesh):
    rows, copied = P("seq", "tensor"), P(None, "tensor")
    return jax.shard_map(
        on_device,
        mesh=mesh,
        in_specs=(rows,) * 5 + (copied,) * 4,
        out_specs=(rows,) * 3 + (copied,) * 4,
        check_vma=False,
    )
```

time: 96 us -> 87.1 us (0.907)
  blocking collectives: 17.1 us -> 34.1 us
  Pallas kernels: 41.9 us -> 30.3 us
  waiting for transfers between devices: 13.6 us -> 3.74 us
  starting transfers between devices: 14.8 us -> 8.32 us
  local copies, waits for them, and re-layouts: 5.14 us -> 9.29 us
  other arithmetic: 2.3 us -> 0.08 us
    all_to_all x0 -> x1, blocking collectives: none -> 17.8 us  [on_device(): gathered = lax.all_to_all(share, 'tensor', 0, 0)]
    all_to_all x1 -> x0, waiting for transfers between devices: 11.6 us -> none  [on_device(): gathered = lax.all_to_all(share, 'tensor', 0, 0)]
    pallas_call x6 -> x7, Pallas kernels: 41.9 us -> 30.3 us  [the longest x1 14.2 us: on_device(): pl.pallas_call(plain_kernel, grid=(2,), in_specs=[pl.BlockSpec((ROWS, 2 *...]
    unnamed x6 -> x26, local copies, waits for them, and re-layouts: 2.35 us -> 9.26 us
    all_to_all x1 -> x0, starting transfers between devices: 5.38 us -> none  [on_device(): gathered = lax.all_to_all(share, 'tensor', 0, 0)]
    slice x6 -> x0, local copies, waits for them, and re-layouts: 1.86 us -> none  [the longest x1 0.92 us: on_device(): key[HALF:]]
    ppermute x1, waiting for transfers between devices: 0.01 us -> 1.81 us  [on_device(): back = lax.ppermute(back, 'seq', [(s, (s - 1) % seq) for s in range(seq)])]
    concatenate x3 -> x0, other arithmetic: 1.31 us -> none  [the longest x1 0.68 us: on_device(): both = jnp.concatenate([left[:3 * RANK], right[:3 * RANK]], axis=1)]
  transfers between devices with their start and end apart: 5 -> 4, of which waited for: 3 -> 3; matrix products, arithmetic and copies ran while one was open for 0% -> 0% of each run, Pallas kernels for 26% -> 21%
where the time goes in v2:
time: 87.1 us; the launch traced here: 86.5 us
  blocking collectives  34.1 us (39%)
  Pallas kernels  30.3 us (35%)
  local copies, waits for them, and re-layouts  9.29 us (11%)
  starting transfers between devices  8.32 us (10%)
  waiting for transfers between devices  3.74 us (4%)
    all_to_all x1, blocking collectives, on_device(): gathered = lax.all_to_all(share, 'tensor', 0, 0)  17.8 us
    all_to_all x1, blocking collectives, on_device(): lax.all_to_all(jnp.broadcast_to(part[None], (chips,) + part.shape), 'seq'...  16.4 us
    pallas_call x1, Pallas kernels, on_device(): pl.pallas_call(plain_kernel, grid=(2,), in_specs=[pl.BlockSpec((ROWS, 2 *...  14.2 us
    unnamed x26, local copies, waits for them, and re-layouts  9.26 us
    pallas_call x1, Pallas kernels, on_device(): pl.pallas_call(cross_kernel, grid=(2,), in_specs=[pl.BlockSpec((HALF, 2 *...  9.03 us
    pallas_call x1, Pallas kernels, on_device(): pl.pallas_call(late_kernel, grid=(1,), in_specs=[corner, corner, bottom,...  3.98 us
    ppermute x1, starting transfers between devices, on_device(): part = (keep + lax.ppermute(give, 'seq', swap)).astype(BF16)  3.92 us
    ppermute x1, starting transfers between devices, on_device(): kv = lax.ppermute(kv, 'seq', [(s, (s + 1) % seq) for s in range(seq)])  2.76 us
  transfers between devices with their start and end apart: 4, of which 3 were waited for; matrix products, arithmetic and copies ran while one was open for 0% of the time, Pallas kernels for 21%

profile of v2, /device:TPU:1, one launch (start us, length us, event | category | flops | bytes accessed | tf_op | source)
XLA Modules:
  0.0 86.5 jit_solution(13586452995002346284)
XLA Ops:
  0.6 0.0 copy-start.4
  0.6 0.9 %copy-done.4 = bf16[1024,128]{1,0:T(8,128)(2,1)S(1)} copy-done((bf16[1024,128]{1,0:T(8,128)(2,1)S(1)}, bf16[1024,128]{1,0:T(8,128)(2,1)}, u32[]{:S(2)}) %copy-start.4) | copy-done | bytes 262168
  1.6 0.0 copy-start.6
  1.6 0.9 %copy-done.6 = bf16[1024,128]{1,0:T(8,128)(2,1)S(1)} copy-done((bf16[1024,128]{1,0:T(8,128)(2,1)S(1)}, bf16[1024,128]{1,0:T(8,128)(2,1)}, u32[]{:S(2)}) %copy-start.6) | copy-done | bytes 262168
  2.6 2.8 %collective-permute-start = (bf16[512,256]{1,0:T(8,128)(2,1)S(1)}, bf16[512,256]{1,0:T(8,128)(2,1)S(1)}, u32[]{:S(2)}, u32[]{:S(2)}) collective-permute-start(bf16[512,256]{1,0:T(8,128)(2,1)S(1)} %pack.1), channel_id=1, source_target_pairs={{0,8},{8,16},{16,24},{24,32},{32,40},{40,48},{48,56},{56,64},{64,7... | collective-permute-start | bytes 786440 | tf_op jit(solution)/shard_map/ppermute | solution.py:246
  5.3 0.0 copy-start
  5.3 1.6 %copy-done = bf16[1024,1024]{1,0:T(8,128)(2,1)S(1)} copy-done((bf16[1024,1024]{1,0:T(8,128)(2,1)S(1)}, bf16[1024,1024]{1,0:T(8,128)(2,1)}, u32[]{:S(2)}) %copy-start) | copy-done | bytes 2097176
  6.9 0.0 copy-start.1
  6.9 1.6 %copy-done.1 = bf16[1024,1024]{1,0:T(8,128)(2,1)S(1)} copy-done((bf16[1024,1024]{1,0:T(8,128)(2,1)S(1)}, bf16[1024,1024]{1,0:T(8,128)(2,1)}, u32[]{:S(2)}) %copy-start.1) | copy-done | bytes 2097176
  8.5 0.0 copy-start.5
  8.5 0.9 %copy-done.5 = bf16[1024,128]{1,0:T(8,128)(2,1)S(1)} copy-done((bf16[1024,128]{1,0:T(8,128)(2,1)S(1)}, bf16[1024,128]{1,0:T(8,128)(2,1)}, u32[]{:S(2)}) %copy-start.5) | copy-done | bytes 262168
  9.5 0.0 copy-start.7
  9.5 0.9 %copy-done.7 = bf16[1024,128]{1,0:T(8,128)(2,1)S(1)} copy-done((bf16[1024,128]{1,0:T(8,128)(2,1)S(1)}, bf16[1024,128]{1,0:T(8,128)(2,1)}, u32[]{:S(2)}) %copy-start.7) | copy-done | bytes 262168
  10.4 0.0 copy-start.8
  10.4 0.8 copy-done.8
  11.2 0.0 copy-start.10
  11.2 0.8 copy-done.10
  11.9 0.0 copy-start.11
  11.9 0.8 copy-done.11
  12.7 14.2 %plain.1 = (bf16[1024,1024]{1,0:T(8,128)(2,1)}, f32[1024,128]{1,0:T(8,128)S(1)}, f32[1024,128]{1,0:T(8,128)S(1)}, f32[16,1024]{1,0:T(8,128)S(1)}, bf16[32,1024]{1,0:T(8,128)(2,1)S(1)}) custom-call(bf16[1024,1024]{1,0:T(8,128)(2,1)S(1)} %copy-done, bf16[1024,1024]{1,0:T(8,128)(2,1)S(1)} %copy-done.1, bf16[1024,128]{1,0:T(8,128)(2,1)S(1)} %copy-done.5, ...), custom_call_target="tpu_custom_call" | custom-call | tf_op jit(solution)/shard_map/plain/pallas_call | solution.py:249
  26.9 0.0 collective-permute-done.kv_ref
  26.9 9.0 %cross.1 = (bf16[1024,1024]{1,0:T(8,128)(2,1)}, f32[512,128]{1,0:T(8,128)S(1)}, f32[512,128]{1,0:T(8,128)S(1)}, f32[16,512]{1,0:T(8,128)S(1)}, bf16[512,256]{1,0:T(8,128)(2,1)S(1)}) custom-call(bf16[1024,1024]{1,0:T(8,128)(2,1)S(1)} %copy-done, bf16[1024,1024]{1,0:T(8,128)(2,1)S(1)} %copy-done.1, ...), custom_call_target="tpu_custom_call", output_to_operand_aliasing={{0}: (6, {})} | custom-call | tf_op jit(solution)/shard_map/cross/pallas_call | solution.py:271
  35.9 0.0 collective-permute-start.1
  35.9 0.0 copy-start.12
  35.9 4.0 %late.1 = (bf16[1024,1024]{1,0:T(8,128)(2,1)}, f32[512,128]{1,0:T(8,128)S(1)}, f32[512,128]{1,0:T(8,128)S(1)}, f32[16,512]{1,0:T(8,128)S(1)}) custom-call(bf16[1024,1024]{1,0:T(8,128)(2,1)S(1)} %copy-done, bf16[1024,1024]{1,0:T(8,128)(2,1)S(1)} %copy-done.1, bf16[1024,128]{1,0:T(8,128)(2,1)S(1)} %copy-done.5, ...), custom_call_target="tpu_custom_call", output_to_operand_aliasing={{0}: (5, {})} | custom-call | tf_op jit(solution)/shard_map/late/pallas_call | solution.py:299
  39.9 1.8 %collective-permute-done.1.back_ref = bf16[512,256]{1,0:T(8,128)(2,1)S(1)} collective-permute-done((bf16[512,256]{1,0:T(8,128)(2,1)S(1)}, bf16[512,256]{1,0:T(8,128)(2,1)S(1)}, u32[]{:S(2)}, u32[]{:S(2)}) %collective-permute-start.1) | collective-permute-done | bytes 262176 | tf_op jit(solution)/shard_map/ppermute | solution.py:296
  41.7 0.0 copy-done.12
  41.7 0.0 copy-start.2
  41.7 0.0 copy-start.3
  41.7 1.0 %close.1 = (bf16[1024,128]{1,0:T(8,128)(2,1)}, bf16[1024,128]{1,0:T(8,128)(2,1)}, bf16[8,64,1024]{2,1,0:T(8,128)(2,1)S(1)}) custom-call(f32[1024,128]{1,0:T(8,128)S(1)} %get-tuple-element.33.dk_ref, f32[1024,128]{1,0:T(8,128)S(1)} %get-tuple-element.34.dv_ref, f32[512,128]{1,0:T(8,128)S(1)} %get-tuple-element.35.dkb_ref, ...), custom_call_target="tpu_custom_call" | custom-call | tf_op jit(solution)/shard_map/close/pallas_call | solution.py:311
  42.7 0.0 copy-start.9
  42.7 17.8 %all_to_all.10.all_ref = bf16[8,64,1024]{2,1,0:T(8,128)(2,1)S(1)} all-to-all(bf16[8,64,1024]{2,1,0:T(8,128)(2,1)S(1)} %get-tuple-element.46), channel_id=1, replica_groups=mesh['seq'=16,'tensor'=8] {'tensor'}, dimensions={0} | all-to-all | bytes 2097152 | tf_op jit(solution)/shard_map/all_to_all | solution.py:321
  60.5 0.0 copy-done.2
  60.5 0.0 copy-done.3
  60.5 0.0 copy-done.9
  60.5 1.4 %weights.1 = (f32[56,512]{1,0:T(8,128)S(1)}, f32[56,512]{1,0:T(8,128)S(1)}) custom-call(bf16[8,64,1024]{2,1,0:T(8,128)(2,1)S(1)} %all_to_all.10.all_ref, bf16[1024,1024]{1,0:T(8,128)(2,1)S(1)} %copy-done.3, bf16[1024,1024]{1,0:T(8,128)(2,1)S(1)} %copy-done.2, bf16[1024,128]{1,0:T(8,128)(2,1)S(1)} %copy-done.9), custom_call_target="tpu_custom_call" | custom-call | tf_op jit(solution)/shard_map/weights/pallas_call | solution.py:325
  61.9 3.9 %collective-permute-start.2 = (f32[56,512]{1,0:T(8,128)S(1)}, f32[56,512]{1,0:T(8,128)S(1)}, u32[]{:S(2)}, u32[]{:S(2)}) collective-permute-start(f32[56,512]{1,0:T(8,128)S(1)} %get-tuple-element.48), channel_id=1, source_target_pairs={{0,8},{8,0},{16,24},{24,16},{32,40},{40,32},{48,56},{56,48},{64,72... | collective-permute-start | bytes 344072 | tf_op jit(solution)/shard_map/ppermute | solution.py:346
  65.8 1.0 %collective-permute-done.2 = f32[56,512]{1,0:T(8,128)S(1)} collective-permute-done((f32[56,512]{1,0:T(8,128)S(1)}, f32[56,512]{1,0:T(8,128)S(1)}, u32[]{:S(2)}, u32[]{:S(2)}) %collective-permute-start.2) | collective-permute-done | bytes 114720 | tf_op jit(solution)/shard_map/ppermute | solution.py:346
  66.8 16.4 %all_to_all.11 = bf16[8,56,512]{2,1,0:T(8,128)(2,1)S(1)} all-to-all(bf16[8,56,512]{2,1,0:T(8,128)(2,1)S(1)} %broadcast_in_dim.2), channel_id=1, replica_groups={{0,16,32,48,64,80,96,112},{8,24,40,56,72,88,104,120},{1,17,33,49,65,81,..., dimensions={0} | all-to-all | bytes 917504 | tf_op jit(solution)/shard_map/all_to_all | solution.py:348
  83.2 0.1 convert_reduce_fusion.mine_ref
  83.2 1.6 %collective-permute-start.3 = (f32[56,512]{1,0:T(8,128)S(1)}, f32[56,512]{1,0:T(8,128)S(1)}, u32[]{:S(2)}, u32[]{:S(2)}) collective-permute-start(f32[56,512]{1,0:T(8,128)S(1)} %convert_reduce_fusion.mine_ref), channel_id=1, source_target_pairs={{0,8},{8,0},{16,24},{24,16},{32,40},{40,32},{48,56},{56,48},{64,72... | collective-permute-start | bytes 344072 | tf_op jit(solution)/shard_map/ppermute | solution.py:356
  84.9 1.0 %collective-permute-done.3.other_ref = f32[56,512]{1,0:T(8,128)S(1)} collective-permute-done((f32[56,512]{1,0:T(8,128)S(1)}, f32[56,512]{1,0:T(8,128)S(1)}, u32[]{:S(2)}, u32[]{:S(2)}) %collective-permute-start.3) | collective-permute-done | bytes 114720 | tf_op jit(solution)/shard_map/ppermute | solution.py:356
  85.9 0.7 place.1
  (3 shorter events, 0.1 us)
Async XLA Ops:
  0.6 1.0 %copy-start.4 = (bf16[1024,128]{1,0:T(8,128)(2,1)S(1)}, bf16[1024,128]{1,0:T(8,128)(2,1)}, u32[]{:S(2)}) copy-start(bf16[1024,128]{1,0:T(8,128)(2,1)} %k_ref.7) | copy-start | bytes 786436
  1.6 0.9 %copy-start.6 = (bf16[1024,128]{1,0:T(8,128)(2,1)S(1)}, bf16[1024,128]{1,0:T(8,128)(2,1)}, u32[]{:S(2)}) copy-start(bf16[1024,128]{1,0:T(8,128)(2,1)} %v_ref.7) | copy-start | bytes 786436
  2.6 24.3 %collective-permute-start = (bf16[512,256]{1,0:T(8,128)(2,1)S(1)}, bf16[512,256]{1,0:T(8,128)(2,1)S(1)}, u32[]{:S(2)}, u32[]{:S(2)}) collective-permute-start(bf16[512,256]{1,0:T(8,128)(2,1)S(1)} %pack.1), channel_id=1, source_target_pairs={{0,8},{8,16},{16,24},{24,32},{32,40},{40,48},{48,56},{56,64},{64,7... | collective-permute-start | bytes 786440 | tf_op jit(solution)/shard_map/ppermute | solution.py:246
  5.3 1.6 %copy-start = (bf16[1024,1024]{1,0:T(8,128)(2,1)S(1)}, bf16[1024,1024]{1,0:T(8,128)(2,1)}, u32[]{:S(2)}) copy-start(bf16[1024,1024]{1,0:T(8,128)(2,1)} %q_ref.5) | copy-start | bytes 6291460
  6.9 1.6 %copy-start.1 = (bf16[1024,1024]{1,0:T(8,128)(2,1)S(1)}, bf16[1024,1024]{1,0:T(8,128)(2,1)}, u32[]{:S(2)}) copy-start(bf16[1024,1024]{1,0:T(8,128)(2,1)} %do_ref.5) | copy-start | bytes 6291460
  8.5 0.9 %copy-start.5 = (bf16[1024,128]{1,0:T(8,128)(2,1)S(1)}, bf16[1024,128]{1,0:T(8,128)(2,1)}, u32[]{:S(2)}) copy-start(bf16[1024,128]{1,0:T(8,128)(2,1)} %k_ref.7) | copy-start | bytes 786436
  9.5 0.9 %copy-start.7 = (bf16[1024,128]{1,0:T(8,128)(2,1)S(1)}, bf16[1024,128]{1,0:T(8,128)(2,1)}, u32[]{:S(2)}) copy-start(bf16[1024,128]{1,0:T(8,128)(2,1)} %v_ref.7) | copy-start | bytes 786436
  10.4 0.8 copy-start.8
  11.2 0.8 copy-start.10
  11.9 0.8 copy-start.11
  35.9 5.8 %collective-permute-start.1 = (bf16[512,256]{1,0:T(8,128)(2,1)S(1)}, bf16[512,256]{1,0:T(8,128)(2,1)S(1)}, u32[]{:S(2)}, u32[]{:S(2)}) collective-permute-start(bf16[512,256]{1,0:T(8,128)(2,1)S(1)} %get-tuple-element.39), channel_id=1, source_target_pairs={{0,120},{8,0},{16,8},{24,16},{32,24},{40,32},{48,40},{56,48},{64,5... | collective-permute-start | bytes 786440 | tf_op jit(solution)/shard_map/ppermute | solution.py:296
  35.9 5.8 %copy-start.12 = (bf16[16,128]{1,0:T(8,128)(2,1)S(1)}, bf16[16,128]{1,0:T(8,128)(2,1)}, u32[]{:S(2)}) copy-start(bf16[16,128]{1,0:T(8,128)(2,1)} %up_ref.7) | copy-start | bytes 12292
  41.7 18.8 %copy-start.2 = (bf16[1024,1024]{1,0:T(8,128)(2,1)S(1)}, bf16[1024,1024]{1,0:T(8,128)(2,1)}, u32[]{:S(2)}) copy-start(bf16[1024,1024]{1,0:T(8,128)(2,1)} %get-tuple-element.23.dq_ref) | copy-start | bytes 6291460
  41.7 18.8 %copy-start.3 = (bf16[1024,1024]{1,0:T(8,128)(2,1)S(1)}, bf16[1024,1024]{1,0:T(8,128)(2,1)}, u32[]{:S(2)}) copy-start(bf16[1024,1024]{1,0:T(8,128)(2,1)} %x_ref.3) | copy-start | bytes 6291460
  42.7 17.8 %copy-start.9 = (bf16[1024,128]{1,0:T(8,128)(2,1)S(1)}, bf16[1024,128]{1,0:T(8,128)(2,1)}, u32[]{:S(2)}) copy-start(bf16[1024,128]{1,0:T(8,128)(2,1)} %get-tuple-element.25.gv_ref) | copy-start | bytes 786436
  61.9 4.9 %collective-permute-start.2 = (f32[56,512]{1,0:T(8,128)S(1)}, f32[56,512]{1,0:T(8,128)S(1)}, u32[]{:S(2)}, u32[]{:S(2)}) collective-permute-start(f32[56,512]{1,0:T(8,128)S(1)} %get-tuple-element.48), channel_id=1, source_target_pairs={{0,8},{8,0},{16,24},{24,16},{32,40},{40,32},{48,56},{56,48},{64,72... | collective-permute-start | bytes 344072 | tf_op jit(solution)/shard_map/ppermute | solution.py:346
  83.2 2.6 %collective-permute-start.3 = (f32[56,512]{1,0:T(8,128)S(1)}, f32[56,512]{1,0:T(8,128)S(1)}, u32[]{:S(2)}, u32[]{:S(2)}) collective-permute-start(f32[56,512]{1,0:T(8,128)S(1)} %convert_reduce_fusion.mine_ref), channel_id=1, source_target_pairs={{0,8},{8,0},{16,24},{24,16},{32,40},{40,32},{48,56},{56,48},{64,72... | collective-permute-start | bytes 344072 | tf_op jit(solution)/shard_map/ppermute | solution.py:356

commit v3 on v2

--- a/solution.py
+++ b/solution.py
@@ -19,7 +19,7 @@
 F32 = jnp.float32
 BF16 = jnp.bfloat16
 NT = (((1,), (1,)), ((), ()))
-LARGE = pltpu.CompilerParams(vmem_limit_bytes=48 * 2**20)
+LARGE = pltpu.CompilerParams(vmem_limit_bytes=60 * 2**20)
 SMALL = pltpu.CompilerParams(vmem_limit_bytes=24 * 2**20)
 
 
@@ -91,8 +91,8 @@
         dv_ref[...] = jnp.zeros_like(dv_ref)
         bq_ref[...] = jnp.zeros_like(bq_ref)
 
-    low_ref[:RANK] = lax.dot_general(qd_ref[...], x_ref[...], NT, preferred_element_type=F32).astype(BF16)
-    low_ref[RANK:] = lax.dot_general(vd_ref[...], x_ref[...], NT, preferred_element_type=F32).astype(BF16)
+    downs = jnp.concatenate([qd_ref[...], vd_ref[...]], 0)
+    low_ref[...] = lax.dot_general(downs, x_ref[...], NT, preferred_element_type=F32).astype(BF16)
 
     def add(ks, dk, dv):
         dk_ref[ks] += dk
@@ -141,22 +141,28 @@
 
 
 def late_kernel(
-    q_ref, do_ref, k_ref, v_ref, up_ref, _, dq_ref, dk_ref, dv_ref, bq_ref, twice_ref, kt_ref
+    q_ref, do_ref, k_ref, v_ref, up_ref, _, dka_ref, dva_ref, bqa_ref, dkb_ref, dvb_ref, bqb_ref,
+    dq_ref, gk_ref, gv_ref, dk_ref, dv_ref, bq_ref, twice_ref, kt_ref, dk_sum, dv_sum, bq_sum,
 ):
     twice_ref[:, :HD] = k_ref[...]
     twice_ref[:, HD:] = k_ref[...]
     kt_ref[...] = k_ref[...].T
-    dk_ref[...] = jnp.zeros_like(dk_ref)
-    dv_ref[...] = jnp.zeros_like(dv_ref)
-    bq_ref[...] = jnp.zeros_like(bq_ref)
+    dk_sum[...] = jnp.zeros_like(dk_sum)
+    dv_sum[...] = dva_ref[HALF:]
+    bq_sum[...] = bqa_ref[:, HALF:]
+    gk_ref[...] = (dka_ref[:HALF] + dkb_ref[...]).astype(BF16)
+    gv_ref[...] = (dva_ref[:HALF] + dvb_ref[...]).astype(BF16)
+    bq_ref[:, :HALF] = (bqa_ref[:, :HALF] + bqb_ref[...]).astype(BF16)
 
     def add(ks, dk, dv):
-        dk_ref[ks] += dk
-        dv_ref[ks] += dv
+        dk_sum[ks] += dk
+        dv_sum[ks] += dv
 
     jobs = [(head, at, slice(0, at + BLOCK)) for head in range(4) for at in range(0, HALF, BLOCK)]
-    sweep(jobs, q_ref, do_ref, up_ref, twice_ref, v_ref, kt_ref, dq_ref, bq_ref, add)
-    dk_ref[...] = dk_ref[...] * SCALE
+    sweep(jobs, q_ref, do_ref, up_ref, twice_ref, v_ref, kt_ref, dq_ref, bq_sum, add)
+    dk_ref[...] = dka_ref[HALF:] + dk_sum[...] * SCALE
+    dv_ref[...] = dv_sum[...]
+    bq_ref[:, HALF:] = bq_sum[...].astype(BF16)
 
 
 def pack_kernel(k_ref, v_ref, kv_ref):
@@ -165,20 +171,16 @@
 
 
 def close_kernel(
-    dk_ref, dv_ref, dkb_ref, dvb_ref, dkc_ref, dvc_ref, back_ref, bq_ref, bqb_ref, bqc_ref, low_ref, up_ref,
-    gk_ref, gv_ref, share_ref,
+    top_k_ref, top_v_ref, dk_ref, dv_ref, back_ref, bq_ref, low_ref, up_ref, gk_ref, gv_ref, share_ref
 ):
-    gk_ref[:HALF] = (dk_ref[:HALF] + dkb_ref[...]).astype(BF16)
-    gk_ref[HALF:] = (dk_ref[HALF:] + dkc_ref[...] + back_ref[:, :HD].astype(F32)).astype(BF16)
-    gv_ref[:HALF] = (dv_ref[:HALF] + dvb_ref[...]).astype(BF16)
-    gv_ref[HALF:] = (dv_ref[HALF:] + dvc_ref[...] + back_ref[:, HD:].astype(F32)).astype(BF16)
+    gk_ref[:HALF] = top_k_ref[...]
+    gk_ref[HALF:] = (dk_ref[...] + back_ref[:, :HD].astype(F32)).astype(BF16)
+    gv_ref[:HALF] = top_v_ref[...]
+    gv_ref[HALF:] = (dv_ref[...] + back_ref[:, HD:].astype(F32)).astype(BF16)
     bv = lax.dot_general(up_ref[...], gv_ref[...], NT, preferred_element_type=F32).astype(BF16)
-    bq_low = (bq_ref[:, :HALF] + bqb_ref[...]).astype(BF16)
-    bq_high = (bq_ref[:, HALF:] + bqc_ref[...]).astype(BF16)
     for peer in range(share_ref.shape[0]):
         share_ref[peer, : 2 * RANK] = low_ref[...]
-        share_ref[peer, 2 * RANK : 3 * RANK, :HALF] = bq_low
-        share_ref[peer, 2 * RANK : 3 * RANK, HALF:] = bq_high
+        share_ref[peer, 2 * RANK : 3 * RANK] = bq_ref[...]
         share_ref[peer, 3 * RANK :] = bv
 
 
@@ -240,7 +242,7 @@
         in_specs=[bottom, bottom],
         out_specs=whole(HALF, 2 * HD),
         out_shape=struct(HALF, 2 * HD, dtype=BF16),
-        compiler_params=SMALL,
+        compiler_params=LARGE,
         name="pack",
     )(key, value)
     kv = lax.ppermute(kv, "seq", [(s, (s + 1) % seq) for s in range(seq)])
@@ -296,17 +298,28 @@
     back = lax.ppermute(back, "seq", [(s, (s - 1) % seq) for s in range(seq)])
 
     corner = pl.BlockSpec((HALF, 4 * HD), lambda h: (1, 1))
-    dq, dk_c, dv_c, bq_c = pl.pallas_call(
+    dq, top_k, top_v, dk, dv, bq = pl.pallas_call(
         late_kernel,
         grid=(1,),
-        in_specs=[corner, corner, bottom, bottom, pl.BlockSpec((RANK, 4 * HD), lambda h: (0, 1)), untouched],
-        out_specs=[corner, whole(HALF, HD), whole(HALF, HD), whole(RANK, HALF)],
-        out_shape=[struct(ROWS, WIDTH, dtype=BF16), struct(HALF, HD), struct(HALF, HD), struct(RANK, HALF)],
-        scratch_shapes=[pltpu.VMEM((HALF, 2 * HD), BF16), pltpu.VMEM((HD, HALF), BF16)],
+        in_specs=[corner, corner, bottom, bottom, pl.BlockSpec((RANK, 4 * HD), lambda h: (0, 1)), untouched]
+        + [whole(ROWS, HD), whole(ROWS, HD), whole(RANK, ROWS)]
+        + [whole(HALF, HD), whole(HALF, HD), whole(RANK, HALF)],
+        out_specs=[corner] + [whole(HALF, HD)] * 4 + [whole(RANK, ROWS)],
+        out_shape=[struct(ROWS, WIDTH, dtype=BF16)]
+        + [struct(HALF, HD, dtype=BF16)] * 2
+        + [struct(HALF, HD)] * 2
+        + [struct(RANK, ROWS, dtype=BF16)],
+        scratch_shapes=[
+            pltpu.VMEM((HALF, 2 * HD), BF16),
+            pltpu.VMEM((HD, HALF), BF16),
+            pltpu.VMEM((HALF, HD), F32),
+            pltpu.VMEM((HALF, HD), F32),
+            pltpu.VMEM((RANK, HALF), F32),
+        ],
         input_output_aliases={5: 0},
         compiler_params=LARGE,
         name="late",
-    )(query, cotangent, key, value, q_up, dq)
+    )(query, cotangent, key, value, q_up, dq, dk, dv, bq, dk_b, dv_b, bq_b)
 
     grad_key, grad_value, share = pl.pallas_call(
         close_kernel,
@@ -315,9 +328,9 @@
             struct(ROWS, HD, dtype=BF16),
             struct(tensor, 4 * RANK, ROWS, dtype=BF16),
         ],
-        compiler_params=SMALL,
+        compiler_params=LARGE,
         name="close",
-    )(dk, dv, dk_b, dv_b, dk_c, dv_c, back, bq, bq_b, bq_c, low, v_up)
+    )(top_k, top_v, dk, dv, back, bq, low, v_up)
     gathered = lax.all_to_all(share, "tensor", 0, 0)
 
     down = lambda h: (h, 0)

time: 87.1 us -> 87.9 us (level)
  Pallas kernels: 30.3 us -> 37.3 us
  local copies, waits for them, and re-layouts: 9.29 us -> 3.04 us
  waiting for transfers between devices: 3.74 us -> 1.97 us
  starting transfers between devices: 8.32 us -> 10 us
    unnamed x26 -> x10, local copies, waits for them, and re-layouts: 9.26 us -> 3.01 us
    pallas_call x1, Pallas kernels: 3.98 us -> 5.95 us  [on_device(): pl.pallas_call(late_kernel, grid=(1,), in_specs=[corner, corner, bottom,...]
    ppermute x1, waiting for transfers between devices: 1.81 us -> 0.04 us  [on_device(): back = lax.ppermute(back, 'seq', [(s, (s - 1) % seq) for s in range(seq)])]
    pallas_call x1, Pallas kernels: 0.05 us -> 1.72 us  [on_device(): pl.pallas_call(pack_kernel, grid=(1,), in_specs=[bottom, bottom], out_spe...]
    all_to_all x1, blocking collectives: 16.4 us -> 18 us  [on_device(): lax.all_to_all(jnp.broadcast_to(part[None], (chips,) + part.shape), 'seq'...]
    ppermute x1, starting transfers between devices: 3.92 us -> 5.47 us  [on_device(): part = (keep + lax.ppermute(give, 'seq', swap)).astype(BF16)]
    pallas_call x1, Pallas kernels: 1 us -> 2.48 us  [on_device(): pl.pallas_call(close_kernel, out_shape=[struct(ROWS, HD, dtype=BF16), str...]
    pallas_call x1, Pallas kernels: 9.03 us -> 10.5 us  [on_device(): pl.pallas_call(cross_kernel, grid=(2,), in_specs=[pl.BlockSpec((HALF, 2 *...]
  transfers between devices with their start and end apart: 4 -> 4, of which waited for: 3 -> 2; matrix products, arithmetic and copies ran while one was open for 0% -> 0% of each run, Pallas kernels for 21% -> 24%
where the time goes in v3:
time: 87.9 us; the launch traced here: 87.6 us
  Pallas kernels  37.3 us (42%)
  blocking collectives  34.4 us (39%)
  starting transfers between devices  10 us (11%)
  local copies, waits for them, and re-layouts  3.04 us (3%)
  waiting for transfers between devices  1.97 us (2%)
    all_to_all x1, blocking collectives, on_device(): lax.all_to_all(jnp.broadcast_to(part[None], (chips,) + part.shape), 'seq'...  18 us
    all_to_all x1, blocking collectives, on_device(): gathered = lax.all_to_all(share, 'tensor', 0, 0)  16.4 us
    pallas_call x1, Pallas kernels, on_device(): pl.pallas_call(plain_kernel, grid=(2,), in_specs=[pl.BlockSpec((ROWS, 2 *...  14.7 us
    pallas_call x1, Pallas kernels, on_device(): pl.pallas_call(cross_kernel, grid=(2,), in_specs=[pl.BlockSpec((HALF, 2 *...  10.5 us
    pallas_call x1, Pallas kernels, on_device(): pl.pallas_call(late_kernel, grid=(1,), in_specs=[corner, corner, bottom,...  5.95 us
    ppermute x1, starting transfers between devices, on_device(): part = (keep + lax.ppermute(give, 'seq', swap)).astype(BF16)  5.47 us
    unnamed x10, local copies, waits for them, and re-layouts  3.01 us
    ppermute x1, starting transfers between devices, on_device(): kv = lax.ppermute(kv, 'seq', [(s, (s + 1) % seq) for s in range(seq)])  2.69 us
  transfers between devices with their start and end apart: 4, of which 2 were waited for; matrix products, arithmetic and copies ran while one was open for 0% of the time, Pallas kernels for 24%

profile of v3, /device:TPU:1, one launch (start us, length us, event | category | flops | bytes accessed | tf_op | source)
XLA Modules:
  0.0 87.6 jit_solution(9706669704129496201)
XLA Ops:
  0.6 1.7 %pack.1 = bf16[512,256]{1,0:T(8,128)(2,1)} custom-call(bf16[1024,128]{1,0:T(8,128)(2,1)} %k_ref.7, bf16[1024,128]{1,0:T(8,128)(2,1)} %v_ref.7), custom_call_target="tpu_custom_call" | custom-call | tf_op jit(solution)/shard_map/pack/pallas_call | solution.py:239
  2.4 2.7 %collective-permute-start = (bf16[512,256]{1,0:T(8,128)(2,1)}, bf16[512,256]{1,0:T(8,128)(2,1)S(1)}, u32[]{:S(2)}, u32[]{:S(2)}) collective-permute-start(bf16[512,256]{1,0:T(8,128)(2,1)} %pack.1), channel_id=1, source_target_pairs={{0,8},{8,16},{16,24},{24,32},{32,40},{40,48},{48,56},{56,64},{64,7... | collective-permute-start | bytes 786440 | tf_op jit(solution)/shard_map/ppermute | solution.py:248
  5.0 14.7 %plain.1 = (bf16[1024,1024]{1,0:T(8,128)(2,1)}, f32[1024,128]{1,0:T(8,128)}, f32[1024,128]{1,0:T(8,128)}, f32[16,1024]{1,0:T(8,128)}, bf16[32,1024]{1,0:T(8,128)(2,1)}) custom-call(bf16[1024,1024]{1,0:T(8,128)(2,1)} %q_ref.5, bf16[1024,1024]{1,0:T(8,128)(2,1)} %do_ref.5, bf16[1024,128]{1,0:T(8,128)(2,1)} %k_ref.7, bf16[1024,128]{1,0:T(8,128)(2,1)} %v_ref.7, ...), custom_call_target="tpu_custom_call" | custom-call | tf_op jit(solution)/shard_map/plain/pallas_call | solution.py:251
  19.7 0.0 collective-permute-done.kv_ref
  19.7 0.0 copy-start.3
  19.7 0.7 copy-done.3
  20.4 10.5 %cross.1 = (bf16[1024,1024]{1,0:T(8,128)(2,1)}, f32[512,128]{1,0:T(8,128)}, f32[512,128]{1,0:T(8,128)}, f32[16,512]{1,0:T(8,128)}, bf16[512,256]{1,0:T(8,128)(2,1)}) custom-call(bf16[1024,1024]{1,0:T(8,128)(2,1)} %q_ref.5, bf16[1024,1024]{1,0:T(8,128)(2,1)} %do_ref.5, bf16[1024,128]{1,0:T(8,128)(2,1)} %k_ref.7, ...), custom_call_target="tpu_custom_call", output_to_operand_aliasing={{0}: (6, {})} | custom-call | tf_op jit(solution)/shard_map/cross/pallas_call | solution.py:273
  30.9 0.2 collective-permute-start.1
  31.1 5.9 %late.1 = (bf16[1024,1024]{1,0:T(8,128)(2,1)}, bf16[512,128]{1,0:T(8,128)(2,1)}, bf16[512,128]{1,0:T(8,128)(2,1)}, f32[512,128]{1,0:T(8,128)}, f32[512,128]{1,0:T(8,128)}, /*index=5*/bf16[16,1024]{1,0:T(8,128)(2,1)}) custom-call(bf16[1024,1024]{1,0:T(8,128)(2,1)} %q_ref.5, bf16[1024,1024]{1,0:T(8,128)(2,1)} %do_ref.5, ...), custom_call_target="tpu_custom_call", output_to_operand_aliasing={{0}: (5, {})} | custom-call | tf_op jit(solution)/shard_map/late/pallas_call | solution.py:301
  37.1 0.0 copy-start
  37.1 0.0 collective-permute-done.1.back_ref
  37.1 0.0 copy-start.4
  37.1 0.7 copy-done.4
  37.8 2.5 %close.1 = (bf16[1024,128]{1,0:T(8,128)(2,1)}, bf16[1024,128]{1,0:T(8,128)(2,1)}, bf16[8,64,1024]{2,1,0:T(8,128)(2,1)}) custom-call(bf16[512,128]{1,0:T(8,128)(2,1)} %get-tuple-element.41.top_k_ref, bf16[512,128]{1,0:T(8,128)(2,1)} %get-tuple-element.42.top_v_ref, f32[512,128]{1,0:T(8,128)} %get-tuple-element.43.dk_ref, ...), custom_call_target="tpu_custom_call" | custom-call | tf_op jit(solution)/shard_map/close/pallas_call | solution.py:324
  40.3 0.0 copy-start.2
  40.3 16.4 %all_to_all.10.all_ref = bf16[8,64,1024]{2,1,0:T(8,128)(2,1)S(1)} all-to-all(bf16[8,64,1024]{2,1,0:T(8,128)(2,1)} %get-tuple-element.50), channel_id=1, replica_groups=mesh['seq'=16,'tensor'=8] {'tensor'}, dimensions={0} | all-to-all | bytes 2097152 | tf_op jit(solution)/shard_map/all_to_all | solution.py:334
  56.7 0.0 copy-done
  56.7 0.0 copy-done.2
  56.7 0.0 copy-start.1
  56.7 1.6 %copy-done.1 = bf16[1024,1024]{1,0:T(8,128)(2,1)S(1)} copy-done((bf16[1024,1024]{1,0:T(8,128)(2,1)S(1)}, bf16[1024,1024]{1,0:T(8,128)(2,1)}, u32[]{:S(2)}) %copy-start.1) | copy-done | bytes 2097176
  58.3 1.4 %weights.1 = (f32[56,512]{1,0:T(8,128)S(1)}, f32[56,512]{1,0:T(8,128)S(1)}) custom-call(bf16[8,64,1024]{2,1,0:T(8,128)(2,1)S(1)} %all_to_all.10.all_ref, bf16[1024,1024]{1,0:T(8,128)(2,1)S(1)} %copy-done.1, bf16[1024,1024]{1,0:T(8,128)(2,1)S(1)} %copy-done, bf16[1024,128]{1,0:T(8,128)(2,1)S(1)} %copy-done.2), custom_call_target="tpu_custom_call" | custom-call | tf_op jit(solution)/shard_map/weights/pallas_call | solution.py:338
  59.7 5.5 %collective-permute-start.2 = (f32[56,512]{1,0:T(8,128)S(1)}, f32[56,512]{1,0:T(8,128)S(1)}, u32[]{:S(2)}, u32[]{:S(2)}) collective-permute-start(f32[56,512]{1,0:T(8,128)S(1)} %get-tuple-element.52), channel_id=1, source_target_pairs={{0,8},{8,0},{16,24},{24,16},{32,40},{40,32},{48,56},{56,48},{64,72... | collective-permute-start | bytes 344072 | tf_op jit(solution)/shard_map/ppermute | solution.py:359
  65.2 1.0 %collective-permute-done.2 = f32[56,512]{1,0:T(8,128)S(1)} collective-permute-done((f32[56,512]{1,0:T(8,128)S(1)}, f32[56,512]{1,0:T(8,128)S(1)}, u32[]{:S(2)}, u32[]{:S(2)}) %collective-permute-start.2) | collective-permute-done | bytes 114720 | tf_op jit(solution)/shard_map/ppermute | solution.py:359
  66.2 18.0 %all_to_all.11 = bf16[8,56,512]{2,1,0:T(8,128)(2,1)S(1)} all-to-all(bf16[8,56,512]{2,1,0:T(8,128)(2,1)S(1)} %broadcast_in_dim.2), channel_id=1, replica_groups={{0,16,32,48,64,80,96,112},{8,24,40,56,72,88,104,120},{1,17,33,49,65,81,..., dimensions={0} | all-to-all | bytes 917504 | tf_op jit(solution)/shard_map/all_to_all | solution.py:361
  84.2 0.1 convert_reduce_fusion.mine_ref
  84.3 1.7 %collective-permute-start.3 = (f32[56,512]{1,0:T(8,128)S(1)}, f32[56,512]{1,0:T(8,128)S(1)}, u32[]{:S(2)}, u32[]{:S(2)}) collective-permute-start(f32[56,512]{1,0:T(8,128)S(1)} %convert_reduce_fusion.mine_ref), channel_id=1, source_target_pairs={{0,8},{8,0},{16,24},{24,16},{32,40},{40,32},{48,56},{56,48},{64,72... | collective-permute-start | bytes 344072 | tf_op jit(solution)/shard_map/ppermute | solution.py:369
  85.9 1.0 %collective-permute-done.3.other_ref = f32[56,512]{1,0:T(8,128)S(1)} collective-permute-done((f32[56,512]{1,0:T(8,128)S(1)}, f32[56,512]{1,0:T(8,128)S(1)}, u32[]{:S(2)}, u32[]{:S(2)}) %collective-permute-start.3) | collective-permute-done | bytes 114720 | tf_op jit(solution)/shard_map/ppermute | solution.py:369
  86.9 0.7 place.1
  (2 shorter events, 0.0 us)
Async XLA Ops:
  2.4 17.3 %collective-permute-start = (bf16[512,256]{1,0:T(8,128)(2,1)}, bf16[512,256]{1,0:T(8,128)(2,1)S(1)}, u32[]{:S(2)}, u32[]{:S(2)}) collective-permute-start(bf16[512,256]{1,0:T(8,128)(2,1)} %pack.1), channel_id=1, source_target_pairs={{0,8},{8,16},{16,24},{24,32},{32,40},{40,48},{48,56},{56,64},{64,7... | collective-permute-start | bytes 786440 | tf_op jit(solution)/shard_map/ppermute | solution.py:248
  19.7 0.7 copy-start.3
  30.9 6.2 %collective-permute-start.1 = (bf16[512,256]{1,0:T(8,128)(2,1)}, bf16[512,256]{1,0:T(8,128)(2,1)S(1)}, u32[]{:S(2)}, u32[]{:S(2)}) collective-permute-start(bf16[512,256]{1,0:T(8,128)(2,1)} %get-tuple-element.45), channel_id=1, source_target_pairs={{0,120},{8,0},{16,8},{24,16},{32,24},{40,32},{48,40},{56,48},{64,5... | collective-permute-start | bytes 786440 | tf_op jit(solution)/shard_map/ppermute | solution.py:298
  37.1 19.7 %copy-start = (bf16[1024,1024]{1,0:T(8,128)(2,1)S(1)}, bf16[1024,1024]{1,0:T(8,128)(2,1)}, u32[]{:S(2)}) copy-start(bf16[1024,1024]{1,0:T(8,128)(2,1)} %get-tuple-element.25.dq_ref) | copy-start | bytes 6291460
  37.1 0.7 copy-start.4
  40.3 16.4 %copy-start.2 = (bf16[1024,128]{1,0:T(8,128)(2,1)S(1)}, bf16[1024,128]{1,0:T(8,128)(2,1)}, u32[]{:S(2)}) copy-start(bf16[1024,128]{1,0:T(8,128)(2,1)} %get-tuple-element.27.gv_ref) | copy-start | bytes 786436
  56.7 1.6 %copy-start.1 = (bf16[1024,1024]{1,0:T(8,128)(2,1)S(1)}, bf16[1024,1024]{1,0:T(8,128)(2,1)}, u32[]{:S(2)}) copy-start(bf16[1024,1024]{1,0:T(8,128)(2,1)} %x_ref.3) | copy-start | bytes 6291460
  59.7 6.4 %collective-permute-start.2 = (f32[56,512]{1,0:T(8,128)S(1)}, f32[56,512]{1,0:T(8,128)S(1)}, u32[]{:S(2)}, u32[]{:S(2)}) collective-permute-start(f32[56,512]{1,0:T(8,128)S(1)} %get-tuple-element.52), channel_id=1, source_target_pairs={{0,8},{8,0},{16,24},{24,16},{32,40},{40,32},{48,56},{56,48},{64,72... | collective-permute-start | bytes 344072 | tf_op jit(solution)/shard_map/ppermute | solution.py:359
  84.3 2.6 %collective-permute-start.3 = (f32[56,512]{1,0:T(8,128)S(1)}, f32[56,512]{1,0:T(8,128)S(1)}, u32[]{:S(2)}, u32[]{:S(2)}) collective-permute-start(f32[56,512]{1,0:T(8,128)S(1)} %convert_reduce_fusion.mine_ref), channel_id=1, source_target_pairs={{0,8},{8,0},{16,24},{24,16},{32,40},{40,32},{48,56},{56,48},{64,72... | collective-permute-start | bytes 344072 | tf_op jit(solution)/shard_map/ppermute | solution.py:369

commit v4 on v3

--- a/solution.py
+++ b/solution.py
@@ -45,17 +45,14 @@
     return p.astype(BF16), (p * (dp - delta)).astype(BF16)
 
 
-def sweep(jobs, q_ref, do_ref, up_ref, twice, values, keys_t, dq_ref, bq_ref, add):
+def sweep(jobs, q_ref, do_ref, up_ref, twice, values, keys_t, dq_ref, dq_t_ref, add):
     tile = lambda ref, head, at: ref[at : at + BLOCK, head * HD : (head + 1) * HD]
     begin = lambda head, at, ks: products(tile(q_ref, head, at), tile(do_ref, head, at), twice[ks], values[ks])
 
     def finish(head, at, ks, p, ds):
         q, do = tile(q_ref, head, at), tile(do_ref, head, at)
-        dq_t = (jnp.dot(keys_t[:, ks], ds, preferred_element_type=F32) * SCALE).astype(BF16)
-        dq_ref[at : at + BLOCK, head * HD : (head + 1) * HD] = dq_t.T
-        bq_ref[:, at : at + BLOCK] += jnp.dot(
-            up_ref[:, head * HD : (head + 1) * HD], dq_t, preferred_element_type=F32
-        )
+        dq_t = jnp.dot(keys_t[:, ks], ds, preferred_element_type=F32) * SCALE
+        dq_t_ref[head * HD : (head + 1) * HD, at : at + BLOCK] = dq_t.astype(BF16)
         add(
             ks,
             jnp.dot(ds, q, preferred_element_type=F32),
@@ -69,6 +66,8 @@
         if n > 0:
             finish(*jobs[n - 1], *softened)
         ready, softened = coming, now
+    dq_ref[...] = dq_t_ref[...].T
+    return jnp.dot(up_ref[...], dq_t_ref[...], preferred_element_type=F32)
 
 
 def first_last():
@@ -78,7 +77,7 @@
 
 def plain_kernel(
     q_ref, do_ref, k_ref, v_ref, up_ref, x_ref, qd_ref, vd_ref,
-    dq_ref, dk_ref, dv_ref, bq_ref, low_ref, twice_ref, kt_ref,
+    dq_ref, dk_ref, dv_ref, bq_ref, low_ref, twice_ref, kt_ref, dqt_ref,
 ):
     first, last = first_last()
 
@@ -99,7 +98,7 @@
         dv_ref[ks] += dv
 
     jobs = [(head, at, slice(0, at + BLOCK)) for head in range(2) for at in range(0, ROWS, BLOCK)]
-    sweep(jobs, q_ref, do_ref, up_ref, twice_ref, v_ref, kt_ref, dq_ref, bq_ref, add)
+    bq_ref[...] += sweep(jobs, q_ref, do_ref, up_ref, twice_ref, v_ref, kt_ref, dq_ref, dqt_ref, add)
 
     @pl.when(last)
     def _():
@@ -108,7 +107,7 @@
 
 def cross_kernel(
     q_ref, do_ref, k_ref, v_ref, kv_ref, up_ref, _,
-    dq_ref, dk_ref, dv_ref, bq_ref, back_ref, twice_ref, values_ref, kt_ref, dkx_ref, dvx_ref,
+    dq_ref, dk_ref, dv_ref, bq_ref, back_ref, twice_ref, values_ref, kt_ref, dkx_ref, dvx_ref, dqt_ref,
 ):
     first, last = first_last()
 
@@ -130,7 +129,7 @@
         dvx_ref[ks] += dv
 
     jobs = [(head, at, slice(0, HALF + at + BLOCK)) for head in range(2) for at in range(0, HALF, BLOCK)]
-    sweep(jobs, q_ref, do_ref, up_ref, twice_ref, values_ref, kt_ref, dq_ref, bq_ref, add)
+    bq_ref[...] += sweep(jobs, q_ref, do_ref, up_ref, twice_ref, values_ref, kt_ref, dq_ref, dqt_ref, add)
 
     @pl.when(last)
     def _():
@@ -142,14 +141,13 @@
 
 def late_kernel(
     q_ref, do_ref, k_ref, v_ref, up_ref, _, dka_ref, dva_ref, bqa_ref, dkb_ref, dvb_ref, bqb_ref,
-    dq_ref, gk_ref, gv_ref, dk_ref, dv_ref, bq_ref, twice_ref, kt_ref, dk_sum, dv_sum, bq_sum,
+    dq_ref, gk_ref, gv_ref, dk_ref, dv_ref, bq_ref, twice_ref, kt_ref, dk_sum, dv_sum, dqt_ref,
 ):
     twice_ref[:, :HD] = k_ref[...]
     twice_ref[:, HD:] = k_ref[...]
     kt_ref[...] = k_ref[...].T
     dk_sum[...] = jnp.zeros_like(dk_sum)
     dv_sum[...] = dva_ref[HALF:]
-    bq_sum[...] = bqa_ref[:, HALF:]
     gk_ref[...] = (dka_ref[:HALF] + dkb_ref[...]).astype(BF16)
     gv_ref[...] = (dva_ref[:HALF] + dvb_ref[...]).astype(BF16)
     bq_ref[:, :HALF] = (bqa_ref[:, :HALF] + bqb_ref[...]).astype(BF16)
@@ -159,10 +157,10 @@
         dv_sum[ks] += dv
 
     jobs = [(head, at, slice(0, at + BLOCK)) for head in range(4) for at in range(0, HALF, BLOCK)]
-    sweep(jobs, q_ref, do_ref, up_ref, twice_ref, v_ref, kt_ref, dq_ref, bq_sum, add)
+    bq = sweep(jobs, q_ref, do_ref, up_ref, twice_ref, v_ref, kt_ref, dq_ref, dqt_ref, add)
     dk_ref[...] = dka_ref[HALF:] + dk_sum[...] * SCALE
     dv_ref[...] = dv_sum[...]
-    bq_ref[:, HALF:] = bq_sum[...].astype(BF16)
+    bq_ref[:, HALF:] = (bqa_ref[:, HALF:] + bq).astype(BF16)
 
 
 def pack_kernel(k_ref, v_ref, kv_ref):
@@ -264,7 +262,11 @@
             struct(RANK, ROWS),
             struct(2 * RANK, ROWS, dtype=BF16),
         ],
-        scratch_shapes=[pltpu.VMEM((ROWS, 2 * HD), BF16), pltpu.VMEM((HD, ROWS), BF16)],
+        scratch_shapes=[
+            pltpu.VMEM((ROWS, 2 * HD), BF16),
+            pltpu.VMEM((HD, ROWS), BF16),
+            pltpu.VMEM((2 * HD, ROWS), BF16),
+        ],
         compiler_params=LARGE,
         name="plain",
     )(query, cotangent, key, value, q_up, x, q_down, v_down)
@@ -290,6 +292,7 @@
             pltpu.VMEM((HD, ROWS), BF16),
             pltpu.VMEM((ROWS, HD), F32),
             pltpu.VMEM((ROWS, HD), F32),
+            pltpu.VMEM((2 * HD, HALF), BF16),
         ],
         input_output_aliases={6: 0},
         compiler_params=LARGE,
@@ -314,7 +317,7 @@
             pltpu.VMEM((HD, HALF), BF16),
             pltpu.VMEM((HALF, HD), F32),
             pltpu.VMEM((HALF, HD), F32),
-            pltpu.VMEM((RANK, HALF), F32),
+            pltpu.VMEM((4 * HD, HALF), BF16),
         ],
         input_output_aliases={5: 0},
         compiler_params=LARGE,

time: 87.9 us -> 83.2 us (0.947)
  Pallas kernels: 37.3 us -> 32.9 us
    pallas_call x1, Pallas kernels: 14.7 us -> 12.5 us  [on_device(): pl.pallas_call(plain_kernel, grid=(2,), in_specs=[pl.BlockSpec((ROWS, 2 *...]
    pallas_call x1, Pallas kernels: 10.5 us -> 8.78 us  [on_device(): pl.pallas_call(cross_kernel, grid=(2,), in_specs=[pl.BlockSpec((HALF, 2 *...]
  transfers between devices with their start and end apart: 4 -> 4, of which waited for: 2 -> 3; matrix products, arithmetic and copies ran while one was open for 0% -> 0% of each run, Pallas kernels for 24% -> 21%
where the time goes in v4:
time: 83.2 us; the launch traced here: 82.9 us
  blocking collectives  34.3 us (41%)
  Pallas kernels  32.9 us (40%)
  starting transfers between devices  9.4 us (11%)
  local copies, waits for them, and re-layouts  3.04 us (4%)
  waiting for transfers between devices  2.57 us (3%)
    all_to_all x1, blocking collectives, on_device(): lax.all_to_all(jnp.broadcast_to(part[None], (chips,) + part.shape), 'seq'...  17.4 us
    all_to_all x1, blocking collectives, on_device(): gathered = lax.all_to_all(share, 'tensor', 0, 0)  16.9 us
    pallas_call x1, Pallas kernels, on_device(): pl.pallas_call(plain_kernel, grid=(2,), in_specs=[pl.BlockSpec((ROWS, 2 *...  12.5 us
    pallas_call x1, Pallas kernels, on_device(): pl.pallas_call(cross_kernel, grid=(2,), in_specs=[pl.BlockSpec((HALF, 2 *...  8.78 us
    pallas_call x1, Pallas kernels, on_device(): pl.pallas_call(late_kernel, grid=(1,), in_specs=[corner, corner, bottom,...  5.35 us
    ppermute x1, starting transfers between devices, on_device(): part = (keep + lax.ppermute(give, 'seq', swap)).astype(BF16)  5.01 us
    unnamed x10, local copies, waits for them, and re-layouts  3.01 us
    ppermute x1, starting transfers between devices, on_device(): kv = lax.ppermute(kv, 'seq', [(s, (s + 1) % seq) for s in range(seq)])  2.69 us
  transfers between devices with their start and end apart: 4, of which 3 were waited for; matrix products, arithmetic and copies ran while one was open for 0% of the time, Pallas kernels for 21%

profile of v4, /device:TPU:1, one launch (start us, length us, event | category | flops | bytes accessed | tf_op | source)
XLA Modules:
  0.0 82.9 jit_solution(16648779626892161172)
XLA Ops:
  0.6 1.7 %pack.1 = bf16[512,256]{1,0:T(8,128)(2,1)} custom-call(bf16[1024,128]{1,0:T(8,128)(2,1)} %k_ref.7, bf16[1024,128]{1,0:T(8,128)(2,1)} %v_ref.7), custom_call_target="tpu_custom_call" | custom-call | tf_op jit(solution)/shard_map/pack/pallas_call | solution.py:237
  2.4 2.7 %collective-permute-start = (bf16[512,256]{1,0:T(8,128)(2,1)}, bf16[512,256]{1,0:T(8,128)(2,1)S(1)}, u32[]{:S(2)}, u32[]{:S(2)}) collective-permute-start(bf16[512,256]{1,0:T(8,128)(2,1)} %pack.1), channel_id=1, source_target_pairs={{0,8},{8,16},{16,24},{24,32},{32,40},{40,48},{48,56},{56,64},{64,7... | collective-permute-start | bytes 786440 | tf_op jit(solution)/shard_map/ppermute | solution.py:246
  5.0 12.5 %plain.1 = (bf16[1024,1024]{1,0:T(8,128)(2,1)}, f32[1024,128]{1,0:T(8,128)}, f32[1024,128]{1,0:T(8,128)}, f32[16,1024]{1,0:T(8,128)}, bf16[32,1024]{1,0:T(8,128)(2,1)}) custom-call(bf16[1024,1024]{1,0:T(8,128)(2,1)} %q_ref.5, bf16[1024,1024]{1,0:T(8,128)(2,1)} %do_ref.5, bf16[1024,128]{1,0:T(8,128)(2,1)} %k_ref.7, bf16[1024,128]{1,0:T(8,128)(2,1)} %v_ref.7, ...), custom_call_target="tpu_custom_call" | custom-call | tf_op jit(solution)/shard_map/plain/pallas_call | solution.py:249
  17.5 0.0 collective-permute-done.kv_ref
  17.5 0.0 copy-start.3
  17.5 0.7 copy-done.3
  18.2 8.8 %cross.1 = (bf16[1024,1024]{1,0:T(8,128)(2,1)}, f32[512,128]{1,0:T(8,128)}, f32[512,128]{1,0:T(8,128)}, f32[16,512]{1,0:T(8,128)}, bf16[512,256]{1,0:T(8,128)(2,1)}) custom-call(bf16[1024,1024]{1,0:T(8,128)(2,1)} %q_ref.5, bf16[1024,1024]{1,0:T(8,128)(2,1)} %do_ref.5, bf16[1024,128]{1,0:T(8,128)(2,1)} %k_ref.7, ...), custom_call_target="tpu_custom_call", output_to_operand_aliasing={{0}: (6, {})} | custom-call | tf_op jit(solution)/shard_map/cross/pallas_call | solution.py:275
  27.0 0.0 collective-permute-start.1
  27.0 5.4 %late.1 = (bf16[1024,1024]{1,0:T(8,128)(2,1)}, bf16[512,128]{1,0:T(8,128)(2,1)}, bf16[512,128]{1,0:T(8,128)(2,1)}, f32[512,128]{1,0:T(8,128)}, f32[512,128]{1,0:T(8,128)}, /*index=5*/bf16[16,1024]{1,0:T(8,128)(2,1)}) custom-call(bf16[1024,1024]{1,0:T(8,128)(2,1)} %q_ref.5, bf16[1024,1024]{1,0:T(8,128)(2,1)} %do_ref.5, ...), custom_call_target="tpu_custom_call", output_to_operand_aliasing={{0}: (5, {})} | custom-call | tf_op jit(solution)/shard_map/late/pallas_call | solution.py:304
  32.4 0.0 copy-start
  32.4 0.6 collective-permute-done.1.back_ref
  33.0 0.0 copy-start.4
  33.0 0.7 copy-done.4
  33.8 2.5 %close.1 = (bf16[1024,128]{1,0:T(8,128)(2,1)}, bf16[1024,128]{1,0:T(8,128)(2,1)}, bf16[8,64,1024]{2,1,0:T(8,128)(2,1)}) custom-call(bf16[512,128]{1,0:T(8,128)(2,1)} %get-tuple-element.41.top_k_ref, bf16[512,128]{1,0:T(8,128)(2,1)} %get-tuple-element.42.top_v_ref, f32[512,128]{1,0:T(8,128)} %get-tuple-element.43.dk_ref, ...), custom_call_target="tpu_custom_call" | custom-call | tf_op jit(solution)/shard_map/close/pallas_call | solution.py:327
  36.2 0.0 copy-start.2
  36.2 16.9 %all_to_all.10.all_ref = bf16[8,64,1024]{2,1,0:T(8,128)(2,1)S(1)} all-to-all(bf16[8,64,1024]{2,1,0:T(8,128)(2,1)} %get-tuple-element.50), channel_id=1, replica_groups=mesh['seq'=16,'tensor'=8] {'tensor'}, dimensions={0} | all-to-all | bytes 2097152 | tf_op jit(solution)/shard_map/all_to_all | solution.py:337
  53.1 0.0 copy-done
  53.1 0.0 copy-done.2
  53.1 0.0 copy-start.1
  53.1 1.6 %copy-done.1 = bf16[1024,1024]{1,0:T(8,128)(2,1)S(1)} copy-done((bf16[1024,1024]{1,0:T(8,128)(2,1)S(1)}, bf16[1024,1024]{1,0:T(8,128)(2,1)}, u32[]{:S(2)}) %copy-start.1) | copy-done | bytes 2097176
  54.7 1.4 %weights.1 = (f32[56,512]{1,0:T(8,128)S(1)}, f32[56,512]{1,0:T(8,128)S(1)}) custom-call(bf16[8,64,1024]{2,1,0:T(8,128)(2,1)S(1)} %all_to_all.10.all_ref, bf16[1024,1024]{1,0:T(8,128)(2,1)S(1)} %copy-done.1, bf16[1024,1024]{1,0:T(8,128)(2,1)S(1)} %copy-done, bf16[1024,128]{1,0:T(8,128)(2,1)S(1)} %copy-done.2), custom_call_target="tpu_custom_call" | custom-call | tf_op jit(solution)/shard_map/weights/pallas_call | solution.py:341
  56.1 5.0 %collective-permute-start.2 = (f32[56,512]{1,0:T(8,128)S(1)}, f32[56,512]{1,0:T(8,128)S(1)}, u32[]{:S(2)}, u32[]{:S(2)}) collective-permute-start(f32[56,512]{1,0:T(8,128)S(1)} %get-tuple-element.52), channel_id=1, source_target_pairs={{0,8},{8,0},{16,24},{24,16},{32,40},{40,32},{48,56},{56,48},{64,72... | collective-permute-start | bytes 344072 | tf_op jit(solution)/shard_map/ppermute | solution.py:362
  61.1 1.0 %collective-permute-done.2 = f32[56,512]{1,0:T(8,128)S(1)} collective-permute-done((f32[56,512]{1,0:T(8,128)S(1)}, f32[56,512]{1,0:T(8,128)S(1)}, u32[]{:S(2)}, u32[]{:S(2)}) %collective-permute-start.2) | collective-permute-done | bytes 114720 | tf_op jit(solution)/shard_map/ppermute | solution.py:362
  62.1 17.4 %all_to_all.11 = bf16[8,56,512]{2,1,0:T(8,128)(2,1)S(1)} all-to-all(bf16[8,56,512]{2,1,0:T(8,128)(2,1)S(1)} %broadcast_in_dim.2), channel_id=1, replica_groups={{0,16,32,48,64,80,96,112},{8,24,40,56,72,88,104,120},{1,17,33,49,65,81,..., dimensions={0} | all-to-all | bytes 917504 | tf_op jit(solution)/shard_map/all_to_all | solution.py:364
  79.5 0.1 convert_reduce_fusion.mine_ref
  79.6 1.7 %collective-permute-start.3 = (f32[56,512]{1,0:T(8,128)S(1)}, f32[56,512]{1,0:T(8,128)S(1)}, u32[]{:S(2)}, u32[]{:S(2)}) collective-permute-start(f32[56,512]{1,0:T(8,128)S(1)} %convert_reduce_fusion.mine_ref), channel_id=1, source_target_pairs={{0,8},{8,0},{16,24},{24,16},{32,40},{40,32},{48,56},{56,48},{64,72... | collective-permute-start | bytes 344072 | tf_op jit(solution)/shard_map/ppermute | solution.py:372
  81.3 1.0 %collective-permute-done.3.other_ref = f32[56,512]{1,0:T(8,128)S(1)} collective-permute-done((f32[56,512]{1,0:T(8,128)S(1)}, f32[56,512]{1,0:T(8,128)S(1)}, u32[]{:S(2)}, u32[]{:S(2)}) %collective-permute-start.3) | collective-permute-done | bytes 114720 | tf_op jit(solution)/shard_map/ppermute | solution.py:372
  82.2 0.7 place.1
  (2 shorter events, 0.0 us)
Async XLA Ops:
  2.4 15.2 %collective-permute-start = (bf16[512,256]{1,0:T(8,128)(2,1)}, bf16[512,256]{1,0:T(8,128)(2,1)S(1)}, u32[]{:S(2)}, u32[]{:S(2)}) collective-permute-start(bf16[512,256]{1,0:T(8,128)(2,1)} %pack.1), channel_id=1, source_target_pairs={{0,8},{8,16},{16,24},{24,32},{32,40},{40,48},{48,56},{56,64},{64,7... | collective-permute-start | bytes 786440 | tf_op jit(solution)/shard_map/ppermute | solution.py:246
  17.5 0.7 copy-start.3
  27.0 6.0 %collective-permute-start.1 = (bf16[512,256]{1,0:T(8,128)(2,1)}, bf16[512,256]{1,0:T(8,128)(2,1)S(1)}, u32[]{:S(2)}, u32[]{:S(2)}) collective-permute-start(bf16[512,256]{1,0:T(8,128)(2,1)} %get-tuple-element.45), channel_id=1, source_target_pairs={{0,120},{8,0},{16,8},{24,16},{32,24},{40,32},{48,40},{56,48},{64,5... | collective-permute-start | bytes 786440 | tf_op jit(solution)/shard_map/ppermute | solution.py:301
  32.4 20.7 %copy-start = (bf16[1024,1024]{1,0:T(8,128)(2,1)S(1)}, bf16[1024,1024]{1,0:T(8,128)(2,1)}, u32[]{:S(2)}) copy-start(bf16[1024,1024]{1,0:T(8,128)(2,1)} %get-tuple-element.25.dq_ref) | copy-start | bytes 6291460
  33.0 0.7 copy-start.4
  36.2 16.9 %copy-start.2 = (bf16[1024,128]{1,0:T(8,128)(2,1)S(1)}, bf16[1024,128]{1,0:T(8,128)(2,1)}, u32[]{:S(2)}) copy-start(bf16[1024,128]{1,0:T(8,128)(2,1)} %get-tuple-element.27.gv_ref) | copy-start | bytes 786436
  53.1 1.6 %copy-start.1 = (bf16[1024,1024]{1,0:T(8,128)(2,1)S(1)}, bf16[1024,1024]{1,0:T(8,128)(2,1)}, u32[]{:S(2)}) copy-start(bf16[1024,1024]{1,0:T(8,128)(2,1)} %x_ref.3) | copy-start | bytes 6291460
  56.1 6.0 %collective-permute-start.2 = (f32[56,512]{1,0:T(8,128)S(1)}, f32[56,512]{1,0:T(8,128)S(1)}, u32[]{:S(2)}, u32[]{:S(2)}) collective-permute-start(f32[56,512]{1,0:T(8,128)S(1)} %get-tuple-element.52), channel_id=1, source_target_pairs={{0,8},{8,0},{16,24},{24,16},{32,40},{40,32},{48,56},{56,48},{64,72... | collective-permute-start | bytes 344072 | tf_op jit(solution)/shard_map/ppermute | solution.py:362
  79.6 2.6 %collective-permute-start.3 = (f32[56,512]{1,0:T(8,128)S(1)}, f32[56,512]{1,0:T(8,128)S(1)}, u32[]{:S(2)}, u32[]{:S(2)}) collective-permute-start(f32[56,512]{1,0:T(8,128)S(1)} %convert_reduce_fusion.mine_ref), channel_id=1, source_target_pairs={{0,8},{8,0},{16,24},{24,16},{32,40},{40,32},{48,56},{56,48},{64,72... | collective-permute-start | bytes 344072 | tf_op jit(solution)/shard_map/ppermute | solution.py:372

commit v5 on v4

v5 whole, which is shorter than its diff:
```python
import math

import jax
import jax.numpy as jnp
from jax import lax
from jax.experimental import pallas as pl
from jax.experimental.pallas import tpu as pltpu
from jax.sharding import PartitionSpec as P

HD = 128
RANK = 16
STEADY = 4
ROWS = 1024
HALF = 512
WIDTH = 1024
BLOCK = 256
SCALE = 1.0 / math.sqrt(HD)
FOLDED = SCALE * 1.4426950408889634
F32 = jnp.float32
BF16 = jnp.bfloat16
NT = (((1,), (1,)), ((), ()))
LARGE = pltpu.CompilerParams(vmem_limit_bytes=60 * 2**20)
SMALL = pltpu.CompilerParams(vmem_limit_bytes=24 * 2**20)


def products(q, do, keys_twice, values):
    scaled = q.astype(F32) * FOLDED
    big = scaled.astype(BF16)
    rest = (scaled - big.astype(F32)).astype(BF16)
    s = lax.dot_general(keys_twice, jnp.concatenate([big, rest], 1), NT, preferred_element_type=F32)
    dp = lax.dot_general(values, do, NT, preferred_element_type=F32)
    return s, dp


def softmax_back(s, dp):
    length, size = s.shape
    row = lax.broadcasted_iota(jnp.int32, (size, size), 0)
    col = lax.broadcasted_iota(jnp.int32, (size, size), 1)
    own = jnp.where(row <= col, s[length - size :], -1e30)
    s = jnp.concatenate([s[: length - size], own], 0) if length > size else own
    e = jnp.exp2(s - jnp.max(s, axis=0, keepdims=True))
    r = 1.0 / jnp.sum(e, axis=0, keepdims=True)
    delta = jnp.sum(e * dp, axis=0, keepdims=True) * r
    p = e * r
    return p.astype(BF16), (p * (dp - delta)).astype(BF16)


def sweep(jobs, q_ref, do_ref, up_ref, twice, values, keys_t, dq_ref, dq_t_ref, add):
    tile = lambda ref, head, at: ref[at : at + BLOCK, head * HD : (head + 1) * HD]
    begin = lambda head, at, ks: products(tile(q_ref, head, at), tile(do_ref, head, at), twice[ks], values[ks])

    def finish(head, at, ks, p, ds):
        q, do = tile(q_ref, head, at), tile(do_ref, head, at)
        dq_t = jnp.dot(keys_t[:, ks], ds, preferred_element_type=F32) * SCALE
        dq_t_ref[head * HD : (head + 1) * HD, at : at + BLOCK] = dq_t.astype(BF16)
        add(
            ks,
            jnp.dot(ds, q, preferred_element_type=F32),
            jnp.dot(p, do, preferred_element_type=F32),
        )

    ready, softened = begin(*jobs[0]), None
    for n in range(len(jobs) + 1):
        coming = begin(*jobs[n + 1]) if n + 1 < len(jobs) else None
        now = softmax_back(*ready) if n < len(jobs) else None
        if n > 0:
            finish(*jobs[n - 1], *softened)
        ready, softened = coming, now
    dq_ref[...] = dq_t_ref[...].T
    return jnp.dot(up_ref[...], dq_t_ref[...], preferred_element_type=F32)


def first_last():
    step = pl.program_id(0)
    return step == 0, step == pl.num_programs(0) - 1


def plain_kernel(
    q_ref, do_ref, k_ref, v_ref, up_ref, x_ref, qd_ref, vd_ref,
    dq_ref, dk_ref, dv_ref, bq_ref, low_ref, lent_ref, twice_ref, kt_ref, dqt_ref,
):
    first, last = first_last()

    @pl.when(first)
    def _():
        twice_ref[:, :HD] = k_ref[...]
        twice_ref[:, HD:] = k_ref[...]
        kt_ref[...] = k_ref[...].T
        dk_ref[...] = jnp.zeros_like(dk_ref)
        dv_ref[...] = jnp.zeros_like(dv_ref)
        bq_ref[...] = jnp.zeros_like(bq_ref)

    downs = jnp.concatenate([qd_ref[...], vd_ref[...]], 0)
    low_ref[...] = lax.dot_general(downs, x_ref[...], NT, preferred_element_type=F32).astype(BF16)

    def add(ks, dk, dv):
        dk_ref[ks] += dk
        dv_ref[ks] += dv

    jobs = [(head, at, slice(0, at + BLOCK)) for head in range(2) for at in range(0, ROWS, BLOCK)]
    bq_ref[...] += sweep(jobs, q_ref, do_ref, up_ref, twice_ref, v_ref, kt_ref, dq_ref, dqt_ref, add)

    @pl.when(last)
    def _():
        lent_ref[...] = x_ref[...]


def rolled_kernel(
    q_ref, do_ref, k_ref, v_ref, kv_ref, up_ref, _, dka_ref, dva_ref, bqa_ref, low_ref, vu_ref,
    dq_ref, back_ref, top_ref, dk_ref, dv_ref, share_ref,
    twice_ref, values_ref, kt_ref, dk_sum, dv_sum, bq_sum, dqt_ref,
):
    first, last = first_last()

    @pl.when(first)
    def _():
        for part in (slice(0, HD), slice(HD, 2 * HD)):
            twice_ref[:HALF, part] = kv_ref[:, :HD]
            twice_ref[HALF:, part] = k_ref[...]
        values_ref[:HALF] = kv_ref[:, HD:]
        values_ref[HALF:] = v_ref[...]
        kt_ref[:, :HALF] = kv_ref[:, :HD].T
        kt_ref[:, HALF:] = k_ref[...].T
        dk_sum[:HALF] = jnp.zeros((HALF, HD), F32)
        dv_sum[:HALF] = jnp.zeros((HALF, HD), F32)
        dk_sum[HALF:] = dka_ref[...]
        dv_sum[HALF:] = dva_ref[...]
        bq_sum[...] = bqa_ref[...]

    def add(ks, dk, dv):
        dk_sum[ks] += dk
        dv_sum[ks] += dv

    jobs = []
    for head in range(2):
        for at in range(0, ROWS, BLOCK):
            jobs.append((head, at, slice(0 if at < HALF else ROWS, HALF + at + BLOCK)))
    bq_sum[...] += sweep(jobs, q_ref, do_ref, up_ref, twice_ref, values_ref, kt_ref, dq_ref, dqt_ref, add)

    @pl.when(last)
    def _():
        dv_low = dv_sum[...].astype(BF16)
        bv = lax.dot_general(vu_ref[...], dv_low, NT, preferred_element_type=F32).astype(BF16)
        bq = bq_sum[...].astype(BF16)
        rows = [slice(n * RANK, (n + 1) * RANK) for n in range(3)]
        for peer in range(share_ref.shape[0]):
            share_ref[peer, rows[0], :ROWS] = low_ref[:RANK]
            share_ref[peer, rows[1], :ROWS] = low_ref[RANK:]
            share_ref[peer, rows[0], ROWS:] = bv[:, :HALF]
            share_ref[peer, rows[1], ROWS:] = bq[:, :HALF]
            share_ref[peer, rows[2], :HALF] = bq[:, HALF:]
            share_ref[peer, rows[2], HALF:] = bv[:, HALF:]
        back_ref[:, :HD] = (dk_sum[:HALF] * SCALE).astype(BF16)
        back_ref[:, HD:] = dv_low[:HALF]
        top_ref[:, :HD] = (dk_sum[HALF:ROWS] * SCALE).astype(BF16)
        top_ref[:, HD:] = dv_low[HALF:ROWS]
        dk_ref[...] = dk_sum[ROWS:] * SCALE
        dv_ref[...] = dv_sum[ROWS:]


def pack_kernel(k_ref, v_ref, kv_ref):
    kv_ref[:, :HD] = k_ref[...]
    kv_ref[:, HD:] = v_ref[...]


def finish_kernel(top_ref, dk_ref, dv_ref, back_ref, gk_ref, gv_ref):
    gk_ref[:HALF] = top_ref[:, :HD]
    gv_ref[:HALF] = top_ref[:, HD:]
    gk_ref[HALF:] = (dk_ref[...] + back_ref[:, :HD].astype(F32)).astype(BF16)
    gv_ref[HALF:] = (dv_ref[...] + back_ref[:, HD:].astype(F32)).astype(BF16)


def weights_kernel(
    all_ref, x_ref, lent_ref, dq_ref, gv_ref,
    keep_ref, give_ref, low_q_ref, both_ref, lent_rank_ref, down_ref, upq_ref, upv_ref,
):
    first, last = first_last()

    @pl.when(first)
    def _():
        total = all_ref[0].astype(F32)
        for peer in range(1, all_ref.shape[0]):
            total = total + all_ref[peer].astype(F32)
        total = total.astype(BF16)
        rows = [total[n * RANK : (n + 1) * RANK] for n in range(3)]
        low_q_ref[...] = rows[0][:, :ROWS]
        both_ref[:RANK, :HALF] = rows[1][:, ROWS:]
        both_ref[:RANK, HALF:] = rows[2][:, :HALF]
        both_ref[RANK:] = rows[2][:, HALF:]
        lent_rank_ref[:RANK] = jnp.zeros((RANK, HALF), BF16)
        lent_rank_ref[RANK:] = rows[0][:, ROWS:]
        upv_ref[...] = jnp.dot(rows[1][:, :ROWS], gv_ref[...], preferred_element_type=F32)
        down_ref[...] = jnp.zeros_like(down_ref)
        upq_ref[...] = jnp.zeros_like(upq_ref)

    step = pl.program_id(0)
    now = pl.ds(pl.multiple_of(step * BLOCK, BLOCK), BLOCK)
    lent_now = pl.ds(pl.multiple_of(step * (BLOCK // 2), BLOCK // 2), BLOCK // 2)
    down_ref[...] += jnp.dot(both_ref[:, now], x_ref[...], preferred_element_type=F32) + jnp.dot(
        lent_rank_ref[:, lent_now], lent_ref[...], preferred_element_type=F32
    )
    upq_ref[...] += jnp.dot(low_q_ref[:, now], dq_ref[...], preferred_element_type=F32)

    @pl.when(last)
    def _():
        even = lax.rem(lax.axis_index("seq"), 2) == 0
        for ref, left in ((keep_ref, even), (give_ref, jnp.logical_not(even))):
            pick = lambda a, b: 2.0 * jnp.where(left, a, b)
            ref[: 2 * RANK] = pick(down_ref[:, :HALF], down_ref[:, HALF:])
            ref[2 * RANK : 3 * RANK] = pick(upq_ref[:, :HALF], upq_ref[:, HALF:])
            ref[3 * RANK :, :HD] = pick(upv_ref[:8], upv_ref[8:])
            ref[3 * RANK :, HD:] = jnp.zeros((8, HALF - HD), F32)


def place_kernel(mine_ref, other_ref, qd_ref, qu_ref, vd_ref, vu_ref):
    even = lax.rem(lax.axis_index("seq"), 2) == 0
    left = jnp.where(even, mine_ref[...], other_ref[...])
    right = jnp.where(even, other_ref[...], mine_ref[...])
    for ref, at in ((qd_ref, 0), (vd_ref, RANK), (qu_ref, 2 * RANK)):
        ref[:, :HALF] = left[at : at + RANK]
        ref[:, HALF:] = right[at : at + RANK]
    vu_ref[:8] = left[3 * RANK :, :HD]
    vu_ref[8:] = right[3 * RANK :, :HD]


def whole(*shape):
    return pl.BlockSpec(shape, lambda h: (0,) * len(shape))


def struct(*shape, dtype=F32):
    return jax.ShapeDtypeStruct(shape, dtype)


def on_device(query, key, value, cotangent, x, q_down, q_up, v_down, v_up):
    seq, tensor = lax.axis_size("seq"), lax.axis_size("tensor")
    untouched = pl.BlockSpec(memory_space=pl.ANY)
    bottom = pl.BlockSpec((HALF, HD), lambda h: (1, 0))

    kv = pl.pallas_call(
        pack_kernel,
        grid=(1,),
        in_specs=[bottom, bottom],
        out_specs=whole(HALF, 2 * HD),
        out_shape=struct(HALF, 2 * HD, dtype=BF16),
        compiler_params=LARGE,
        name="pack",
    )(key, value)
    kv = lax.ppermute(kv, "seq", [(s, (s + 1) % seq) for s in range(seq)])

    pair = lambda h: (0, h)
    dq, dk, dv, bq, low, lent = pl.pallas_call(
        plain_kernel,
        grid=(2,),
        in_specs=[pl.BlockSpec((ROWS, 2 * HD), pair)] * 2
        + [whole(ROWS, HD)] * 2
        + [pl.BlockSpec((RANK, 2 * HD), pair), pl.BlockSpec((HALF, WIDTH), lambda h: (h, 0))]
        + [whole(RANK, WIDTH)] * 2,
        out_specs=[pl.BlockSpec((ROWS, 2 * HD), pair), whole(ROWS, HD), whole(ROWS, HD), whole(RANK, ROWS)]
        + [pl.BlockSpec((2 * RANK, HALF), pair), whole(HALF, WIDTH)],
        out_shape=[
            struct(ROWS, WIDTH, dtype=BF16),
            struct(ROWS, HD),
            struct(ROWS, HD),
            struct(RANK, ROWS),
            struct(2 * RANK, ROWS, dtype=BF16),
            struct(HALF, WIDTH, dtype=BF16),
        ],
        scratch_shapes=[
            pltpu.VMEM((ROWS, 2 * HD), BF16),
            pltpu.VMEM((HD, ROWS), BF16),
            pltpu.VMEM((2 * HD, ROWS), BF16),
        ],
        compiler_params=LARGE,
        name="plain",
    )(query, cotangent, key, value, q_up, x, q_down, v_down)
    lent = lax.ppermute(lent, "seq", [(s, (s + 1) % seq) for s in range(seq)])

    rolled = lambda h: (0, 2 + h)
    keys = ROWS + HALF
    dq, back, top, dk, dv, share = pl.pallas_call(
        rolled_kernel,
        grid=(2,),
        in_specs=[pl.BlockSpec((ROWS, 2 * HD), rolled)] * 2
        + [whole(ROWS, HD)] * 2
        + [whole(HALF, 2 * HD), pl.BlockSpec((RANK, 2 * HD), rolled), untouched]
        + [whole(ROWS, HD), whole(ROWS, HD), whole(RANK, ROWS), whole(2 * RANK, ROWS), whole(RANK, HD)],
        out_specs=[pl.BlockSpec((ROWS, 2 * HD), rolled), whole(HALF, 2 * HD), whole(HALF, 2 * HD)]
        + [whole(HALF, HD), whole(HALF, HD), whole(tensor, 3 * RANK, keys)],
        out_shape=[
            struct(ROWS, WIDTH, dtype=BF16),
            struct(HALF, 2 * HD, dtype=BF16),
            struct(HALF, 2 * HD, dtype=BF16),
            struct(HALF, HD),
            struct(HALF, HD),
            struct(tensor, 3 * RANK, keys, dtype=BF16),
        ],
        scratch_shapes=[
            pltpu.VMEM((keys, 2 * HD), BF16),
            pltpu.VMEM((keys, HD), BF16),
            pltpu.VMEM((HD, keys), BF16),
            pltpu.VMEM((keys, HD), F32),
            pltpu.VMEM((keys, HD), F32),
            pltpu.VMEM((RANK, ROWS), F32),
            pltpu.VMEM((2 * HD, ROWS), BF16),
        ],
        input_output_aliases={6: 0},
        compiler_params=LARGE,
        name="rolled",
    )(query, cotangent, key, value, kv, q_up, dq, dk, dv, bq, low, v_up)
    back = lax.ppermute(back, "seq", [(s, (s - 1) % seq) for s in range(seq)])
    gathered = lax.all_to_all(share, "tensor", 0, 0)
    grad_key, grad_value = pl.pallas_call(
        finish_kernel,
        out_shape=[struct(ROWS, HD, dtype=BF16)] * 2,
        compiler_params=LARGE,
        name="finish",
    )(top, dk, dv, back)

    down = lambda h: (h, 0)
    part_rows = 3 * RANK + 8
    keep, give = pl.pallas_call(
        weights_kernel,
        grid=(ROWS // BLOCK,),
        in_specs=[
            whole(tensor, 3 * RANK, keys),
            pl.BlockSpec((BLOCK, WIDTH), down),
            pl.BlockSpec((BLOCK // 2, WIDTH), down),
            pl.BlockSpec((BLOCK, WIDTH), down),
            whole(ROWS, HD),
        ],
        out_specs=[whole(part_rows, HALF)] * 2,
        out_shape=[struct(part_rows, HALF)] * 2,
        scratch_shapes=[
            pltpu.VMEM((RANK, ROWS), BF16),
            pltpu.VMEM((2 * RANK, ROWS), BF16),
            pltpu.VMEM((2 * RANK, HALF), BF16),
            pltpu.VMEM((2 * RANK, WIDTH), F32),
            pltpu.VMEM((RANK, WIDTH), F32),
            pltpu.VMEM((RANK, HD), F32),
        ],
        compiler_params=LARGE,
        name="weights",
    )(gathered, x, lent, dq, grad_value)

    swap = [(s, s ^ 1) for s in range(seq)]
    part = (keep + lax.ppermute(give, "seq", swap)).astype(BF16)
    chips = seq // 2
    parts = lax.all_to_all(
        jnp.broadcast_to(part[None], (chips,) + part.shape),
        "seq",
        0,
        0,
        axis_index_groups=[[2 * i + c for i in range(chips)] for c in range(2)],
    )
    total = jnp.sum(parts.astype(F32), axis=0)
    other = lax.ppermute(total, "seq", swap)
    q_down_grad, q_up_grad, v_down_grad, v_up_grad = pl.pallas_call(
        place_kernel,
        out_shape=[struct(RANK, WIDTH)] * 3 + [struct(RANK, HD)],
        compiler_params=SMALL,
        name="place",
    )(total, other)
    return dq, grad_key, grad_value, q_down_grad, q_up_grad, v_down_grad, v_up_grad


def solution(mesh):
    rows, copied = P("seq", "tensor"), P(None, "tensor")
    return jax.shard_map(
        on_device,
        mesh=mesh,
        in_specs=(rows,) * 5 + (copied,) * 4,
        out_specs=(rows,) * 3 + (copied,) * 4,
        check_vma=False,
    )
```

time: 83.2 us -> 85.3 us (1.025)
  blocking collectives: 34.3 us -> 17 us
  waiting for transfers between devices: 2.57 us -> 16.1 us
  starting transfers between devices: 9.4 us -> 12.3 us
  Pallas kernels: 32.9 us -> 35.4 us
  other arithmetic: 0.08 us -> 0.98 us
    all_to_all x1 -> x0, blocking collectives: 16.9 us -> none  [on_device(): gathered = lax.all_to_all(share, 'tensor', 0, 0)]
    all_to_all x0 -> x1, waiting for transfers between devices: none -> 8.41 us  [on_device(): gathered = lax.all_to_all(share, 'tensor', 0, 0)]
    all_to_all x0 -> x1, starting transfers between devices: none -> 5.52 us  [on_device(): gathered = lax.all_to_all(share, 'tensor', 0, 0)]
    ppermute x1, waiting for transfers between devices: 0.64 us -> 5.53 us  [on_device(): back = lax.ppermute(back, 'seq', [(s, (s - 1) % seq) for s in range(seq)])]
    ppermute x1, starting transfers between devices: 5.01 us -> 1.51 us  [on_device(): part = (keep + lax.ppermute(give, 'seq', swap)).astype(BF16)]
    pallas_call x4 -> x3, Pallas kernels: 18 us -> 20.2 us  [the longest x1 12.9 us: on_device(): pl.pallas_call(rolled_kernel, grid=(2,), in_specs=[pl.BlockSpec((ROWS, 2...]
    convert_element_type x1, other arithmetic: 0.02 us -> 0.92 us  [on_device(): part = (keep + lax.ppermute(give, 'seq', swap)).astype(BF16)]
  transfers between devices with their start and end apart: 4 -> 6, of which waited for: 3 -> 4; matrix products, arithmetic and copies ran while one was open for 0% -> 0% of each run, Pallas kernels for 21% -> 33%
where the time goes in v5:
time: 85.3 us; the launch traced here: 84.9 us
  Pallas kernels  35.4 us (42%)
  blocking collectives  17 us (20%)
  waiting for transfers between devices  16.1 us (19%)
  starting transfers between devices  12.3 us (14%)
  local copies, waits for them, and re-layouts  2.48 us (3%)
  other arithmetic  0.98 us (1%)
    all_to_all x1, blocking collectives, on_device(): lax.all_to_all(jnp.broadcast_to(part[None], (chips,) + part.shape), 'seq'...  17 us
    pallas_call x1, Pallas kernels, on_device(): pl.pallas_call(rolled_kernel, grid=(2,), in_specs=[pl.BlockSpec((ROWS, 2...  12.9 us
    pallas_call x1, Pallas kernels, on_device(): pl.pallas_call(plain_kernel, grid=(2,), in_specs=[pl.BlockSpec((ROWS, 2 *...  12.9 us
    all_to_all x1, waiting for transfers between devices, on_device(): gathered = lax.all_to_all(share, 'tensor', 0, 0)  8.41 us
    ppermute x1, waiting for transfers between devices, on_device(): back = lax.ppermute(back, 'seq', [(s, (s - 1) % seq) for s in range(seq)])  5.53 us
    all_to_all x1, starting transfers between devices, on_device(): gathered = lax.all_to_all(share, 'tensor', 0, 0)  5.52 us
    pallas_call x1, Pallas kernels, on_device(): pl.pallas_call(weights_kernel, grid=(ROWS // BLOCK,), in_specs=[whole(ten...  5.21 us
    ppermute x1, starting transfers between devices, on_device(): kv = lax.ppermute(kv, 'seq', [(s, (s + 1) % seq) for s in range(seq)])  2.69 us
  transfers between devices with their start and end apart: 6, of which 4 were waited for; matrix products, arithmetic and copies ran while one was open for 0% of the time, Pallas kernels for 33%

profile of v5, /device:TPU:1, one launch (start us, length us, event | category | flops | bytes accessed | tf_op | source)
XLA Modules:
  0.0 84.9 jit_solution(13379616405363313276)
XLA Ops:
  0.6 1.7 %pack.1 = bf16[512,256]{1,0:T(8,128)(2,1)} custom-call(bf16[1024,128]{1,0:T(8,128)(2,1)} %k_ref.5, bf16[1024,128]{1,0:T(8,128)(2,1)} %v_ref.5), custom_call_target="tpu_custom_call" | custom-call | tf_op jit(solution)/shard_map/pack/pallas_call | solution.py:239
  2.4 2.7 %collective-permute-start = (bf16[512,256]{1,0:T(8,128)(2,1)}, bf16[512,256]{1,0:T(8,128)(2,1)S(1)}, u32[]{:S(2)}, u32[]{:S(2)}) collective-permute-start(bf16[512,256]{1,0:T(8,128)(2,1)} %pack.1), channel_id=1, source_target_pairs={{0,8},{8,16},{16,24},{24,32},{32,40},{40,48},{48,56},{56,64},{64,7... | collective-permute-start | bytes 786440 | tf_op jit(solution)/shard_map/ppermute | solution.py:248
  5.0 12.9 %plain.1 = (bf16[1024,1024]{1,0:T(8,128)(2,1)}, f32[1024,128]{1,0:T(8,128)}, f32[1024,128]{1,0:T(8,128)}, f32[16,1024]{1,0:T(8,128)}, bf16[32,1024]{1,0:T(8,128)(2,1)}, /*index=5*/bf16[512,1024]{1,0:T(8,128)(2,1)}) custom-call(bf16[1024,1024]{1,0:T(8,128)(2,1)} %q_ref.3, bf16[1024,1024]{1,0:T(8,128)(2,1)} %do_ref.3, bf16[1024,128]{1,0:T(8,128)(2,1)} %k_ref.5, ...), custom_call_target="tpu_custom_call" | custom-call | tf_op jit(solution)/shard_map/plain/pallas_call | solution.py:251
  17.9 0.1 collective-permute-start.2
  18.0 0.0 collective-permute-done.kv_ref
  18.0 0.0 copy-start.2
  18.0 0.7 copy-done.2
  18.7 12.9 %rolled.1 = (bf16[1024,1024]{1,0:T(8,128)(2,1)}, bf16[512,256]{1,0:T(8,128)(2,1)}, bf16[512,256]{1,0:T(8,128)(2,1)}, f32[512,128]{1,0:T(8,128)}, f32[512,128]{1,0:T(8,128)}, /*index=5*/bf16[8,48,1536]{2,1,0:T(8,128)(2,1)}) custom-call(bf16[1024,1024]{1,0:T(8,128)(2,1)} %q_ref.3, bf16[1024,1024]{1,0:T(8,128)(2,1)} %do_ref.3, ...), custom_call_target="tpu_custom_call", output_to_operand_aliasing={{0}: (6, {})} | custom-call | tf_op jit(solution)/shard_map/rolled/pallas_call | solution.py:280
  31.6 0.0 copy-start.4
  31.6 5.5 %all-to-all-start = ((bf16[8,48,1536]{2,1,0:T(8,128)(2,1)}), bf16[8,48,1536]{2,1,0:T(8,128)(2,1)S(1)}, u32[]{:S(2)}, u32[]{:S(2)}) async-start(bf16[8,48,1536]{2,1,0:T(8,128)(2,1)} %get-tuple-element.39), calls=%async_computation | async-start | bytes 2359296 | tf_op jit(solution)/shard_map/all_to_all | solution.py:311
  37.1 0.0 copy-done.4
  37.1 0.8 collective-permute-start.1
  38.0 5.5 %collective-permute-done.1.back_ref = bf16[512,256]{1,0:T(8,128)(2,1)S(1)} collective-permute-done((bf16[512,256]{1,0:T(8,128)(2,1)S(1)}, bf16[512,256]{1,0:T(8,128)(2,1)S(1)}, u32[]{:S(2)}, u32[]{:S(2)}) %collective-permute-start.1) | collective-permute-done | bytes 262176 | tf_op jit(solution)/shard_map/ppermute | solution.py:310
  43.5 0.0 copy-start.3
  43.5 0.7 copy-done.3
  44.2 2.0 %finish.1 = (bf16[1024,128]{1,0:T(8,128)(2,1)}, bf16[1024,128]{1,0:T(8,128)(2,1)}) custom-call(bf16[512,256]{1,0:T(8,128)(2,1)} %get-tuple-element.33.top_ref, f32[512,128]{1,0:T(8,128)} %get-tuple-element.34.dk_ref, f32[512,128]{1,0:T(8,128)} %get-tuple-element.35.dv_ref, bf16[512,256]{1,0:T(8,128)(2,1)} %copy-done.3), custom_call_target="tpu_custom_call" | custom-call | tf_op jit(solution)/shard_map/finish/pallas_call | solution.py:312
  46.3 0.0 collective-permute-done.2.lent_ref
  46.3 0.0 copy-start.1
  46.3 8.4 %all-to-all-done.all_ref = bf16[8,48,1536]{2,1,0:T(8,128)(2,1)S(1)} async-done(((bf16[8,48,1536]{2,1,0:T(8,128)(2,1)}), bf16[8,48,1536]{2,1,0:T(8,128)(2,1)S(1)}, u32[]{:S(2)}, u32[]{:S(2)}) %all-to-all-start) | async-done | bytes 1179680 | tf_op jit(solution)/shard_map/all_to_all | solution.py:311
  54.7 0.0 copy-start
  54.7 0.0 copy-done.1
  54.7 1.0 %copy-done = bf16[8,48,1536]{2,1,0:T(8,128)(2,1)} copy-done((bf16[8,48,1536]{2,1,0:T(8,128)(2,1)}, bf16[8,48,1536]{2,1,0:T(8,128)(2,1)S(1)}, u32[]{:S(2)}) %copy-start) | copy-done | bytes 1179672
  55.7 5.2 %weights.1 = (f32[56,512]{1,0:T(8,128)}, f32[56,512]{1,0:T(8,128)}) custom-call(bf16[8,48,1536]{2,1,0:T(8,128)(2,1)} %copy-done, bf16[1024,1024]{1,0:T(8,128)(2,1)} %x_ref.3, bf16[512,1024]{1,0:T(8,128)(2,1)} %copy-done.1, bf16[1024,1024]{1,0:T(8,128)(2,1)} %get-tuple-element.20.dq_ref, bf16[1024,128]{1,0:T(8,128)(2,1)} %get-tuple-element.22.gv_ref), custom_call_target="tpu_custom_call" | custom-call | tf_op jit(solution)/shard_map/weights/pallas_call | solution.py:321
  60.9 1.5 %collective-permute-start.3 = (f32[56,512]{1,0:T(8,128)}, f32[56,512]{1,0:T(8,128)S(1)}, u32[]{:S(2)}, u32[]{:S(2)}) collective-permute-start(f32[56,512]{1,0:T(8,128)} %get-tuple-element.42), channel_id=1, source_target_pairs={{0,8},{8,0},{16,24},{24,16},{32,40},{40,32},{48,56},{56,48},{64,72... | collective-permute-start | bytes 344072 | tf_op jit(solution)/shard_map/ppermute | solution.py:346
  62.4 1.2 %collective-permute-done.3 = f32[56,512]{1,0:T(8,128)S(1)} collective-permute-done((f32[56,512]{1,0:T(8,128)}, f32[56,512]{1,0:T(8,128)S(1)}, u32[]{:S(2)}, u32[]{:S(2)}) %collective-permute-start.3) | collective-permute-done | bytes 114720 | tf_op jit(solution)/shard_map/ppermute | solution.py:346
  63.6 0.9 %add_convert_fusion = bf16[56,512]{1,0:T(8,128)(2,1)S(1)} fusion(f32[56,512]{1,0:T(8,128)} %get-tuple-element.41, f32[56,512]{1,0:T(8,128)S(1)} %collective-permute-done.3), kind=kLoop, calls=%fused_computation.1 | loop fusion | flops 57344 | bytes 286720 | tf_op jit(solution)/shard_map/convert_element_type | solution.py:346
  64.6 17.0 %all_to_all.10 = bf16[8,56,512]{2,1,0:T(8,128)(2,1)S(1)} all-to-all(bf16[8,56,512]{2,1,0:T(8,128)(2,1)S(1)} %broadcast_in_dim.2), channel_id=1, replica_groups={{0,16,32,48,64,80,96,112},{8,24,40,56,72,88,104,120},{1,17,33,49,65,81,..., dimensions={0} | all-to-all | bytes 917504 | tf_op jit(solution)/shard_map/all_to_all | solution.py:348
  81.6 0.1 convert_reduce_fusion.mine_ref
  81.6 1.6 %collective-permute-start.4 = (f32[56,512]{1,0:T(8,128)S(1)}, f32[56,512]{1,0:T(8,128)S(1)}, u32[]{:S(2)}, u32[]{:S(2)}) collective-permute-start(f32[56,512]{1,0:T(8,128)S(1)} %convert_reduce_fusion.mine_ref), channel_id=1, source_target_pairs={{0,8},{8,0},{16,24},{24,16},{32,40},{40,32},{48,56},{56,48},{64,72... | collective-permute-start | bytes 344072 | tf_op jit(solution)/shard_map/ppermute | solution.py:356
  83.3 1.0 %collective-permute-done.4.other_ref = f32[56,512]{1,0:T(8,128)S(1)} collective-permute-done((f32[56,512]{1,0:T(8,128)S(1)}, f32[56,512]{1,0:T(8,128)S(1)}, u32[]{:S(2)}, u32[]{:S(2)}) %collective-permute-start.4) | collective-permute-done | bytes 114720 | tf_op jit(solution)/shard_map/ppermute | solution.py:356
  84.2 0.7 place.1
  (1 shorter events, 0.0 us)
Async XLA Ops:
  2.4 15.6 %collective-permute-start = (bf16[512,256]{1,0:T(8,128)(2,1)}, bf16[512,256]{1,0:T(8,128)(2,1)S(1)}, u32[]{:S(2)}, u32[]{:S(2)}) collective-permute-start(bf16[512,256]{1,0:T(8,128)(2,1)} %pack.1), channel_id=1, source_target_pairs={{0,8},{8,16},{16,24},{24,32},{32,40},{40,48},{48,56},{56,64},{64,7... | collective-permute-start | bytes 786440 | tf_op jit(solution)/shard_map/ppermute | solution.py:248
  17.9 28.4 %collective-permute-start.2 = (bf16[512,1024]{1,0:T(8,128)(2,1)}, bf16[512,1024]{1,0:T(8,128)(2,1)S(1)}, u32[]{:S(2)}, u32[]{:S(2)}) collective-permute-start(bf16[512,1024]{1,0:T(8,128)(2,1)} %get-tuple-element.40), channel_id=1, source_target_pairs={{0,8},{8,16},{16,24},{24,32},{32,40},{40,48},{48,56},{56,64},{64,7... | collective-permute-start | bytes 3145736 | tf_op jit(solution)/shard_map/ppermute | solution.py:276
  18.0 0.7 copy-start.2
  31.6 5.5 %copy-start.4 = (bf16[512,256]{1,0:T(8,128)(2,1)S(1)}, bf16[512,256]{1,0:T(8,128)(2,1)}, u32[]{:S(2)}) copy-start(bf16[512,256]{1,0:T(8,128)(2,1)} %get-tuple-element.36) | copy-start | bytes 786436
  31.6 23.1 %all-to-all-start = ((bf16[8,48,1536]{2,1,0:T(8,128)(2,1)}), bf16[8,48,1536]{2,1,0:T(8,128)(2,1)S(1)}, u32[]{:S(2)}, u32[]{:S(2)}) async-start(bf16[8,48,1536]{2,1,0:T(8,128)(2,1)} %get-tuple-element.39), calls=%async_computation | async-start | bytes 2359296 | tf_op jit(solution)/shard_map/all_to_all | solution.py:311
  37.1 6.4 %collective-permute-start.1 = (bf16[512,256]{1,0:T(8,128)(2,1)S(1)}, bf16[512,256]{1,0:T(8,128)(2,1)S(1)}, u32[]{:S(2)}, u32[]{:S(2)}) collective-permute-start(bf16[512,256]{1,0:T(8,128)(2,1)S(1)} %copy-done.4), channel_id=1, source_target_pairs={{0,120},{8,0},{16,8},{24,16},{32,24},{40,32},{48,40},{56,48},{64,5... | collective-permute-start | bytes 786440 | tf_op jit(solution)/shard_map/ppermute | solution.py:310
  43.5 0.7 copy-start.3
  46.3 8.4 %copy-start.1 = (bf16[512,1024]{1,0:T(8,128)(2,1)}, bf16[512,1024]{1,0:T(8,128)(2,1)S(1)}, u32[]{:S(2)}) copy-start(bf16[512,1024]{1,0:T(8,128)(2,1)S(1)} %collective-permute-done.2.lent_ref) | copy-start | bytes 3145732
  54.7 1.0 %copy-start = (bf16[8,48,1536]{2,1,0:T(8,128)(2,1)}, bf16[8,48,1536]{2,1,0:T(8,128)(2,1)S(1)}, u32[]{:S(2)}) copy-start(bf16[8,48,1536]{2,1,0:T(8,128)(2,1)S(1)} %all-to-all-done.all_ref) | copy-start | bytes 3538948
  60.9 2.7 %collective-permute-start.3 = (f32[56,512]{1,0:T(8,128)}, f32[56,512]{1,0:T(8,128)S(1)}, u32[]{:S(2)}, u32[]{:S(2)}) collective-permute-start(f32[56,512]{1,0:T(8,128)} %get-tuple-element.42), channel_id=1, source_target_pairs={{0,8},{8,0},{16,24},{24,16},{32,40},{40,32},{48,56},{56,48},{64,72... | collective-permute-start | bytes 344072 | tf_op jit(solution)/shard_map/ppermute | solution.py:346
  81.6 2.6 %collective-permute-start.4 = (f32[56,512]{1,0:T(8,128)S(1)}, f32[56,512]{1,0:T(8,128)S(1)}, u32[]{:S(2)}, u32[]{:S(2)}) collective-permute-start(f32[56,512]{1,0:T(8,128)S(1)} %convert_reduce_fusion.mine_ref), channel_id=1, source_target_pairs={{0,8},{8,0},{16,24},{24,16},{32,40},{40,32},{48,56},{56,48},{64,72... | collective-permute-start | bytes 344072 | tf_op jit(solution)/shard_map/ppermute | solution.py:356

commit v6 on v5

--- a/solution.py
+++ b/solution.py
@@ -171,45 +171,34 @@
 
 
 def weights_kernel(
-    all_ref, x_ref, lent_ref, dq_ref, gv_ref,
-    keep_ref, give_ref, low_q_ref, both_ref, lent_rank_ref, down_ref, upq_ref, upv_ref,
+    all_ref, x_ref, lent_hbm, dq_hbm, gv_hbm, keep_ref, give_ref, _, __, lent_ref, dq_ref, gv_ref, sems
 ):
-    first, last = first_last()
-
-    @pl.when(first)
-    def _():
-        total = all_ref[0].astype(F32)
-        for peer in range(1, all_ref.shape[0]):
-            total = total + all_ref[peer].astype(F32)
-        total = total.astype(BF16)
-        rows = [total[n * RANK : (n + 1) * RANK] for n in range(3)]
-        low_q_ref[...] = rows[0][:, :ROWS]
-        both_ref[:RANK, :HALF] = rows[1][:, ROWS:]
-        both_ref[:RANK, HALF:] = rows[2][:, :HALF]
-        both_ref[RANK:] = rows[2][:, HALF:]
-        lent_rank_ref[:RANK] = jnp.zeros((RANK, HALF), BF16)
-        lent_rank_ref[RANK:] = rows[0][:, ROWS:]
-        upv_ref[...] = jnp.dot(rows[1][:, :ROWS], gv_ref[...], preferred_element_type=F32)
-        down_ref[...] = jnp.zeros_like(down_ref)
-        upq_ref[...] = jnp.zeros_like(upq_ref)
-
-    step = pl.program_id(0)
-    now = pl.ds(pl.multiple_of(step * BLOCK, BLOCK), BLOCK)
-    lent_now = pl.ds(pl.multiple_of(step * (BLOCK // 2), BLOCK // 2), BLOCK // 2)
-    down_ref[...] += jnp.dot(both_ref[:, now], x_ref[...], preferred_element_type=F32) + jnp.dot(
-        lent_rank_ref[:, lent_now], lent_ref[...], preferred_element_type=F32
-    )
-    upq_ref[...] += jnp.dot(low_q_ref[:, now], dq_ref[...], preferred_element_type=F32)
-
-    @pl.when(last)
-    def _():
-        even = lax.rem(lax.axis_index("seq"), 2) == 0
-        for ref, left in ((keep_ref, even), (give_ref, jnp.logical_not(even))):
-            pick = lambda a, b: 2.0 * jnp.where(left, a, b)
-            ref[: 2 * RANK] = pick(down_ref[:, :HALF], down_ref[:, HALF:])
-            ref[2 * RANK : 3 * RANK] = pick(upq_ref[:, :HALF], upq_ref[:, HALF:])
-            ref[3 * RANK :, :HD] = pick(upv_ref[:8], upv_ref[8:])
-            ref[3 * RANK :, HD:] = jnp.zeros((8, HALF - HD), F32)
+    copies = []
+    for n, (source, target) in enumerate(((lent_hbm, lent_ref), (gv_hbm, gv_ref), (dq_hbm, dq_ref))):
+        copies.append(pltpu.make_async_copy(source, target, sems.at[n]))
+        copies[n].start()
+    total = all_ref[0].astype(F32)
+    for peer in range(1, all_ref.shape[0]):
+        total = total + all_ref[peer].astype(F32)
+    total = (2.0 * total).astype(BF16)
+    rows = [total[n * RANK : (n + 1) * RANK] for n in range(3)]
+    bq = jnp.concatenate([rows[1][:, ROWS:], rows[2][:, :HALF]], 1)
+    both = jnp.concatenate([bq, rows[2][:, HALF:]], 0)
+    down = jnp.dot(both, x_ref[...], preferred_element_type=F32)
+    copies[0].wait()
+    lent = jnp.dot(rows[0][:, ROWS:], lent_ref[...], preferred_element_type=F32)
+    copies[1].wait()
+    up_v = jnp.dot(rows[1][:, :ROWS], gv_ref[...], preferred_element_type=F32)
+    copies[2].wait()
+    up_q = jnp.dot(rows[0][:, :ROWS], dq_ref[...], preferred_element_type=F32)
+    down_q, down_v = down[:RANK], down[RANK:] + lent
+
+    even = lax.rem(lax.axis_index("seq"), 2) == 0
+    for ref, left in ((keep_ref, even), (give_ref, jnp.logical_not(even))):
+        for n, wide in enumerate((down_q, down_v, up_q)):
+            ref[n * RANK : (n + 1) * RANK] = jnp.where(left, wide[:, :HALF], wide[:, HALF:])
+        ref[3 * RANK :, :HD] = jnp.where(left, up_v[:8], up_v[8:])
+        ref[3 * RANK :, HD:] = jnp.zeros((8, HALF - HD), F32)
 
 
 def place_kernel(mine_ref, other_ref, qd_ref, qu_ref, vd_ref, vu_ref):
@@ -312,33 +301,26 @@
     grad_key, grad_value = pl.pallas_call(
         finish_kernel,
         out_shape=[struct(ROWS, HD, dtype=BF16)] * 2,
-        compiler_params=LARGE,
+        compiler_params=SMALL,
         name="finish",
     )(top, dk, dv, back)
 
-    down = lambda h: (h, 0)
     part_rows = 3 * RANK + 8
-    keep, give = pl.pallas_call(
+    inside = pl.BlockSpec(memory_space=pltpu.VMEM)
+    keep, give, dq, grad_value = pl.pallas_call(
         weights_kernel,
-        grid=(ROWS // BLOCK,),
-        in_specs=[
-            whole(tensor, 3 * RANK, keys),
-            pl.BlockSpec((BLOCK, WIDTH), down),
-            pl.BlockSpec((BLOCK // 2, WIDTH), down),
-            pl.BlockSpec((BLOCK, WIDTH), down),
-            whole(ROWS, HD),
-        ],
-        out_specs=[whole(part_rows, HALF)] * 2,
-        out_shape=[struct(part_rows, HALF)] * 2,
+        in_specs=[inside] * 2 + [untouched] * 3,
+        out_specs=[inside] * 2 + [untouched] * 2,
+        out_shape=[struct(part_rows, HALF)] * 2
+        + [struct(ROWS, WIDTH, dtype=BF16), struct(ROWS, HD, dtype=BF16)],
+        input_output_aliases={3: 2, 4: 3},
         scratch_shapes=[
-            pltpu.VMEM((RANK, ROWS), BF16),
-            pltpu.VMEM((2 * RANK, ROWS), BF16),
-            pltpu.VMEM((2 * RANK, HALF), BF16),
-            pltpu.VMEM((2 * RANK, WIDTH), F32),
-            pltpu.VMEM((RANK, WIDTH), F32),
-            pltpu.VMEM((RANK, HD), F32),
-        ],
-        compiler_params=LARGE,
+            pltpu.VMEM((HALF, WIDTH), BF16),
+            pltpu.VMEM((ROWS, WIDTH), BF16),
+            pltpu.VMEM((ROWS, HD), BF16),
+            pltpu.SemaphoreType.DMA((3,)),
+        ],
+        compiler_params=SMALL,
         name="weights",
     )(gathered, x, lent, dq, grad_value)
 

time: 85.3 us -> 80.8 us (0.947)
  Pallas kernels: 35.4 us -> 31.9 us
  other arithmetic: 0.98 us -> 0.08 us
    pallas_call x1, Pallas kernels: 5.21 us -> 2.83 us  [on_device(): pl.pallas_call(weights_kernel, in_specs=[inside] * 2 + [untouched] * 3, o...]
    pallas_call x1, Pallas kernels: 2.04 us -> 0.87 us  [on_device(): pl.pallas_call(finish_kernel, out_shape=[struct(ROWS, HD, dtype=BF16)] *...]
    convert_element_type x1, other arithmetic: 0.92 us -> 0.02 us  [on_device(): part = (keep + lax.ppermute(give, 'seq', swap)).astype(BF16)]
where the time goes in v6:
time: 80.8 us; the launch traced here: 80.5 us
  Pallas kernels  31.9 us (39%)
  blocking collectives  17 us (21%)
  waiting for transfers between devices  15.9 us (20%)
  starting transfers between devices  12.3 us (15%)
  local copies, waits for them, and re-layouts  2.64 us (3%)
    all_to_all x1, blocking collectives, on_device(): lax.all_to_all(jnp.broadcast_to(part[None], (chips,) + part.shape), 'seq'...  17 us
    pallas_call x1, Pallas kernels, on_device(): pl.pallas_call(rolled_kernel, grid=(2,), in_specs=[pl.BlockSpec((ROWS, 2...  12.9 us
    pallas_call x1, Pallas kernels, on_device(): pl.pallas_call(plain_kernel, grid=(2,), in_specs=[pl.BlockSpec((ROWS, 2 *...  12.9 us
    all_to_all x1, waiting for transfers between devices, on_device(): gathered = lax.all_to_all(share, 'tensor', 0, 0)  8.27 us
    ppermute x1, waiting for transfers between devices, on_device(): back = lax.ppermute(back, 'seq', [(s, (s - 1) % seq) for s in range(seq)])  5.73 us
    all_to_all x1, starting transfers between devices, on_device(): gathered = lax.all_to_all(share, 'tensor', 0, 0)  5.52 us
    pallas_call x1, Pallas kernels, on_device(): pl.pallas_call(weights_kernel, in_specs=[inside] * 2 + [untouched] * 3, o...  2.83 us
    ppermute x1, starting transfers between devices, on_device(): kv = lax.ppermute(kv, 'seq', [(s, (s + 1) % seq) for s in range(seq)])  2.69 us
  transfers between devices with their start and end apart: 6, of which 4 were waited for; matrix products, arithmetic and copies ran while one was open for 0% of the time, Pallas kernels for 33%

profile of v6, /device:TPU:1, one launch (start us, length us, event | category | flops | bytes accessed | tf_op | source)
XLA Modules:
  0.0 80.5 jit_solution(9023028368139786119)
XLA Ops:
  0.6 1.7 %pack.1 = bf16[512,256]{1,0:T(8,128)(2,1)} custom-call(bf16[1024,128]{1,0:T(8,128)(2,1)} %k_ref.5, bf16[1024,128]{1,0:T(8,128)(2,1)} %v_ref.5), custom_call_target="tpu_custom_call" | custom-call | tf_op jit(solution)/shard_map/pack/pallas_call | solution.py:228
  2.4 2.7 %collective-permute-start = (bf16[512,256]{1,0:T(8,128)(2,1)}, bf16[512,256]{1,0:T(8,128)(2,1)S(1)}, u32[]{:S(2)}, u32[]{:S(2)}) collective-permute-start(bf16[512,256]{1,0:T(8,128)(2,1)} %pack.1), channel_id=1, source_target_pairs={{0,8},{8,16},{16,24},{24,32},{32,40},{40,48},{48,56},{56,64},{64,7... | collective-permute-start | bytes 786440 | tf_op jit(solution)/shard_map/ppermute | solution.py:237
  5.0 12.9 %plain.1 = (bf16[1024,1024]{1,0:T(8,128)(2,1)}, f32[1024,128]{1,0:T(8,128)}, f32[1024,128]{1,0:T(8,128)}, f32[16,1024]{1,0:T(8,128)}, bf16[32,1024]{1,0:T(8,128)(2,1)}, /*index=5*/bf16[512,1024]{1,0:T(8,128)(2,1)}) custom-call(bf16[1024,1024]{1,0:T(8,128)(2,1)} %q_ref.3, bf16[1024,1024]{1,0:T(8,128)(2,1)} %do_ref.3, bf16[1024,128]{1,0:T(8,128)(2,1)} %k_ref.5, ...), custom_call_target="tpu_custom_call" | custom-call | tf_op jit(solution)/shard_map/plain/pallas_call | solution.py:240
  17.9 0.1 collective-permute-start.1
  18.0 0.0 collective-permute-done.kv_ref
  18.0 0.0 copy-start.4
  18.0 0.7 copy-done.4
  18.7 12.9 %rolled.1 = (bf16[1024,1024]{1,0:T(8,128)(2,1)}, bf16[512,256]{1,0:T(8,128)(2,1)}, bf16[512,256]{1,0:T(8,128)(2,1)}, f32[512,128]{1,0:T(8,128)}, f32[512,128]{1,0:T(8,128)}, /*index=5*/bf16[8,48,1536]{2,1,0:T(8,128)(2,1)}) custom-call(bf16[1024,1024]{1,0:T(8,128)(2,1)} %q_ref.3, bf16[1024,1024]{1,0:T(8,128)(2,1)} %do_ref.3, ...), custom_call_target="tpu_custom_call", output_to_operand_aliasing={{0}: (6, {})} | custom-call | tf_op jit(solution)/shard_map/rolled/pallas_call | solution.py:269
  31.6 0.0 copy-start.1
  31.6 0.0 copy-start
  31.6 5.5 %all-to-all-start = ((bf16[8,48,1536]{2,1,0:T(8,128)(2,1)}), bf16[8,48,1536]{2,1,0:T(8,128)(2,1)S(1)}, u32[]{:S(2)}, u32[]{:S(2)}) async-start(bf16[8,48,1536]{2,1,0:T(8,128)(2,1)} %get-tuple-element.34), calls=%async_computation | async-start | bytes 2359296 | tf_op jit(solution)/shard_map/all_to_all | solution.py:300
  37.1 0.8 collective-permute-start.2
  37.9 5.7 %collective-permute-done.2.back_ref = bf16[512,256]{1,0:T(8,128)(2,1)S(1)} collective-permute-done((bf16[512,256]{1,0:T(8,128)(2,1)}, bf16[512,256]{1,0:T(8,128)(2,1)S(1)}, u32[]{:S(2)}, u32[]{:S(2)}) %collective-permute-start.2) | collective-permute-done | bytes 262176 | tf_op jit(solution)/shard_map/ppermute | solution.py:299
  43.6 0.0 copy-done.1
  43.6 0.0 copy-start.2
  43.7 0.9 %copy-done.2 = f32[512,128]{1,0:T(8,128)S(1)} copy-done((f32[512,128]{1,0:T(8,128)S(1)}, f32[512,128]{1,0:T(8,128)}, u32[]{:S(2)}) %copy-start.2) | copy-done | bytes 262168
  44.6 0.0 copy-start.3
  44.6 0.9 %copy-done.3 = f32[512,128]{1,0:T(8,128)S(1)} copy-done((f32[512,128]{1,0:T(8,128)S(1)}, f32[512,128]{1,0:T(8,128)}, u32[]{:S(2)}) %copy-start.3) | copy-done | bytes 262168
  45.6 0.9 %finish.1 = (bf16[1024,128]{1,0:T(8,128)(2,1)}, bf16[1024,128]{1,0:T(8,128)(2,1)}) custom-call(bf16[512,256]{1,0:T(8,128)(2,1)S(1)} %copy-done.1, f32[512,128]{1,0:T(8,128)S(1)} %copy-done.2, f32[512,128]{1,0:T(8,128)S(1)} %copy-done.3, bf16[512,256]{1,0:T(8,128)(2,1)S(1)} %collective-permute-done.2.back_ref), custom_call_target="tpu_custom_call" | custom-call | tf_op jit(solution)/shard_map/finish/pallas_call | solution.py:301
  46.4 0.0 collective-permute-done.1.lent_hbm
  46.4 8.3 %all-to-all-done.all_ref = bf16[8,48,1536]{2,1,0:T(8,128)(2,1)S(1)} async-done(((bf16[8,48,1536]{2,1,0:T(8,128)(2,1)}), bf16[8,48,1536]{2,1,0:T(8,128)(2,1)S(1)}, u32[]{:S(2)}, u32[]{:S(2)}) %all-to-all-start) | async-done | bytes 1179680 | tf_op jit(solution)/shard_map/all_to_all | solution.py:300
  54.7 0.0 copy-done
  54.7 2.8 %weights.1 = (f32[56,512]{1,0:T(8,128)S(1)}, f32[56,512]{1,0:T(8,128)S(1)}, bf16[1024,1024]{1,0:T(8,128)(2,1)}, bf16[1024,128]{1,0:T(8,128)(2,1)}) custom-call(bf16[8,48,1536]{2,1,0:T(8,128)(2,1)S(1)} %all-to-all-done.all_ref, bf16[1024,1024]{1,0:T(8,128)(2,1)S(1)} %copy-done, ...), custom_call_target="tpu_custom_call", output_to_operand_aliasing={{2}: (3, {}), {3}: (4, {})} | custom-call | tf_op jit(solution)/shard_map/weights/pallas_call | solution.py:310
  57.5 1.6 %collective-permute-start.3 = (f32[56,512]{1,0:T(8,128)S(1)}, f32[56,512]{1,0:T(8,128)S(1)}, u32[]{:S(2)}, u32[]{:S(2)}) collective-permute-start(f32[56,512]{1,0:T(8,128)S(1)} %get-tuple-element.46), channel_id=1, source_target_pairs={{0,8},{8,0},{16,24},{24,16},{32,40},{40,32},{48,56},{56,48},{64,72... | collective-permute-start | bytes 344072 | tf_op jit(solution)/shard_map/ppermute | solution.py:328
  59.1 1.0 %collective-permute-done.3 = f32[56,512]{1,0:T(8,128)S(1)} collective-permute-done((f32[56,512]{1,0:T(8,128)S(1)}, f32[56,512]{1,0:T(8,128)S(1)}, u32[]{:S(2)}, u32[]{:S(2)}) %collective-permute-start.3) | collective-permute-done | bytes 114720 | tf_op jit(solution)/shard_map/ppermute | solution.py:328
  60.2 17.0 %all_to_all.10 = bf16[8,56,512]{2,1,0:T(8,128)(2,1)S(1)} all-to-all(bf16[8,56,512]{2,1,0:T(8,128)(2,1)S(1)} %broadcast_in_dim.2), channel_id=1, replica_groups={{0,16,32,48,64,80,96,112},{8,24,40,56,72,88,104,120},{1,17,33,49,65,81,..., dimensions={0} | all-to-all | bytes 917504 | tf_op jit(solution)/shard_map/all_to_all | solution.py:330
  77.1 0.1 convert_reduce_fusion.mine_ref
  77.2 1.6 %collective-permute-start.4 = (f32[56,512]{1,0:T(8,128)S(1)}, f32[56,512]{1,0:T(8,128)S(1)}, u32[]{:S(2)}, u32[]{:S(2)}) collective-permute-start(f32[56,512]{1,0:T(8,128)S(1)} %convert_reduce_fusion.mine_ref), channel_id=1, source_target_pairs={{0,8},{8,0},{16,24},{24,16},{32,40},{40,32},{48,56},{56,48},{64,72... | collective-permute-start | bytes 344072 | tf_op jit(solution)/shard_map/ppermute | solution.py:338
  78.8 1.0 %collective-permute-done.4.other_ref = f32[56,512]{1,0:T(8,128)S(1)} collective-permute-done((f32[56,512]{1,0:T(8,128)S(1)}, f32[56,512]{1,0:T(8,128)S(1)}, u32[]{:S(2)}, u32[]{:S(2)}) %collective-permute-start.4) | collective-permute-done | bytes 114720 | tf_op jit(solution)/shard_map/ppermute | solution.py:338
  79.8 0.7 place.1
  (2 shorter events, 0.0 us)
Async XLA Ops:
  2.4 15.6 %collective-permute-start = (bf16[512,256]{1,0:T(8,128)(2,1)}, bf16[512,256]{1,0:T(8,128)(2,1)S(1)}, u32[]{:S(2)}, u32[]{:S(2)}) collective-permute-start(bf16[512,256]{1,0:T(8,128)(2,1)} %pack.1), channel_id=1, source_target_pairs={{0,8},{8,16},{16,24},{24,32},{32,40},{40,48},{48,56},{56,64},{64,7... | collective-permute-start | bytes 786440 | tf_op jit(solution)/shard_map/ppermute | solution.py:237
  17.9 28.5 %collective-permute-start.1 = (bf16[512,1024]{1,0:T(8,128)(2,1)}, bf16[512,1024]{1,0:T(8,128)(2,1)}, u32[]{:S(2)}, u32[]{:S(2)}) collective-permute-start(bf16[512,1024]{1,0:T(8,128)(2,1)} %get-tuple-element.35), channel_id=1, source_target_pairs={{0,8},{8,16},{16,24},{24,32},{32,40},{40,48},{48,56},{56,64},{64,7... | collective-permute-start | bytes 3145736 | tf_op jit(solution)/shard_map/ppermute | solution.py:265
  18.0 0.7 copy-start.4
  31.6 12.0 %copy-start.1 = (bf16[512,256]{1,0:T(8,128)(2,1)S(1)}, bf16[512,256]{1,0:T(8,128)(2,1)}, u32[]{:S(2)}) copy-start(bf16[512,256]{1,0:T(8,128)(2,1)} %get-tuple-element.37.top_ref) | copy-start | bytes 786436
  31.6 23.1 %copy-start = (bf16[1024,1024]{1,0:T(8,128)(2,1)S(1)}, bf16[1024,1024]{1,0:T(8,128)(2,1)}, u32[]{:S(2)}) copy-start(bf16[1024,1024]{1,0:T(8,128)(2,1)} %x_ref.3) | copy-start | bytes 6291460
  31.6 23.1 %all-to-all-start = ((bf16[8,48,1536]{2,1,0:T(8,128)(2,1)}), bf16[8,48,1536]{2,1,0:T(8,128)(2,1)S(1)}, u32[]{:S(2)}, u32[]{:S(2)}) async-start(bf16[8,48,1536]{2,1,0:T(8,128)(2,1)} %get-tuple-element.34), calls=%async_computation | async-start | bytes 2359296 | tf_op jit(solution)/shard_map/all_to_all | solution.py:300
  37.1 6.5 %collective-permute-start.2 = (bf16[512,256]{1,0:T(8,128)(2,1)}, bf16[512,256]{1,0:T(8,128)(2,1)S(1)}, u32[]{:S(2)}, u32[]{:S(2)}) collective-permute-start(bf16[512,256]{1,0:T(8,128)(2,1)} %get-tuple-element.40), channel_id=1, source_target_pairs={{0,120},{8,0},{16,8},{24,16},{32,24},{40,32},{48,40},{56,48},{64,5... | collective-permute-start | bytes 786440 | tf_op jit(solution)/shard_map/ppermute | solution.py:299
  43.6 1.0 %copy-start.2 = (f32[512,128]{1,0:T(8,128)S(1)}, f32[512,128]{1,0:T(8,128)}, u32[]{:S(2)}) copy-start(f32[512,128]{1,0:T(8,128)} %get-tuple-element.38.dk_ref) | copy-start | bytes 786436
  44.6 0.9 %copy-start.3 = (f32[512,128]{1,0:T(8,128)S(1)}, f32[512,128]{1,0:T(8,128)}, u32[]{:S(2)}) copy-start(f32[512,128]{1,0:T(8,128)} %get-tuple-element.39.dv_ref) | copy-start | bytes 786436
  57.5 2.6 %collective-permute-start.3 = (f32[56,512]{1,0:T(8,128)S(1)}, f32[56,512]{1,0:T(8,128)S(1)}, u32[]{:S(2)}, u32[]{:S(2)}) collective-permute-start(f32[56,512]{1,0:T(8,128)S(1)} %get-tuple-element.46), channel_id=1, source_target_pairs={{0,8},{8,0},{16,24},{24,16},{32,40},{40,32},{48,56},{56,48},{64,72... | collective-permute-start | bytes 344072 | tf_op jit(solution)/shard_map/ppermute | solution.py:328
  77.2 2.6 %collective-permute-start.4 = (f32[56,512]{1,0:T(8,128)S(1)}, f32[56,512]{1,0:T(8,128)S(1)}, u32[]{:S(2)}, u32[]{:S(2)}) collective-permute-start(f32[56,512]{1,0:T(8,128)S(1)} %convert_reduce_fusion.mine_ref), channel_id=1, source_target_pairs={{0,8},{8,0},{16,24},{24,16},{32,40},{40,32},{48,56},{56,48},{64,72... | collective-permute-start | bytes 344072 | tf_op jit(solution)/shard_map/ppermute | solution.py:338

commit v7 on v6

--- a/solution.py
+++ b/solution.py
@@ -76,13 +76,17 @@
 
 
 def plain_kernel(
-    q_ref, do_ref, k_ref, v_ref, up_ref, x_ref, qd_ref, vd_ref,
-    dq_ref, dk_ref, dv_ref, bq_ref, low_ref, lent_ref, twice_ref, kt_ref, dqt_ref,
+    q_ref, do_ref, k_ref, v_ref, up_ref, x_hbm, qd_ref, vd_ref,
+    dq_ref, dk_ref, dv_ref, bq_ref, low_ref, lent_hbm, twice_ref, kt_ref, dqt_ref, x_ref, sems,
 ):
     first, last = first_last()
+    fetch = pltpu.make_async_copy(x_hbm, x_ref, sems.at[0])
+    lend = pltpu.make_async_copy(x_hbm.at[HALF:], lent_hbm, sems.at[1])
 
     @pl.when(first)
     def _():
+        fetch.start()
+        lend.start()
         twice_ref[:, :HD] = k_ref[...]
         twice_ref[:, HD:] = k_ref[...]
         kt_ref[...] = k_ref[...].T
@@ -90,9 +94,6 @@
         dv_ref[...] = jnp.zeros_like(dv_ref)
         bq_ref[...] = jnp.zeros_like(bq_ref)
 
-    downs = jnp.concatenate([qd_ref[...], vd_ref[...]], 0)
-    low_ref[...] = lax.dot_general(downs, x_ref[...], NT, preferred_element_type=F32).astype(BF16)
-
     def add(ks, dk, dv):
         dk_ref[ks] += dk
         dv_ref[ks] += dv
@@ -102,18 +103,27 @@
 
     @pl.when(last)
     def _():
-        lent_ref[...] = x_ref[...]
+        fetch.wait()
+        downs = jnp.concatenate([qd_ref[...], vd_ref[...]], 0)
+        low_ref[...] = lax.dot_general(downs, x_ref[...], NT, preferred_element_type=F32).astype(BF16)
+        lend.wait()
 
 
 def rolled_kernel(
-    q_ref, do_ref, k_ref, v_ref, kv_ref, up_ref, _, dka_ref, dva_ref, bqa_ref, low_ref, vu_ref,
-    dq_ref, back_ref, top_ref, dk_ref, dv_ref, share_ref,
-    twice_ref, values_ref, kt_ref, dk_sum, dv_sum, bq_sum, dqt_ref,
+    q_ref, do_ref, k_ref, v_ref, kv_ref, up_ref, _, dka_hbm, dva_hbm, bqa_ref, low_ref, vu_ref,
+    dq_ref, back_ref, top_ref, rest_ref, share_ref,
+    twice_ref, values_ref, kt_ref, dk_sum, dv_sum, bq_sum, dqt_ref, dka_ref, dva_ref, sems,
 ):
     first, last = first_last()
+    fetches = [
+        pltpu.make_async_copy(dka_hbm, dka_ref, sems.at[0]),
+        pltpu.make_async_copy(dva_hbm, dva_ref, sems.at[1]),
+    ]
 
     @pl.when(first)
     def _():
+        for fetch in fetches:
+            fetch.start()
         for part in (slice(0, HD), slice(HD, 2 * HD)):
             twice_ref[:HALF, part] = kv_ref[:, :HD]
             twice_ref[HALF:, part] = k_ref[...]
@@ -121,10 +131,8 @@
         values_ref[HALF:] = v_ref[...]
         kt_ref[:, :HALF] = kv_ref[:, :HD].T
         kt_ref[:, HALF:] = k_ref[...].T
-        dk_sum[:HALF] = jnp.zeros((HALF, HD), F32)
-        dv_sum[:HALF] = jnp.zeros((HALF, HD), F32)
-        dk_sum[HALF:] = dka_ref[...]
-        dv_sum[HALF:] = dva_ref[...]
+        dk_sum[...] = jnp.zeros_like(dk_sum)
+        dv_sum[...] = jnp.zeros_like(dv_sum)
         bq_sum[...] = bqa_ref[...]
 
     def add(ks, dk, dv):
@@ -139,7 +147,11 @@
 
     @pl.when(last)
     def _():
-        dv_low = dv_sum[...].astype(BF16)
+        for fetch in fetches:
+            fetch.wait()
+        dk = (dk_sum[HALF:] + dka_ref[...]) * SCALE
+        dv = dv_sum[HALF:] + dva_ref[...]
+        dv_low = jnp.concatenate([dv_sum[:HALF], dv], 0).astype(BF16)
         bv = lax.dot_general(vu_ref[...], dv_low, NT, preferred_element_type=F32).astype(BF16)
         bq = bq_sum[...].astype(BF16)
         rows = [slice(n * RANK, (n + 1) * RANK) for n in range(3)]
@@ -152,10 +164,10 @@
             share_ref[peer, rows[2], HALF:] = bv[:, HALF:]
         back_ref[:, :HD] = (dk_sum[:HALF] * SCALE).astype(BF16)
         back_ref[:, HD:] = dv_low[:HALF]
-        top_ref[:, :HD] = (dk_sum[HALF:ROWS] * SCALE).astype(BF16)
+        top_ref[:, :HD] = dk[:HALF].astype(BF16)
         top_ref[:, HD:] = dv_low[HALF:ROWS]
-        dk_ref[...] = dk_sum[ROWS:] * SCALE
-        dv_ref[...] = dv_sum[ROWS:]
+        rest_ref[:, :HD] = dk[HALF:]
+        rest_ref[:, HD:] = dv[HALF:]
 
 
 def pack_kernel(k_ref, v_ref, kv_ref):
@@ -163,11 +175,11 @@
     kv_ref[:, HD:] = v_ref[...]
 
 
-def finish_kernel(top_ref, dk_ref, dv_ref, back_ref, gk_ref, gv_ref):
+def finish_kernel(top_ref, rest_ref, back_ref, gk_ref, gv_ref):
     gk_ref[:HALF] = top_ref[:, :HD]
     gv_ref[:HALF] = top_ref[:, HD:]
-    gk_ref[HALF:] = (dk_ref[...] + back_ref[:, :HD].astype(F32)).astype(BF16)
-    gv_ref[HALF:] = (dv_ref[...] + back_ref[:, HD:].astype(F32)).astype(BF16)
+    gk_ref[HALF:] = (rest_ref[:, :HD] + back_ref[:, :HD].astype(F32)).astype(BF16)
+    gv_ref[HALF:] = (rest_ref[:, HD:] + back_ref[:, HD:].astype(F32)).astype(BF16)
 
 
 def weights_kernel(
@@ -242,10 +254,10 @@
         grid=(2,),
         in_specs=[pl.BlockSpec((ROWS, 2 * HD), pair)] * 2
         + [whole(ROWS, HD)] * 2
-        + [pl.BlockSpec((RANK, 2 * HD), pair), pl.BlockSpec((HALF, WIDTH), lambda h: (h, 0))]
+        + [pl.BlockSpec((RANK, 2 * HD), pair), untouched]
         + [whole(RANK, WIDTH)] * 2,
         out_specs=[pl.BlockSpec((ROWS, 2 * HD), pair), whole(ROWS, HD), whole(ROWS, HD), whole(RANK, ROWS)]
-        + [pl.BlockSpec((2 * RANK, HALF), pair), whole(HALF, WIDTH)],
+        + [whole(2 * RANK, ROWS), untouched],
         out_shape=[
             struct(ROWS, WIDTH, dtype=BF16),
             struct(ROWS, HD),
@@ -258,6 +270,8 @@
             pltpu.VMEM((ROWS, 2 * HD), BF16),
             pltpu.VMEM((HD, ROWS), BF16),
             pltpu.VMEM((2 * HD, ROWS), BF16),
+            pltpu.VMEM((ROWS, WIDTH), BF16),
+            pltpu.SemaphoreType.DMA((2,)),
         ],
         compiler_params=LARGE,
         name="plain",
@@ -266,21 +280,21 @@
 
     rolled = lambda h: (0, 2 + h)
     keys = ROWS + HALF
-    dq, back, top, dk, dv, share = pl.pallas_call(
+    dq, back, top, rest, share = pl.pallas_call(
         rolled_kernel,
         grid=(2,),
         in_specs=[pl.BlockSpec((ROWS, 2 * HD), rolled)] * 2
         + [whole(ROWS, HD)] * 2
         + [whole(HALF, 2 * HD), pl.BlockSpec((RANK, 2 * HD), rolled), untouched]
-        + [whole(ROWS, HD), whole(ROWS, HD), whole(RANK, ROWS), whole(2 * RANK, ROWS), whole(RANK, HD)],
-        out_specs=[pl.BlockSpec((ROWS, 2 * HD), rolled), whole(HALF, 2 * HD), whole(HALF, 2 * HD)]
-        + [whole(HALF, HD), whole(HALF, HD), whole(tensor, 3 * RANK, keys)],
+        + [untouched, untouched, whole(RANK, ROWS), whole(2 * RANK, ROWS), whole(RANK, HD)],
+        out_specs=[pl.BlockSpec((ROWS, 2 * HD), rolled)]
+        + [whole(HALF, 2 * HD)] * 3
+        + [whole(tensor, 3 * RANK, keys)],
         out_shape=[
             struct(ROWS, WIDTH, dtype=BF16),
             struct(HALF, 2 * HD, dtype=BF16),
             struct(HALF, 2 * HD, dtype=BF16),
-            struct(HALF, HD),
-            struct(HALF, HD),
+            struct(HALF, 2 * HD),
             struct(tensor, 3 * RANK, keys, dtype=BF16),
         ],
         scratch_shapes=[
@@ -291,6 +305,9 @@
             pltpu.VMEM((keys, HD), F32),
             pltpu.VMEM((RANK, ROWS), F32),
             pltpu.VMEM((2 * HD, ROWS), BF16),
+            pltpu.VMEM((ROWS, HD), F32),
+            pltpu.VMEM((ROWS, HD), F32),
+            pltpu.SemaphoreType.DMA((2,)),
         ],
         input_output_aliases={6: 0},
         compiler_params=LARGE,
@@ -303,8 +320,7 @@
         out_shape=[struct(ROWS, HD, dtype=BF16)] * 2,
         compiler_params=SMALL,
         name="finish",
-    )(top, dk, dv, back)
-
+    )(top, rest, back)
     part_rows = 3 * RANK + 8
     inside = pl.BlockSpec(memory_space=pltpu.VMEM)
     keep, give, dq, grad_value = pl.pallas_call(

time: 80.8 us -> 103 us (1.27)
  Pallas kernels: 31.9 us -> 54.4 us
    pallas_call x1, Pallas kernels: 12.9 us -> 35.6 us  [on_device(): pl.pallas_call(plain_kernel, grid=(2,), in_specs=[pl.BlockSpec((ROWS, 2 *...]
    unnamed x10 -> x8, local copies, waits for them, and re-layouts: 2.61 us -> 1.75 us
  transfers between devices with their start and end apart: 6 -> 6, of which waited for: 4 -> 4; matrix products, arithmetic and copies ran while one was open for 0% -> 0% of each run, Pallas kernels for 33% -> 48%
where the time goes in v7:
time: 103 us
  Pallas kernels  54.4 us (53%)
  blocking collectives  17 us (17%)
  waiting for transfers between devices  16.8 us (16%)
  starting transfers between devices  12.3 us (12%)
  local copies, waits for them, and re-layouts  1.78 us (2%)
    pallas_call x1, Pallas kernels, on_device(): pl.pallas_call(plain_kernel, grid=(2,), in_specs=[pl.BlockSpec((ROWS, 2 *...  35.6 us
    all_to_all x1, blocking collectives, on_device(): lax.all_to_all(jnp.broadcast_to(part[None], (chips,) + part.shape), 'seq'...  17 us
    pallas_call x1, Pallas kernels, on_device(): pl.pallas_call(rolled_kernel, grid=(2,), in_specs=[pl.BlockSpec((ROWS, 2...  12.7 us
    all_to_all x1, waiting for transfers between devices, on_device(): gathered = lax.all_to_all(share, 'tensor', 0, 0)  9.11 us
    ppermute x1, waiting for transfers between devices, on_device(): back = lax.ppermute(back, 'seq', [(s, (s - 1) % seq) for s in range(seq)])  5.74 us
    all_to_all x1, starting transfers between devices, on_device(): gathered = lax.all_to_all(share, 'tensor', 0, 0)  5.51 us
    pallas_call x1, Pallas kernels, on_device(): pl.pallas_call(weights_kernel, in_specs=[inside] * 2 + [untouched] * 3, o...  2.83 us
    ppermute x1, starting transfers between devices, on_device(): kv = lax.ppermute(kv, 'seq', [(s, (s + 1) % seq) for s in range(seq)])  2.69 us
  transfers between devices with their start and end apart: 6, of which 4 were waited for; matrix products, arithmetic and copies ran while one was open for 0% of the time, Pallas kernels for 48%

profile of v7, /device:TPU:1, one launch (start us, length us, event | category | flops | bytes accessed | tf_op | source)
XLA Modules:
  0.0 103.1 jit_solution(12737551942172855986)
XLA Ops:
  0.6 1.7 %pack.1 = bf16[512,256]{1,0:T(8,128)(2,1)} custom-call(bf16[1024,128]{1,0:T(8,128)(2,1)} %k_ref.5, bf16[1024,128]{1,0:T(8,128)(2,1)} %v_ref.5), custom_call_target="tpu_custom_call" | custom-call | tf_op jit(solution)/shard_map/pack/pallas_call | solution.py:240
  2.4 2.7 %collective-permute-start = (bf16[512,256]{1,0:T(8,128)(2,1)}, bf16[512,256]{1,0:T(8,128)(2,1)S(1)}, u32[]{:S(2)}, u32[]{:S(2)}) collective-permute-start(bf16[512,256]{1,0:T(8,128)(2,1)} %pack.1), channel_id=1, source_target_pairs={{0,8},{8,16},{16,24},{24,32},{32,40},{40,48},{48,56},{56,64},{64,7... | collective-permute-start | bytes 786440 | tf_op jit(solution)/shard_map/ppermute | solution.py:249
  5.0 35.6 %plain.1 = (bf16[1024,1024]{1,0:T(8,128)(2,1)}, f32[1024,128]{1,0:T(8,128)}, f32[1024,128]{1,0:T(8,128)}, f32[16,1024]{1,0:T(8,128)}, bf16[32,1024]{1,0:T(8,128)(2,1)}, /*index=5*/bf16[512,1024]{1,0:T(8,128)(2,1)}) custom-call(bf16[1024,1024]{1,0:T(8,128)(2,1)} %q_ref.3, bf16[1024,1024]{1,0:T(8,128)(2,1)} %do_ref.3, bf16[1024,128]{1,0:T(8,128)(2,1)} %k_ref.5, ...), custom_call_target="tpu_custom_call" | custom-call | tf_op jit(solution)/shard_map/plain/pallas_call | solution.py:252
  40.7 0.1 collective-permute-start.1
  40.7 0.0 collective-permute-done.kv_ref
  40.8 0.0 copy-start.3
  40.8 0.7 copy-done.3
  41.5 12.7 %rolled.1 = (bf16[1024,1024]{1,0:T(8,128)(2,1)}, bf16[512,256]{1,0:T(8,128)(2,1)}, bf16[512,256]{1,0:T(8,128)(2,1)}, f32[512,256]{1,0:T(8,128)}, bf16[8,48,1536]{2,1,0:T(8,128)(2,1)}) custom-call(bf16[1024,1024]{1,0:T(8,128)(2,1)} %q_ref.3, bf16[1024,1024]{1,0:T(8,128)(2,1)} %do_ref.3, bf16[1024,128]{1,0:T(8,128)(2,1)} %k_ref.5, ...), custom_call_target="tpu_custom_call", output_to_operand_aliasing={{0}: (6, {})} | custom-call | tf_op jit(solution)/shard_map/rolled/pallas_call | solution.py:283
  54.2 0.0 copy-start.2
  54.2 0.0 copy-start
  54.2 5.5 %all-to-all-start = ((bf16[8,48,1536]{2,1,0:T(8,128)(2,1)}), bf16[8,48,1536]{2,1,0:T(8,128)(2,1)S(1)}, u32[]{:S(2)}, u32[]{:S(2)}) async-start(bf16[8,48,1536]{2,1,0:T(8,128)(2,1)} %get-tuple-element.33), calls=%async_computation | async-start | bytes 2359296 | tf_op jit(solution)/shard_map/all_to_all | solution.py:317
  59.7 0.8 collective-permute-start.2
  60.5 5.7 %collective-permute-done.2.back_ref = bf16[512,256]{1,0:T(8,128)(2,1)S(1)} collective-permute-done((bf16[512,256]{1,0:T(8,128)(2,1)}, bf16[512,256]{1,0:T(8,128)(2,1)S(1)}, u32[]{:S(2)}, u32[]{:S(2)}) %collective-permute-start.2) | collective-permute-done | bytes 262176 | tf_op jit(solution)/shard_map/ppermute | solution.py:316
  66.2 0.0 copy-done.2
  66.2 0.0 copy-start.1
  66.2 1.0 %copy-done.1 = f32[512,256]{1,0:T(8,128)S(1)} copy-done((f32[512,256]{1,0:T(8,128)S(1)}, f32[512,256]{1,0:T(8,128)}, u32[]{:S(2)}) %copy-start.1) | copy-done | bytes 524312
  67.3 0.9 finish.1
  68.1 0.0 collective-permute-done.1.lent_hbm
  68.1 9.1 %all-to-all-done.all_ref = bf16[8,48,1536]{2,1,0:T(8,128)(2,1)S(1)} async-done(((bf16[8,48,1536]{2,1,0:T(8,128)(2,1)}), bf16[8,48,1536]{2,1,0:T(8,128)(2,1)S(1)}, u32[]{:S(2)}, u32[]{:S(2)}) %all-to-all-start) | async-done | bytes 1179680 | tf_op jit(solution)/shard_map/all_to_all | solution.py:317
  77.3 0.0 copy-done
  77.3 2.8 %weights.1 = (f32[56,512]{1,0:T(8,128)S(1)}, f32[56,512]{1,0:T(8,128)S(1)}, bf16[1024,1024]{1,0:T(8,128)(2,1)}, bf16[1024,128]{1,0:T(8,128)(2,1)}) custom-call(bf16[8,48,1536]{2,1,0:T(8,128)(2,1)S(1)} %all-to-all-done.all_ref, bf16[1024,1024]{1,0:T(8,128)(2,1)S(1)} %copy-done, ...), custom_call_target="tpu_custom_call", output_to_operand_aliasing={{2}: (3, {}), {3}: (4, {})} | custom-call | tf_op jit(solution)/shard_map/weights/pallas_call | solution.py:326
  80.1 1.6 %collective-permute-start.3 = (f32[56,512]{1,0:T(8,128)S(1)}, f32[56,512]{1,0:T(8,128)S(1)}, u32[]{:S(2)}, u32[]{:S(2)}) collective-permute-start(f32[56,512]{1,0:T(8,128)S(1)} %get-tuple-element.44), channel_id=1, source_target_pairs={{0,8},{8,0},{16,24},{24,16},{32,40},{40,32},{48,56},{56,48},{64,72... | collective-permute-start | bytes 344072 | tf_op jit(solution)/shard_map/ppermute | solution.py:344
  81.7 1.0 collective-permute-done.3
  82.7 17.0 %all_to_all.10 = bf16[8,56,512]{2,1,0:T(8,128)(2,1)S(1)} all-to-all(bf16[8,56,512]{2,1,0:T(8,128)(2,1)S(1)} %broadcast_in_dim.2), channel_id=1, replica_groups={{0,16,32,48,64,80,96,112},{8,24,40,56,72,88,104,120},{1,17,33,49,65,81,..., dimensions={0} | all-to-all | bytes 917504 | tf_op jit(solution)/shard_map/all_to_all | solution.py:346
  99.7 0.1 convert_reduce_fusion.mine_ref
  99.8 1.6 %collective-permute-start.4 = (f32[56,512]{1,0:T(8,128)S(1)}, f32[56,512]{1,0:T(8,128)S(1)}, u32[]{:S(2)}, u32[]{:S(2)}) collective-permute-start(f32[56,512]{1,0:T(8,128)S(1)} %convert_reduce_fusion.mine_ref), channel_id=1, source_target_pairs={{0,8},{8,0},{16,24},{24,16},{32,40},{40,32},{48,56},{56,48},{64,72... | collective-permute-start | bytes 344072 | tf_op jit(solution)/shard_map/ppermute | solution.py:354
  101.4 1.0 collective-permute-done.4.other_ref
  102.4 0.7 place.1
  (2 shorter events, 0.0 us)
Async XLA Ops:
  2.4 38.4 %collective-permute-start = (bf16[512,256]{1,0:T(8,128)(2,1)}, bf16[512,256]{1,0:T(8,128)(2,1)S(1)}, u32[]{:S(2)}, u32[]{:S(2)}) collective-permute-start(bf16[512,256]{1,0:T(8,128)(2,1)} %pack.1), channel_id=1, source_target_pairs={{0,8},{8,16},{16,24},{24,32},{32,40},{40,48},{48,56},{56,64},{64,7... | collective-permute-start | bytes 786440 | tf_op jit(solution)/shard_map/ppermute | solution.py:249
  40.7 27.5 %collective-permute-start.1 = (bf16[512,1024]{1,0:T(8,128)(2,1)}, bf16[512,1024]{1,0:T(8,128)(2,1)}, u32[]{:S(2)}, u32[]{:S(2)}) collective-permute-start(bf16[512,1024]{1,0:T(8,128)(2,1)} %get-tuple-element.34), channel_id=1, source_target_pairs={{0,8},{8,16},{16,24},{24,32},{32,40},{40,48},{48,56},{56,64},{64,7... | collective-permute-start | bytes 3145736 | tf_op jit(solution)/shard_map/ppermute | solution.py:279
  40.8 0.7 copy-start.3
  54.2 12.0 %copy-start.2 = (bf16[512,256]{1,0:T(8,128)(2,1)S(1)}, bf16[512,256]{1,0:T(8,128)(2,1)}, u32[]{:S(2)}) copy-start(bf16[512,256]{1,0:T(8,128)(2,1)} %get-tuple-element.36.top_ref) | copy-start | bytes 786436
  54.2 23.1 %copy-start = (bf16[1024,1024]{1,0:T(8,128)(2,1)S(1)}, bf16[1024,1024]{1,0:T(8,128)(2,1)}, u32[]{:S(2)}) copy-start(bf16[1024,1024]{1,0:T(8,128)(2,1)} %x_ref.1) | copy-start | bytes 6291460
  54.2 23.1 %all-to-all-start = ((bf16[8,48,1536]{2,1,0:T(8,128)(2,1)}), bf16[8,48,1536]{2,1,0:T(8,128)(2,1)S(1)}, u32[]{:S(2)}, u32[]{:S(2)}) async-start(bf16[8,48,1536]{2,1,0:T(8,128)(2,1)} %get-tuple-element.33), calls=%async_computation | async-start | bytes 2359296 | tf_op jit(solution)/shard_map/all_to_all | solution.py:317
  59.7 6.5 %collective-permute-start.2 = (bf16[512,256]{1,0:T(8,128)(2,1)}, bf16[512,256]{1,0:T(8,128)(2,1)S(1)}, u32[]{:S(2)}, u32[]{:S(2)}) collective-permute-start(bf16[512,256]{1,0:T(8,128)(2,1)} %get-tuple-element.38), channel_id=1, source_target_pairs={{0,120},{8,0},{16,8},{24,16},{32,24},{40,32},{48,40},{56,48},{64,5... | collective-permute-start | bytes 786440 | tf_op jit(solution)/shard_map/ppermute | solution.py:316
  66.2 1.0 %copy-start.1 = (f32[512,256]{1,0:T(8,128)S(1)}, f32[512,256]{1,0:T(8,128)}, u32[]{:S(2)}) copy-start(f32[512,256]{1,0:T(8,128)} %get-tuple-element.37.rest_ref) | copy-start | bytes 1572868
  80.1 2.6 %collective-permute-start.3 = (f32[56,512]{1,0:T(8,128)S(1)}, f32[56,512]{1,0:T(8,128)S(1)}, u32[]{:S(2)}, u32[]{:S(2)}) collective-permute-start(f32[56,512]{1,0:T(8,128)S(1)} %get-tuple-element.44), channel_id=1, source_target_pairs={{0,8},{8,0},{16,24},{24,16},{32,40},{40,32},{48,56},{56,48},{64,72... | collective-permute-start | bytes 344072 | tf_op jit(solution)/shard_map/ppermute | solution.py:344
  99.8 2.6 %collective-permute-start.4 = (f32[56,512]{1,0:T(8,128)S(1)}, f32[56,512]{1,0:T(8,128)S(1)}, u32[]{:S(2)}, u32[]{:S(2)}) collective-permute-start(f32[56,512]{1,0:T(8,128)S(1)} %convert_reduce_fusion.mine_ref), channel_id=1, source_target_pairs={{0,8},{8,0},{16,24},{24,16},{32,40},{40,32},{48,56},{56,48},{64,72... | collective-permute-start | bytes 344072 | tf_op jit(solution)/shard_map/ppermute | solution.py:354

commit v8 on v7

--- a/solution.py
+++ b/solution.py
@@ -81,12 +81,11 @@
 ):
     first, last = first_last()
     fetch = pltpu.make_async_copy(x_hbm, x_ref, sems.at[0])
-    lend = pltpu.make_async_copy(x_hbm.at[HALF:], lent_hbm, sems.at[1])
+    lend = pltpu.make_async_copy(x_ref.at[HALF:], lent_hbm, sems.at[1])
 
     @pl.when(first)
     def _():
         fetch.start()
-        lend.start()
         twice_ref[:, :HD] = k_ref[...]
         twice_ref[:, HD:] = k_ref[...]
         kt_ref[...] = k_ref[...].T
@@ -94,6 +93,11 @@
         dv_ref[...] = jnp.zeros_like(dv_ref)
         bq_ref[...] = jnp.zeros_like(bq_ref)
 
+    @pl.when(last)
+    def _():
+        fetch.wait()
+        lend.start()
+
     def add(ks, dk, dv):
         dk_ref[ks] += dk
         dv_ref[ks] += dv
@@ -103,7 +107,6 @@
 
     @pl.when(last)
     def _():
-        fetch.wait()
         downs = jnp.concatenate([qd_ref[...], vd_ref[...]], 0)
         low_ref[...] = lax.dot_general(downs, x_ref[...], NT, preferred_element_type=F32).astype(BF16)
         lend.wait()

time: 103 us -> 80 us (0.78)
  Pallas kernels: 54.4 us -> 31 us
    pallas_call x1, Pallas kernels: 35.6 us -> 12.2 us  [on_device(): pl.pallas_call(plain_kernel, grid=(2,), in_specs=[pl.BlockSpec((ROWS, 2 *...]
  transfers between devices with their start and end apart: 6 -> 6, of which waited for: 4 -> 4; matrix products, arithmetic and copies ran while one was open for 0% -> 0% of each run, Pallas kernels for 48% -> 32%
where the time goes in v8:
time: 80 us; the launch traced here: 79.7 us
  Pallas kernels  31 us (39%)
  blocking collectives  17 us (21%)
  waiting for transfers between devices  16.8 us (21%)
  starting transfers between devices  12.3 us (15%)
  local copies, waits for them, and re-layouts  1.78 us (2%)
    all_to_all x1, blocking collectives, on_device(): lax.all_to_all(jnp.broadcast_to(part[None], (chips,) + part.shape), 'seq'...  17 us
    pallas_call x1, Pallas kernels, on_device(): pl.pallas_call(rolled_kernel, grid=(2,), in_specs=[pl.BlockSpec((ROWS, 2...  12.7 us
    pallas_call x1, Pallas kernels, on_device(): pl.pallas_call(plain_kernel, grid=(2,), in_specs=[pl.BlockSpec((ROWS, 2 *...  12.2 us
    all_to_all x1, waiting for transfers between devices, on_device(): gathered = lax.all_to_all(share, 'tensor', 0, 0)  9.11 us
    ppermute x1, waiting for transfers between devices, on_device(): back = lax.ppermute(back, 'seq', [(s, (s - 1) % seq) for s in range(seq)])  5.74 us
    all_to_all x1, starting transfers between devices, on_device(): gathered = lax.all_to_all(share, 'tensor', 0, 0)  5.52 us
    pallas_call x1, Pallas kernels, on_device(): pl.pallas_call(weights_kernel, in_specs=[inside] * 2 + [untouched] * 3, o...  2.83 us
    ppermute x1, starting transfers between devices, on_device(): kv = lax.ppermute(kv, 'seq', [(s, (s + 1) % seq) for s in range(seq)])  2.69 us
  transfers between devices with their start and end apart: 6, of which 4 were waited for; matrix products, arithmetic and copies ran while one was open for 0% of the time, Pallas kernels for 32%

profile of v8, /device:TPU:1, one launch (start us, length us, event | category | flops | bytes accessed | tf_op | source)
XLA Modules:
  0.0 79.7 jit_solution(12333785689203155971)
XLA Ops:
  0.6 1.7 %pack.1 = bf16[512,256]{1,0:T(8,128)(2,1)} custom-call(bf16[1024,128]{1,0:T(8,128)(2,1)} %k_ref.5, bf16[1024,128]{1,0:T(8,128)(2,1)} %v_ref.5), custom_call_target="tpu_custom_call" | custom-call | tf_op jit(solution)/shard_map/pack/pallas_call | solution.py:243
  2.4 2.7 %collective-permute-start = (bf16[512,256]{1,0:T(8,128)(2,1)}, bf16[512,256]{1,0:T(8,128)(2,1)S(1)}, u32[]{:S(2)}, u32[]{:S(2)}) collective-permute-start(bf16[512,256]{1,0:T(8,128)(2,1)} %pack.1), channel_id=1, source_target_pairs={{0,8},{8,16},{16,24},{24,32},{32,40},{40,48},{48,56},{56,64},{64,7... | collective-permute-start | bytes 786440 | tf_op jit(solution)/shard_map/ppermute | solution.py:252
  5.0 12.2 %plain.1 = (bf16[1024,1024]{1,0:T(8,128)(2,1)}, f32[1024,128]{1,0:T(8,128)}, f32[1024,128]{1,0:T(8,128)}, f32[16,1024]{1,0:T(8,128)}, bf16[32,1024]{1,0:T(8,128)(2,1)}, /*index=5*/bf16[512,1024]{1,0:T(8,128)(2,1)}) custom-call(bf16[1024,1024]{1,0:T(8,128)(2,1)} %q_ref.3, bf16[1024,1024]{1,0:T(8,128)(2,1)} %do_ref.3, bf16[1024,128]{1,0:T(8,128)(2,1)} %k_ref.5, ...), custom_call_target="tpu_custom_call" | custom-call | tf_op jit(solution)/shard_map/plain/pallas_call | solution.py:255
  17.3 0.1 collective-permute-start.1
  17.3 0.0 collective-permute-done.kv_ref
  17.3 0.0 copy-start.3
  17.4 0.7 copy-done.3
  18.1 12.7 %rolled.1 = (bf16[1024,1024]{1,0:T(8,128)(2,1)}, bf16[512,256]{1,0:T(8,128)(2,1)}, bf16[512,256]{1,0:T(8,128)(2,1)}, f32[512,256]{1,0:T(8,128)}, bf16[8,48,1536]{2,1,0:T(8,128)(2,1)}) custom-call(bf16[1024,1024]{1,0:T(8,128)(2,1)} %q_ref.3, bf16[1024,1024]{1,0:T(8,128)(2,1)} %do_ref.3, bf16[1024,128]{1,0:T(8,128)(2,1)} %k_ref.5, ...), custom_call_target="tpu_custom_call", output_to_operand_aliasing={{0}: (6, {})} | custom-call | tf_op jit(solution)/shard_map/rolled/pallas_call | solution.py:286
  30.8 0.0 copy-start.2
  30.8 0.0 copy-start
  30.8 5.5 %all-to-all-start = ((bf16[8,48,1536]{2,1,0:T(8,128)(2,1)}), bf16[8,48,1536]{2,1,0:T(8,128)(2,1)S(1)}, u32[]{:S(2)}, u32[]{:S(2)}) async-start(bf16[8,48,1536]{2,1,0:T(8,128)(2,1)} %get-tuple-element.33), calls=%async_computation | async-start | bytes 2359296 | tf_op jit(solution)/shard_map/all_to_all | solution.py:320
  36.3 0.8 collective-permute-start.2
  37.1 5.7 %collective-permute-done.2.back_ref = bf16[512,256]{1,0:T(8,128)(2,1)S(1)} collective-permute-done((bf16[512,256]{1,0:T(8,128)(2,1)}, bf16[512,256]{1,0:T(8,128)(2,1)S(1)}, u32[]{:S(2)}, u32[]{:S(2)}) %collective-permute-start.2) | collective-permute-done | bytes 262176 | tf_op jit(solution)/shard_map/ppermute | solution.py:319
  42.8 0.0 copy-done.2
  42.8 0.0 copy-start.1
  42.8 1.0 %copy-done.1 = f32[512,256]{1,0:T(8,128)S(1)} copy-done((f32[512,256]{1,0:T(8,128)S(1)}, f32[512,256]{1,0:T(8,128)}, u32[]{:S(2)}) %copy-start.1) | copy-done | bytes 524312
  43.9 0.9 %finish.1 = (bf16[1024,128]{1,0:T(8,128)(2,1)}, bf16[1024,128]{1,0:T(8,128)(2,1)}) custom-call(bf16[512,256]{1,0:T(8,128)(2,1)S(1)} %copy-done.2, f32[512,256]{1,0:T(8,128)S(1)} %copy-done.1, bf16[512,256]{1,0:T(8,128)(2,1)S(1)} %collective-permute-done.2.back_ref), custom_call_target="tpu_custom_call" | custom-call | tf_op jit(solution)/shard_map/finish/pallas_call | solution.py:321
  44.7 0.0 collective-permute-done.1.lent_hbm
  44.7 9.1 %all-to-all-done.all_ref = bf16[8,48,1536]{2,1,0:T(8,128)(2,1)S(1)} async-done(((bf16[8,48,1536]{2,1,0:T(8,128)(2,1)}), bf16[8,48,1536]{2,1,0:T(8,128)(2,1)S(1)}, u32[]{:S(2)}, u32[]{:S(2)}) %all-to-all-start) | async-done | bytes 1179680 | tf_op jit(solution)/shard_map/all_to_all | solution.py:320
  53.9 0.0 copy-done
  53.9 2.8 %weights.1 = (f32[56,512]{1,0:T(8,128)S(1)}, f32[56,512]{1,0:T(8,128)S(1)}, bf16[1024,1024]{1,0:T(8,128)(2,1)}, bf16[1024,128]{1,0:T(8,128)(2,1)}) custom-call(bf16[8,48,1536]{2,1,0:T(8,128)(2,1)S(1)} %all-to-all-done.all_ref, bf16[1024,1024]{1,0:T(8,128)(2,1)S(1)} %copy-done, ...), custom_call_target="tpu_custom_call", output_to_operand_aliasing={{2}: (3, {}), {3}: (4, {})} | custom-call | tf_op jit(solution)/shard_map/weights/pallas_call | solution.py:329
  56.7 1.6 %collective-permute-start.3 = (f32[56,512]{1,0:T(8,128)S(1)}, f32[56,512]{1,0:T(8,128)S(1)}, u32[]{:S(2)}, u32[]{:S(2)}) collective-permute-start(f32[56,512]{1,0:T(8,128)S(1)} %get-tuple-element.44), channel_id=1, source_target_pairs={{0,8},{8,0},{16,24},{24,16},{32,40},{40,32},{48,56},{56,48},{64,72... | collective-permute-start | bytes 344072 | tf_op jit(solution)/shard_map/ppermute | solution.py:347
  58.3 1.0 %collective-permute-done.3 = f32[56,512]{1,0:T(8,128)S(1)} collective-permute-done((f32[56,512]{1,0:T(8,128)S(1)}, f32[56,512]{1,0:T(8,128)S(1)}, u32[]{:S(2)}, u32[]{:S(2)}) %collective-permute-start.3) | collective-permute-done | bytes 114720 | tf_op jit(solution)/shard_map/ppermute | solution.py:347
  59.3 17.0 %all_to_all.10 = bf16[8,56,512]{2,1,0:T(8,128)(2,1)S(1)} all-to-all(bf16[8,56,512]{2,1,0:T(8,128)(2,1)S(1)} %broadcast_in_dim.2), channel_id=1, replica_groups={{0,16,32,48,64,80,96,112},{8,24,40,56,72,88,104,120},{1,17,33,49,65,81,..., dimensions={0} | all-to-all | bytes 917504 | tf_op jit(solution)/shard_map/all_to_all | solution.py:349
  76.3 0.1 convert_reduce_fusion.mine_ref
  76.4 1.6 %collective-permute-start.4 = (f32[56,512]{1,0:T(8,128)S(1)}, f32[56,512]{1,0:T(8,128)S(1)}, u32[]{:S(2)}, u32[]{:S(2)}) collective-permute-start(f32[56,512]{1,0:T(8,128)S(1)} %convert_reduce_fusion.mine_ref), channel_id=1, source_target_pairs={{0,8},{8,0},{16,24},{24,16},{32,40},{40,32},{48,56},{56,48},{64,72... | collective-permute-start | bytes 344072 | tf_op jit(solution)/shard_map/ppermute | solution.py:357
  78.0 1.0 %collective-permute-done.4.other_ref = f32[56,512]{1,0:T(8,128)S(1)} collective-permute-done((f32[56,512]{1,0:T(8,128)S(1)}, f32[56,512]{1,0:T(8,128)S(1)}, u32[]{:S(2)}, u32[]{:S(2)}) %collective-permute-start.4) | collective-permute-done | bytes 114720 | tf_op jit(solution)/shard_map/ppermute | solution.py:357
  79.0 0.7 place.1
  (2 shorter events, 0.0 us)
Async XLA Ops:
  2.4 15.0 %collective-permute-start = (bf16[512,256]{1,0:T(8,128)(2,1)}, bf16[512,256]{1,0:T(8,128)(2,1)S(1)}, u32[]{:S(2)}, u32[]{:S(2)}) collective-permute-start(bf16[512,256]{1,0:T(8,128)(2,1)} %pack.1), channel_id=1, source_target_pairs={{0,8},{8,16},{16,24},{24,32},{32,40},{40,48},{48,56},{56,64},{64,7... | collective-permute-start | bytes 786440 | tf_op jit(solution)/shard_map/ppermute | solution.py:252
  17.3 27.5 %collective-permute-start.1 = (bf16[512,1024]{1,0:T(8,128)(2,1)}, bf16[512,1024]{1,0:T(8,128)(2,1)}, u32[]{:S(2)}, u32[]{:S(2)}) collective-permute-start(bf16[512,1024]{1,0:T(8,128)(2,1)} %get-tuple-element.34), channel_id=1, source_target_pairs={{0,8},{8,16},{16,24},{24,32},{32,40},{40,48},{48,56},{56,64},{64,7... | collective-permute-start | bytes 3145736 | tf_op jit(solution)/shard_map/ppermute | solution.py:282
  17.3 0.7 copy-start.3
  30.8 12.1 %copy-start.2 = (bf16[512,256]{1,0:T(8,128)(2,1)S(1)}, bf16[512,256]{1,0:T(8,128)(2,1)}, u32[]{:S(2)}) copy-start(bf16[512,256]{1,0:T(8,128)(2,1)} %get-tuple-element.36.top_ref) | copy-start | bytes 786436
  30.8 23.1 %copy-start = (bf16[1024,1024]{1,0:T(8,128)(2,1)S(1)}, bf16[1024,1024]{1,0:T(8,128)(2,1)}, u32[]{:S(2)}) copy-start(bf16[1024,1024]{1,0:T(8,128)(2,1)} %x_ref.1) | copy-start | bytes 6291460
  30.8 23.1 %all-to-all-start = ((bf16[8,48,1536]{2,1,0:T(8,128)(2,1)}), bf16[8,48,1536]{2,1,0:T(8,128)(2,1)S(1)}, u32[]{:S(2)}, u32[]{:S(2)}) async-start(bf16[8,48,1536]{2,1,0:T(8,128)(2,1)} %get-tuple-element.33), calls=%async_computation | async-start | bytes 2359296 | tf_op jit(solution)/shard_map/all_to_all | solution.py:320
  36.3 6.5 %collective-permute-start.2 = (bf16[512,256]{1,0:T(8,128)(2,1)}, bf16[512,256]{1,0:T(8,128)(2,1)S(1)}, u32[]{:S(2)}, u32[]{:S(2)}) collective-permute-start(bf16[512,256]{1,0:T(8,128)(2,1)} %get-tuple-element.38), channel_id=1, source_target_pairs={{0,120},{8,0},{16,8},{24,16},{32,24},{40,32},{48,40},{56,48},{64,5... | collective-permute-start | bytes 786440 | tf_op jit(solution)/shard_map/ppermute | solution.py:319
  42.8 1.0 %copy-start.1 = (f32[512,256]{1,0:T(8,128)S(1)}, f32[512,256]{1,0:T(8,128)}, u32[]{:S(2)}) copy-start(f32[512,256]{1,0:T(8,128)} %get-tuple-element.37.rest_ref) | copy-start | bytes 1572868
  56.7 2.6 %collective-permute-start.3 = (f32[56,512]{1,0:T(8,128)S(1)}, f32[56,512]{1,0:T(8,128)S(1)}, u32[]{:S(2)}, u32[]{:S(2)}) collective-permute-start(f32[56,512]{1,0:T(8,128)S(1)} %get-tuple-element.44), channel_id=1, source_target_pairs={{0,8},{8,0},{16,24},{24,16},{32,40},{40,32},{48,56},{56,48},{64,72... | collective-permute-start | bytes 344072 | tf_op jit(solution)/shard_map/ppermute | solution.py:347
  76.4 2.6 %collective-permute-start.4 = (f32[56,512]{1,0:T(8,128)S(1)}, f32[56,512]{1,0:T(8,128)S(1)}, u32[]{:S(2)}, u32[]{:S(2)}) collective-permute-start(f32[56,512]{1,0:T(8,128)S(1)} %convert_reduce_fusion.mine_ref), channel_id=1, source_target_pairs={{0,8},{8,0},{16,24},{24,16},{32,40},{40,32},{48,56},{56,48},{64,72... | collective-permute-start | bytes 344072 | tf_op jit(solution)/shard_map/ppermute | solution.py:357

commit v9 on v8

--- a/solution.py
+++ b/solution.py
@@ -113,7 +113,7 @@
 
 
 def rolled_kernel(
-    q_ref, do_ref, k_ref, v_ref, kv_ref, up_ref, _, dka_hbm, dva_hbm, bqa_ref, low_ref, vu_ref,
+    q_ref, do_ref, k_ref, v_ref, kb_ref, vb_ref, up_ref, _, dka_hbm, dva_hbm, bqa_ref, low_ref, vu_ref,
     dq_ref, back_ref, top_ref, rest_ref, share_ref,
     twice_ref, values_ref, kt_ref, dk_sum, dv_sum, bq_sum, dqt_ref, dka_ref, dva_ref, sems,
 ):
@@ -128,11 +128,11 @@
         for fetch in fetches:
             fetch.start()
         for part in (slice(0, HD), slice(HD, 2 * HD)):
-            twice_ref[:HALF, part] = kv_ref[:, :HD]
+            twice_ref[:HALF, part] = kb_ref[...]
             twice_ref[HALF:, part] = k_ref[...]
-        values_ref[:HALF] = kv_ref[:, HD:]
+        values_ref[:HALF] = vb_ref[...]
         values_ref[HALF:] = v_ref[...]
-        kt_ref[:, :HALF] = kv_ref[:, :HD].T
+        kt_ref[:, :HALF] = kb_ref[...].T
         kt_ref[:, HALF:] = k_ref[...].T
         dk_sum[...] = jnp.zeros_like(dk_sum)
         dv_sum[...] = jnp.zeros_like(dv_sum)
@@ -171,11 +171,6 @@
         top_ref[:, HD:] = dv_low[HALF:ROWS]
         rest_ref[:, :HD] = dk[HALF:]
         rest_ref[:, HD:] = dv[HALF:]
-
-
-def pack_kernel(k_ref, v_ref, kv_ref):
-    kv_ref[:, :HD] = k_ref[...]
-    kv_ref[:, HD:] = v_ref[...]
 
 
 def finish_kernel(top_ref, rest_ref, back_ref, gk_ref, gv_ref):
@@ -240,16 +235,9 @@
     untouched = pl.BlockSpec(memory_space=pl.ANY)
     bottom = pl.BlockSpec((HALF, HD), lambda h: (1, 0))
 
-    kv = pl.pallas_call(
-        pack_kernel,
-        grid=(1,),
-        in_specs=[bottom, bottom],
-        out_specs=whole(HALF, 2 * HD),
-        out_shape=struct(HALF, 2 * HD, dtype=BF16),
-        compiler_params=LARGE,
-        name="pack",
-    )(key, value)
-    kv = lax.ppermute(kv, "seq", [(s, (s + 1) % seq) for s in range(seq)])
+    onward = [(s, (s + 1) % seq) for s in range(seq)]
+    borrowed_key = lax.ppermute(key, "seq", onward)
+    borrowed_value = lax.ppermute(value, "seq", onward)
 
     pair = lambda h: (0, h)
     dq, dk, dv, bq, low, lent = pl.pallas_call(
@@ -279,7 +267,7 @@
         compiler_params=LARGE,
         name="plain",
     )(query, cotangent, key, value, q_up, x, q_down, v_down)
-    lent = lax.ppermute(lent, "seq", [(s, (s + 1) % seq) for s in range(seq)])
+    lent = lax.ppermute(lent, "seq", onward)
 
     rolled = lambda h: (0, 2 + h)
     keys = ROWS + HALF
@@ -288,7 +276,7 @@
         grid=(2,),
         in_specs=[pl.BlockSpec((ROWS, 2 * HD), rolled)] * 2
         + [whole(ROWS, HD)] * 2
-        + [whole(HALF, 2 * HD), pl.BlockSpec((RANK, 2 * HD), rolled), untouched]
+        + [bottom, bottom, pl.BlockSpec((RANK, 2 * HD), rolled), untouched]
         + [untouched, untouched, whole(RANK, ROWS), whole(2 * RANK, ROWS), whole(RANK, HD)],
         out_specs=[pl.BlockSpec((ROWS, 2 * HD), rolled)]
         + [whole(HALF, 2 * HD)] * 3
@@ -312,10 +300,10 @@
             pltpu.VMEM((ROWS, HD), F32),
             pltpu.SemaphoreType.DMA((2,)),
         ],
-        input_output_aliases={6: 0},
+        input_output_aliases={7: 0},
         compiler_params=LARGE,
         name="rolled",
-    )(query, cotangent, key, value, kv, q_up, dq, dk, dv, bq, low, v_up)
+    )(query, cotangent, key, value, borrowed_key, borrowed_value, q_up, dq, dk, dv, bq, low, v_up)
     back = lax.ppermute(back, "seq", [(s, (s - 1) % seq) for s in range(seq)])
     gathered = lax.all_to_all(share, "tensor", 0, 0)
     grad_key, grad_value = pl.pallas_call(

time: 80 us -> 79.9 us (level)
  waiting for transfers between devices: 16.8 us -> 18.8 us
  Pallas kernels: 31 us -> 29.3 us
  blocking collectives: 17 us -> 15.9 us
    ppermute x2 -> x3, starting transfers between devices: 2.78 us -> 4.51 us  [the longest x1 2.76 us: on_device(): borrowed_key = lax.ppermute(key, 'seq', onward)]
    pallas_call x1 -> x0, Pallas kernels: 1.72 us -> none  [on_device(): pl.pallas_call(pack_kernel, grid=(1,), in_specs=[bottom, bottom], out_spe...]
    all_to_all x1, waiting for transfers between devices: 9.11 us -> 10.5 us  [on_device(): gathered = lax.all_to_all(share, 'tensor', 0, 0)]
    ppermute x1, starting transfers between devices: 1.6 us -> 0.47 us  [on_device(): part = (keep + lax.ppermute(give, 'seq', swap)).astype(BF16)]
    all_to_all x1, blocking collectives: 17 us -> 15.9 us  [on_device(): lax.all_to_all(jnp.broadcast_to(part[None], (chips,) + part.shape), 'seq'...]
    unnamed x8 -> x10, local copies, waits for them, and re-layouts: 1.75 us -> 1.83 us
  transfers between devices with their start and end apart: 6 -> 7, of which waited for: 4 -> 4; matrix products, arithmetic and copies ran while one was open for 0% -> 0% of each run, Pallas kernels for 32% -> 33%
where the time goes in v9:
time: 79.9 us; the launch traced here: 78.8 us
  Pallas kernels  29.3 us (37%)
  waiting for transfers between devices  18.8 us (24%)
  blocking collectives  15.9 us (20%)
  starting transfers between devices  12.2 us (15%)
  local copies, waits for them, and re-layouts  1.86 us (2%)
    all_to_all x1, blocking collectives, on_device(): lax.all_to_all(jnp.broadcast_to(part[None], (chips,) + part.shape), 'seq'...  15.9 us
    pallas_call x1, Pallas kernels, on_device(): pl.pallas_call(rolled_kernel, grid=(2,), in_specs=[pl.BlockSpec((ROWS, 2...  12.7 us
    pallas_call x1, Pallas kernels, on_device(): pl.pallas_call(plain_kernel, grid=(2,), in_specs=[pl.BlockSpec((ROWS, 2 *...  12.2 us
    all_to_all x1, waiting for transfers between devices, on_device(): gathered = lax.all_to_all(share, 'tensor', 0, 0)  10.5 us
    ppermute x1, waiting for transfers between devices, on_device(): back = lax.ppermute(back, 'seq', [(s, (s - 1) % seq) for s in range(seq)])  6.29 us
    all_to_all x1, starting transfers between devices, on_device(): gathered = lax.all_to_all(share, 'tensor', 0, 0)  5.52 us
    pallas_call x1, Pallas kernels, on_device(): pl.pallas_call(weights_kernel, in_specs=[inside] * 2 + [untouched] * 3, o...  2.83 us
    ppermute x1, starting transfers between devices, on_device(): borrowed_key = lax.ppermute(key, 'seq', onward)  2.76 us
  transfers between devices with their start and end apart: 7, of which 4 were waited for; matrix products, arithmetic and copies ran while one was open for 0% of the time, Pallas kernels for 33%

profile of v9, /device:TPU:1, one launch (start us, length us, event | category | flops | bytes accessed | tf_op | source)
XLA Modules:
  0.0 78.8 jit_solution(971330843668053891)
XLA Ops:
  0.6 2.8 %collective-permute-start = (bf16[1024,128]{1,0:T(8,128)(2,1)}, bf16[1024,128]{1,0:T(8,128)(2,1)S(1)}, u32[]{:S(2)}, u32[]{:S(2)}) collective-permute-start(bf16[1024,128]{1,0:T(8,128)(2,1)} %k_ref.3), channel_id=1, source_target_pairs={{0,8},{8,16},{16,24},{24,32},{32,40},{40,48},{48,56},{56,64},{64,7... | collective-permute-start | bytes 786440 | tf_op jit(solution)/shard_map/ppermute | solution.py:239
  3.4 0.1 collective-permute-start.1
  3.5 12.2 %plain.1 = (bf16[1024,1024]{1,0:T(8,128)(2,1)}, f32[1024,128]{1,0:T(8,128)}, f32[1024,128]{1,0:T(8,128)}, f32[16,1024]{1,0:T(8,128)}, bf16[32,1024]{1,0:T(8,128)(2,1)}, /*index=5*/bf16[512,1024]{1,0:T(8,128)(2,1)}) custom-call(bf16[1024,1024]{1,0:T(8,128)(2,1)} %q_ref.3, bf16[1024,1024]{1,0:T(8,128)(2,1)} %do_ref.3, bf16[1024,128]{1,0:T(8,128)(2,1)} %k_ref.3, ...), custom_call_target="tpu_custom_call" | custom-call | tf_op jit(solution)/shard_map/plain/pallas_call | solution.py:243
  15.7 1.7 %collective-permute-start.2 = (bf16[512,1024]{1,0:T(8,128)(2,1)}, bf16[512,1024]{1,0:T(8,128)(2,1)}, u32[]{:S(2)}, u32[]{:S(2)}) collective-permute-start(bf16[512,1024]{1,0:T(8,128)(2,1)} %get-tuple-element.34), channel_id=1, source_target_pairs={{0,8},{8,16},{16,24},{24,32},{32,40},{40,48},{48,56},{56,64},{64,7... | collective-permute-start | bytes 3145736 | tf_op jit(solution)/shard_map/ppermute | solution.py:270
  17.4 0.0 collective-permute-done.kb_ref
  17.4 0.0 copy-start.3
  17.4 0.0 collective-permute-done.1.vb_ref
  17.4 0.0 copy-start.4
  17.4 0.7 copy-done.3
  18.1 0.1 copy-done.4
  18.2 12.7 %rolled.1 = (bf16[1024,1024]{1,0:T(8,128)(2,1)}, bf16[512,256]{1,0:T(8,128)(2,1)}, bf16[512,256]{1,0:T(8,128)(2,1)}, f32[512,256]{1,0:T(8,128)}, bf16[8,48,1536]{2,1,0:T(8,128)(2,1)}) custom-call(bf16[1024,1024]{1,0:T(8,128)(2,1)} %q_ref.3, bf16[1024,1024]{1,0:T(8,128)(2,1)} %do_ref.3, bf16[1024,128]{1,0:T(8,128)(2,1)} %k_ref.3, ...), custom_call_target="tpu_custom_call", output_to_operand_aliasing={{0}: (7, {})} | custom-call | tf_op jit(solution)/shard_map/rolled/pallas_call | solution.py:274
  30.9 0.0 copy-start.2
  30.9 0.0 copy-start
  30.9 5.5 %all-to-all-start = ((bf16[8,48,1536]{2,1,0:T(8,128)(2,1)}), bf16[8,48,1536]{2,1,0:T(8,128)(2,1)S(1)}, u32[]{:S(2)}, u32[]{:S(2)}) async-start(bf16[8,48,1536]{2,1,0:T(8,128)(2,1)} %get-tuple-element.33), calls=%async_computation | async-start | bytes 2359296 | tf_op jit(solution)/shard_map/all_to_all | solution.py:308
  36.4 0.0 collective-permute-start.3
  36.4 6.3 %collective-permute-done.3.back_ref = bf16[512,256]{1,0:T(8,128)(2,1)S(1)} collective-permute-done((bf16[512,256]{1,0:T(8,128)(2,1)}, bf16[512,256]{1,0:T(8,128)(2,1)S(1)}, u32[]{:S(2)}, u32[]{:S(2)}) %collective-permute-start.3) | collective-permute-done | bytes 262176 | tf_op jit(solution)/shard_map/ppermute | solution.py:307
  42.7 0.0 copy-done.2
  42.7 0.0 copy-start.1
  42.7 1.0 %copy-done.1 = f32[512,256]{1,0:T(8,128)S(1)} copy-done((f32[512,256]{1,0:T(8,128)S(1)}, f32[512,256]{1,0:T(8,128)}, u32[]{:S(2)}) %copy-start.1) | copy-done | bytes 524312
  43.8 0.9 %finish.1 = (bf16[1024,128]{1,0:T(8,128)(2,1)}, bf16[1024,128]{1,0:T(8,128)(2,1)}) custom-call(bf16[512,256]{1,0:T(8,128)(2,1)S(1)} %copy-done.2, f32[512,256]{1,0:T(8,128)S(1)} %copy-done.1, bf16[512,256]{1,0:T(8,128)(2,1)S(1)} %collective-permute-done.3.back_ref), custom_call_target="tpu_custom_call" | custom-call | tf_op jit(solution)/shard_map/finish/pallas_call | solution.py:309
  44.7 0.0 collective-permute-done.2.lent_hbm
  44.7 10.5 %all-to-all-done.all_ref = bf16[8,48,1536]{2,1,0:T(8,128)(2,1)S(1)} async-done(((bf16[8,48,1536]{2,1,0:T(8,128)(2,1)}), bf16[8,48,1536]{2,1,0:T(8,128)(2,1)S(1)}, u32[]{:S(2)}, u32[]{:S(2)}) %all-to-all-start) | async-done | bytes 1179680 | tf_op jit(solution)/shard_map/all_to_all | solution.py:308
  55.2 0.0 copy-done
  55.2 2.8 %weights.1 = (f32[56,512]{1,0:T(8,128)S(1)}, f32[56,512]{1,0:T(8,128)S(1)}, bf16[1024,1024]{1,0:T(8,128)(2,1)}, bf16[1024,128]{1,0:T(8,128)(2,1)}) custom-call(bf16[8,48,1536]{2,1,0:T(8,128)(2,1)S(1)} %all-to-all-done.all_ref, bf16[1024,1024]{1,0:T(8,128)(2,1)S(1)} %copy-done, ...), custom_call_target="tpu_custom_call", output_to_operand_aliasing={{2}: (3, {}), {3}: (4, {})} | custom-call | tf_op jit(solution)/shard_map/weights/pallas_call | solution.py:317
  58.1 0.5 collective-permute-start.4
  58.5 1.0 %collective-permute-done.4 = f32[56,512]{1,0:T(8,128)S(1)} collective-permute-done((f32[56,512]{1,0:T(8,128)S(1)}, f32[56,512]{1,0:T(8,128)S(1)}, u32[]{:S(2)}, u32[]{:S(2)}) %collective-permute-start.4) | collective-permute-done | bytes 114720 | tf_op jit(solution)/shard_map/ppermute | solution.py:335
  59.6 15.9 %all_to_all.10 = bf16[8,56,512]{2,1,0:T(8,128)(2,1)S(1)} all-to-all(bf16[8,56,512]{2,1,0:T(8,128)(2,1)S(1)} %broadcast_in_dim.2), channel_id=1, replica_groups={{0,16,32,48,64,80,96,112},{8,24,40,56,72,88,104,120},{1,17,33,49,65,81,..., dimensions={0} | all-to-all | bytes 917504 | tf_op jit(solution)/shard_map/all_to_all | solution.py:337
  75.4 0.1 convert_reduce_fusion.mine_ref
  75.5 1.6 %collective-permute-start.5 = (f32[56,512]{1,0:T(8,128)S(1)}, f32[56,512]{1,0:T(8,128)S(1)}, u32[]{:S(2)}, u32[]{:S(2)}) collective-permute-start(f32[56,512]{1,0:T(8,128)S(1)} %convert_reduce_fusion.mine_ref), channel_id=1, source_target_pairs={{0,8},{8,0},{16,24},{24,16},{32,40},{40,32},{48,56},{56,48},{64,72... | collective-permute-start | bytes 344072 | tf_op jit(solution)/shard_map/ppermute | solution.py:345
  77.1 1.0 %collective-permute-done.5.other_ref = f32[56,512]{1,0:T(8,128)S(1)} collective-permute-done((f32[56,512]{1,0:T(8,128)S(1)}, f32[56,512]{1,0:T(8,128)S(1)}, u32[]{:S(2)}, u32[]{:S(2)}) %collective-permute-start.5) | collective-permute-done | bytes 114720 | tf_op jit(solution)/shard_map/ppermute | solution.py:345
  78.1 0.7 place.1
  (2 shorter events, 0.0 us)
Async XLA Ops:
  0.6 16.7 %collective-permute-start = (bf16[1024,128]{1,0:T(8,128)(2,1)}, bf16[1024,128]{1,0:T(8,128)(2,1)S(1)}, u32[]{:S(2)}, u32[]{:S(2)}) collective-permute-start(bf16[1024,128]{1,0:T(8,128)(2,1)} %k_ref.3), channel_id=1, source_target_pairs={{0,8},{8,16},{16,24},{24,32},{32,40},{40,48},{48,56},{56,64},{64,7... | collective-permute-start | bytes 786440 | tf_op jit(solution)/shard_map/ppermute | solution.py:239
  3.4 14.0 %collective-permute-start.1 = (bf16[1024,128]{1,0:T(8,128)(2,1)}, bf16[1024,128]{1,0:T(8,128)(2,1)S(1)}, u32[]{:S(2)}, u32[]{:S(2)}) collective-permute-start(bf16[1024,128]{1,0:T(8,128)(2,1)} %v_ref.3), channel_id=1, source_target_pairs={{0,8},{8,16},{16,24},{24,32},{32,40},{40,48},{48,56},{56,64},{64,7... | collective-permute-start | bytes 786440 | tf_op jit(solution)/shard_map/ppermute | solution.py:240
  15.7 29.0 %collective-permute-start.2 = (bf16[512,1024]{1,0:T(8,128)(2,1)}, bf16[512,1024]{1,0:T(8,128)(2,1)}, u32[]{:S(2)}, u32[]{:S(2)}) collective-permute-start(bf16[512,1024]{1,0:T(8,128)(2,1)} %get-tuple-element.34), channel_id=1, source_target_pairs={{0,8},{8,16},{16,24},{24,32},{32,40},{40,48},{48,56},{56,64},{64,7... | collective-permute-start | bytes 3145736 | tf_op jit(solution)/shard_map/ppermute | solution.py:270
  17.4 0.7 copy-start.3
  17.4 0.8 copy-start.4
  30.9 11.8 %copy-start.2 = (bf16[512,256]{1,0:T(8,128)(2,1)S(1)}, bf16[512,256]{1,0:T(8,128)(2,1)}, u32[]{:S(2)}) copy-start(bf16[512,256]{1,0:T(8,128)(2,1)} %get-tuple-element.36.top_ref) | copy-start | bytes 786436
  30.9 24.3 %copy-start = (bf16[1024,1024]{1,0:T(8,128)(2,1)S(1)}, bf16[1024,1024]{1,0:T(8,128)(2,1)}, u32[]{:S(2)}) copy-start(bf16[1024,1024]{1,0:T(8,128)(2,1)} %x_ref.1) | copy-start | bytes 6291460
  30.9 24.3 %all-to-all-start = ((bf16[8,48,1536]{2,1,0:T(8,128)(2,1)}), bf16[8,48,1536]{2,1,0:T(8,128)(2,1)S(1)}, u32[]{:S(2)}, u32[]{:S(2)}) async-start(bf16[8,48,1536]{2,1,0:T(8,128)(2,1)} %get-tuple-element.33), calls=%async_computation | async-start | bytes 2359296 | tf_op jit(solution)/shard_map/all_to_all | solution.py:308
  36.4 6.3 %collective-permute-start.3 = (bf16[512,256]{1,0:T(8,128)(2,1)}, bf16[512,256]{1,0:T(8,128)(2,1)S(1)}, u32[]{:S(2)}, u32[]{:S(2)}) collective-permute-start(bf16[512,256]{1,0:T(8,128)(2,1)} %get-tuple-element.38), channel_id=1, source_target_pairs={{0,120},{8,0},{16,8},{24,16},{32,24},{40,32},{48,40},{56,48},{64,5... | collective-permute-start | bytes 786440 | tf_op jit(solution)/shard_map/ppermute | solution.py:307
  42.7 1.0 %copy-start.1 = (f32[512,256]{1,0:T(8,128)S(1)}, f32[512,256]{1,0:T(8,128)}, u32[]{:S(2)}) copy-start(f32[512,256]{1,0:T(8,128)} %get-tuple-element.37.rest_ref) | copy-start | bytes 1572868
  58.1 1.4 %collective-permute-start.4 = (f32[56,512]{1,0:T(8,128)S(1)}, f32[56,512]{1,0:T(8,128)S(1)}, u32[]{:S(2)}, u32[]{:S(2)}) collective-permute-start(f32[56,512]{1,0:T(8,128)S(1)} %get-tuple-element.44), channel_id=1, source_target_pairs={{0,8},{8,0},{16,24},{24,16},{32,40},{40,32},{48,56},{56,48},{64,72... | collective-permute-start | bytes 344072 | tf_op jit(solution)/shard_map/ppermute | solution.py:335
  75.5 2.6 %collective-permute-start.5 = (f32[56,512]{1,0:T(8,128)S(1)}, f32[56,512]{1,0:T(8,128)S(1)}, u32[]{:S(2)}, u32[]{:S(2)}) collective-permute-start(f32[56,512]{1,0:T(8,128)S(1)} %convert_reduce_fusion.mine_ref), channel_id=1, source_target_pairs={{0,8},{8,0},{16,24},{24,16},{32,40},{40,32},{48,56},{56,48},{64,72... | collective-permute-start | bytes 344072 | tf_op jit(solution)/shard_map/ppermute | solution.py:345

commit v10 on v9

--- a/solution.py
+++ b/solution.py
@@ -14,6 +14,7 @@
 HALF = 512
 WIDTH = 1024
 BLOCK = 256
+BLOCKS = [slice(at, at + BLOCK) for at in range(0, ROWS, BLOCK)]
 SCALE = 1.0 / math.sqrt(HD)
 FOLDED = SCALE * 1.4426950408889634
 F32 = jnp.float32
@@ -183,10 +184,11 @@
 def weights_kernel(
     all_ref, x_ref, lent_hbm, dq_hbm, gv_hbm, keep_ref, give_ref, _, __, lent_ref, dq_ref, gv_ref, sems
 ):
-    copies = []
-    for n, (source, target) in enumerate(((lent_hbm, lent_ref), (gv_hbm, gv_ref), (dq_hbm, dq_ref))):
-        copies.append(pltpu.make_async_copy(source, target, sems.at[n]))
-        copies[n].start()
+    moves = [(dq_hbm.at[block], dq_ref.at[block]) for block in BLOCKS]
+    moves += [(lent_hbm, lent_ref), (gv_hbm, gv_ref)]
+    copies = [pltpu.make_async_copy(*move, sems.at[n]) for n, move in enumerate(moves)]
+    for copy in copies:
+        copy.start()
     total = all_ref[0].astype(F32)
     for peer in range(1, all_ref.shape[0]):
         total = total + all_ref[peer].astype(F32)
@@ -195,20 +197,23 @@
     bq = jnp.concatenate([rows[1][:, ROWS:], rows[2][:, :HALF]], 1)
     both = jnp.concatenate([bq, rows[2][:, HALF:]], 0)
     down = jnp.dot(both, x_ref[...], preferred_element_type=F32)
-    copies[0].wait()
+    up_q = jnp.zeros((RANK, WIDTH), F32)
+    for block, copy in zip(BLOCKS, copies):
+        copy.wait()
+        up_q = up_q + jnp.dot(rows[0][:, block], dq_ref[block], preferred_element_type=F32)
+    copies[-2].wait()
     lent = jnp.dot(rows[0][:, ROWS:], lent_ref[...], preferred_element_type=F32)
-    copies[1].wait()
+    copies[-1].wait()
     up_v = jnp.dot(rows[1][:, :ROWS], gv_ref[...], preferred_element_type=F32)
-    copies[2].wait()
-    up_q = jnp.dot(rows[0][:, :ROWS], dq_ref[...], preferred_element_type=F32)
     down_q, down_v = down[:RANK], down[RANK:] + lent
 
     even = lax.rem(lax.axis_index("seq"), 2) == 0
     for ref, left in ((keep_ref, even), (give_ref, jnp.logical_not(even))):
         for n, wide in enumerate((down_q, down_v, up_q)):
-            ref[n * RANK : (n + 1) * RANK] = jnp.where(left, wide[:, :HALF], wide[:, HALF:])
-        ref[3 * RANK :, :HD] = jnp.where(left, up_v[:8], up_v[8:])
-        ref[3 * RANK :, HD:] = jnp.zeros((8, HALF - HD), F32)
+            ref[n * RANK : (n + 1) * RANK] = jnp.where(left, wide[:, :HALF], wide[:, HALF:]).astype(ref.dtype)
+        tail = jnp.concatenate([jnp.where(left, up_v[:8], up_v[8:]), jnp.zeros((8, HD), F32)], 0)
+        ref[3 * RANK :, :HD] = tail.astype(ref.dtype)
+        ref[3 * RANK :, HD:] = jnp.zeros((RANK, HALF - HD), ref.dtype)
 
 
 def place_kernel(mine_ref, other_ref, qd_ref, qu_ref, vd_ref, vu_ref):
@@ -218,8 +223,8 @@
     for ref, at in ((qd_ref, 0), (vd_ref, RANK), (qu_ref, 2 * RANK)):
         ref[:, :HALF] = left[at : at + RANK]
         ref[:, HALF:] = right[at : at + RANK]
-    vu_ref[:8] = left[3 * RANK :, :HD]
-    vu_ref[8:] = right[3 * RANK :, :HD]
+    vu_ref[:8] = left[3 * RANK : 3 * RANK + 8, :HD]
+    vu_ref[8:] = right[3 * RANK : 3 * RANK + 8, :HD]
 
 
 def whole(*shape):
@@ -312,27 +317,27 @@
         compiler_params=SMALL,
         name="finish",
     )(top, rest, back)
-    part_rows = 3 * RANK + 8
+    part_rows = 4 * RANK
     inside = pl.BlockSpec(memory_space=pltpu.VMEM)
     keep, give, dq, grad_value = pl.pallas_call(
         weights_kernel,
         in_specs=[inside] * 2 + [untouched] * 3,
         out_specs=[inside] * 2 + [untouched] * 2,
-        out_shape=[struct(part_rows, HALF)] * 2
+        out_shape=[struct(part_rows, HALF), struct(part_rows, HALF, dtype=BF16)]
         + [struct(ROWS, WIDTH, dtype=BF16), struct(ROWS, HD, dtype=BF16)],
         input_output_aliases={3: 2, 4: 3},
         scratch_shapes=[
             pltpu.VMEM((HALF, WIDTH), BF16),
             pltpu.VMEM((ROWS, WIDTH), BF16),
             pltpu.VMEM((ROWS, HD), BF16),
-            pltpu.SemaphoreType.DMA((3,)),
+            pltpu.SemaphoreType.DMA((6,)),
         ],
         compiler_params=SMALL,
         name="weights",
     )(gathered, x, lent, dq, grad_value)
 
     swap = [(s, s ^ 1) for s in range(seq)]
-    part = (keep + lax.ppermute(give, "seq", swap)).astype(BF16)
+    part = (keep + lax.ppermute(give, "seq", swap).astype(F32)).astype(BF16)
     chips = seq // 2
     parts = lax.all_to_all(
         jnp.broadcast_to(part[None], (chips,) + part.shape),

time: 79.9 us -> 80.2 us (level)
  blocking collectives: 15.9 us -> 16.9 us
    all_to_all x1, blocking collectives: 15.9 us -> 16.9 us  [on_device(): lax.all_to_all(jnp.broadcast_to(part[None], (chips,) + part.shape), 'seq'...]
where the time goes in v10:
time: 80.2 us; the launch traced here: 79.1 us
  Pallas kernels  28.9 us (36%)
  waiting for transfers between devices  18.7 us (23%)
  blocking collectives  16.9 us (21%)
  starting transfers between devices  11.8 us (15%)
  local copies, waits for them, and re-layouts  1.86 us (2%)
    all_to_all x1, blocking collectives, on_device(): lax.all_to_all(jnp.broadcast_to(part[None], (chips,) + part.shape), 'seq'...  16.9 us
    pallas_call x1, Pallas kernels, on_device(): pl.pallas_call(rolled_kernel, grid=(2,), in_specs=[pl.BlockSpec((ROWS, 2...  12.7 us
    pallas_call x1, Pallas kernels, on_device(): pl.pallas_call(plain_kernel, grid=(2,), in_specs=[pl.BlockSpec((ROWS, 2 *...  12.2 us
    all_to_all x1, waiting for transfers between devices, on_device(): gathered = lax.all_to_all(share, 'tensor', 0, 0)  10.5 us
    ppermute x1, waiting for transfers between devices, on_device(): back = lax.ppermute(back, 'seq', [(s, (s - 1) % seq) for s in range(seq)])  6.29 us
    all_to_all x1, starting transfers between devices, on_device(): gathered = lax.all_to_all(share, 'tensor', 0, 0)  5.52 us
    ppermute x1, starting transfers between devices, on_device(): borrowed_key = lax.ppermute(key, 'seq', onward)  2.76 us
    pallas_call x1, Pallas kernels, on_device(): pl.pallas_call(weights_kernel, in_specs=[inside] * 2 + [untouched] * 3, o...  2.43 us
  transfers between devices with their start and end apart: 7, of which 4 were waited for; matrix products, arithmetic and copies ran while one was open for 0% of the time, Pallas kernels for 33%

profile of v10, /device:TPU:1, one launch (start us, length us, event | category | flops | bytes accessed | tf_op | source)
XLA Modules:
  0.0 79.1 jit_solution(8443137217953965825)
XLA Ops:
  0.6 2.8 %collective-permute-start = (bf16[1024,128]{1,0:T(8,128)(2,1)}, bf16[1024,128]{1,0:T(8,128)(2,1)S(1)}, u32[]{:S(2)}, u32[]{:S(2)}) collective-permute-start(bf16[1024,128]{1,0:T(8,128)(2,1)} %k_ref.3), channel_id=1, source_target_pairs={{0,8},{8,16},{16,24},{24,32},{32,40},{40,48},{48,56},{56,64},{64,7... | collective-permute-start | bytes 786440 | tf_op jit(solution)/shard_map/ppermute | solution.py:244
  3.4 0.1 collective-permute-start.1
  3.5 12.2 %plain.1 = (bf16[1024,1024]{1,0:T(8,128)(2,1)}, f32[1024,128]{1,0:T(8,128)}, f32[1024,128]{1,0:T(8,128)}, f32[16,1024]{1,0:T(8,128)}, bf16[32,1024]{1,0:T(8,128)(2,1)}, /*index=5*/bf16[512,1024]{1,0:T(8,128)(2,1)}) custom-call(bf16[1024,1024]{1,0:T(8,128)(2,1)} %q_ref.3, bf16[1024,1024]{1,0:T(8,128)(2,1)} %do_ref.3, bf16[1024,128]{1,0:T(8,128)(2,1)} %k_ref.3, ...), custom_call_target="tpu_custom_call" | custom-call | tf_op jit(solution)/shard_map/plain/pallas_call | solution.py:248
  15.7 1.7 %collective-permute-start.2 = (bf16[512,1024]{1,0:T(8,128)(2,1)}, bf16[512,1024]{1,0:T(8,128)(2,1)}, u32[]{:S(2)}, u32[]{:S(2)}) collective-permute-start(bf16[512,1024]{1,0:T(8,128)(2,1)} %get-tuple-element.34), channel_id=1, source_target_pairs={{0,8},{8,16},{16,24},{24,32},{32,40},{40,48},{48,56},{56,64},{64,7... | collective-permute-start | bytes 3145736 | tf_op jit(solution)/shard_map/ppermute | solution.py:275
  17.4 0.0 collective-permute-done.kb_ref
  17.4 0.0 copy-start.3
  17.4 0.0 collective-permute-done.1.vb_ref
  17.4 0.0 copy-start.4
  17.4 0.7 copy-done.3
  18.1 0.1 copy-done.4
  18.2 12.7 %rolled.1 = (bf16[1024,1024]{1,0:T(8,128)(2,1)}, bf16[512,256]{1,0:T(8,128)(2,1)}, bf16[512,256]{1,0:T(8,128)(2,1)}, f32[512,256]{1,0:T(8,128)}, bf16[8,48,1536]{2,1,0:T(8,128)(2,1)}) custom-call(bf16[1024,1024]{1,0:T(8,128)(2,1)} %q_ref.3, bf16[1024,1024]{1,0:T(8,128)(2,1)} %do_ref.3, bf16[1024,128]{1,0:T(8,128)(2,1)} %k_ref.3, ...), custom_call_target="tpu_custom_call", output_to_operand_aliasing={{0}: (7, {})} | custom-call | tf_op jit(solution)/shard_map/rolled/pallas_call | solution.py:279
  30.9 0.0 copy-start.2
  30.9 0.0 copy-start
  30.9 5.5 %all-to-all-start = ((bf16[8,48,1536]{2,1,0:T(8,128)(2,1)}), bf16[8,48,1536]{2,1,0:T(8,128)(2,1)S(1)}, u32[]{:S(2)}, u32[]{:S(2)}) async-start(bf16[8,48,1536]{2,1,0:T(8,128)(2,1)} %get-tuple-element.33), calls=%async_computation | async-start | bytes 2359296 | tf_op jit(solution)/shard_map/all_to_all | solution.py:313
  36.4 0.0 collective-permute-start.3
  36.4 6.3 %collective-permute-done.3.back_ref = bf16[512,256]{1,0:T(8,128)(2,1)S(1)} collective-permute-done((bf16[512,256]{1,0:T(8,128)(2,1)}, bf16[512,256]{1,0:T(8,128)(2,1)S(1)}, u32[]{:S(2)}, u32[]{:S(2)}) %collective-permute-start.3) | collective-permute-done | bytes 262176 | tf_op jit(solution)/shard_map/ppermute | solution.py:312
  42.7 0.0 copy-done.2
  42.7 0.0 copy-start.1
  42.7 1.0 %copy-done.1 = f32[512,256]{1,0:T(8,128)S(1)} copy-done((f32[512,256]{1,0:T(8,128)S(1)}, f32[512,256]{1,0:T(8,128)}, u32[]{:S(2)}) %copy-start.1) | copy-done | bytes 524312
  43.8 0.9 %finish.1 = (bf16[1024,128]{1,0:T(8,128)(2,1)}, bf16[1024,128]{1,0:T(8,128)(2,1)}) custom-call(bf16[512,256]{1,0:T(8,128)(2,1)S(1)} %copy-done.2, f32[512,256]{1,0:T(8,128)S(1)} %copy-done.1, bf16[512,256]{1,0:T(8,128)(2,1)S(1)} %collective-permute-done.3.back_ref), custom_call_target="tpu_custom_call" | custom-call | tf_op jit(solution)/shard_map/finish/pallas_call | solution.py:314
  44.7 0.0 collective-permute-done.2.lent_hbm
  44.7 10.5 %all-to-all-done.all_ref = bf16[8,48,1536]{2,1,0:T(8,128)(2,1)S(1)} async-done(((bf16[8,48,1536]{2,1,0:T(8,128)(2,1)}), bf16[8,48,1536]{2,1,0:T(8,128)(2,1)S(1)}, u32[]{:S(2)}, u32[]{:S(2)}) %all-to-all-start) | async-done | bytes 1179680 | tf_op jit(solution)/shard_map/all_to_all | solution.py:313
  55.2 0.0 copy-done
  55.2 2.4 %weights.1 = (f32[64,512]{1,0:T(8,128)S(1)}, bf16[64,512]{1,0:T(8,128)(2,1)S(1)}, bf16[1024,1024]{1,0:T(8,128)(2,1)}, bf16[1024,128]{1,0:T(8,128)(2,1)}) custom-call(bf16[8,48,1536]{2,1,0:T(8,128)(2,1)S(1)} %all-to-all-done.all_ref, bf16[1024,1024]{1,0:T(8,128)(2,1)S(1)} %copy-done, ...), custom_call_target="tpu_custom_call", output_to_operand_aliasing={{2}: (3, {}), {3}: (4, {})} | custom-call | tf_op jit(solution)/shard_map/weights/pallas_call | solution.py:322
  57.6 0.5 collective-permute-start.4
  58.1 0.9 %collective-permute-done.4 = bf16[64,512]{1,0:T(8,128)(2,1)S(1)} collective-permute-done((bf16[64,512]{1,0:T(8,128)(2,1)S(1)}, bf16[64,512]{1,0:T(8,128)(2,1)S(1)}, u32[]{:S(2)}, u32[]{:S(2)}) %collective-permute-start.4) | collective-permute-done | bytes 65568 | tf_op jit(solution)/shard_map/ppermute | solution.py:340
  59.1 16.9 %all_to_all.10 = bf16[8,64,512]{2,1,0:T(8,128)(2,1)S(1)} all-to-all(bf16[8,64,512]{2,1,0:T(8,128)(2,1)S(1)} %broadcast_in_dim.2), channel_id=1, replica_groups={{0,16,32,48,64,80,96,112},{8,24,40,56,72,88,104,120},{1,17,33,49,65,81,..., dimensions={0} | all-to-all | bytes 1048576 | tf_op jit(solution)/shard_map/all_to_all | solution.py:342
  76.0 0.1 convert_reduce_fusion.mine_ref
  76.1 1.3 %collective-permute-start.5 = (f32[64,512]{1,0:T(8,128)S(1)}, f32[64,512]{1,0:T(8,128)S(1)}, u32[]{:S(2)}, u32[]{:S(2)}) collective-permute-start(f32[64,512]{1,0:T(8,128)S(1)} %convert_reduce_fusion.mine_ref), channel_id=1, source_target_pairs={{0,8},{8,0},{16,24},{24,16},{32,40},{40,32},{48,56},{56,48},{64,72... | collective-permute-start | bytes 393224 | tf_op jit(solution)/shard_map/ppermute | solution.py:350
  77.4 1.0 %collective-permute-done.5.other_ref = f32[64,512]{1,0:T(8,128)S(1)} collective-permute-done((f32[64,512]{1,0:T(8,128)S(1)}, f32[64,512]{1,0:T(8,128)S(1)}, u32[]{:S(2)}, u32[]{:S(2)}) %collective-permute-start.5) | collective-permute-done | bytes 131104 | tf_op jit(solution)/shard_map/ppermute | solution.py:350
  78.4 0.7 place.1
  (2 shorter events, 0.1 us)
Async XLA Ops:
  0.6 16.7 %collective-permute-start = (bf16[1024,128]{1,0:T(8,128)(2,1)}, bf16[1024,128]{1,0:T(8,128)(2,1)S(1)}, u32[]{:S(2)}, u32[]{:S(2)}) collective-permute-start(bf16[1024,128]{1,0:T(8,128)(2,1)} %k_ref.3), channel_id=1, source_target_pairs={{0,8},{8,16},{16,24},{24,32},{32,40},{40,48},{48,56},{56,64},{64,7... | collective-permute-start | bytes 786440 | tf_op jit(solution)/shard_map/ppermute | solution.py:244
  3.4 14.0 %collective-permute-start.1 = (bf16[1024,128]{1,0:T(8,128)(2,1)}, bf16[1024,128]{1,0:T(8,128)(2,1)S(1)}, u32[]{:S(2)}, u32[]{:S(2)}) collective-permute-start(bf16[1024,128]{1,0:T(8,128)(2,1)} %v_ref.3), channel_id=1, source_target_pairs={{0,8},{8,16},{16,24},{24,32},{32,40},{40,48},{48,56},{56,64},{64,7... | collective-permute-start | bytes 786440 | tf_op jit(solution)/shard_map/ppermute | solution.py:245
  15.7 29.0 %collective-permute-start.2 = (bf16[512,1024]{1,0:T(8,128)(2,1)}, bf16[512,1024]{1,0:T(8,128)(2,1)}, u32[]{:S(2)}, u32[]{:S(2)}) collective-permute-start(bf16[512,1024]{1,0:T(8,128)(2,1)} %get-tuple-element.34), channel_id=1, source_target_pairs={{0,8},{8,16},{16,24},{24,32},{32,40},{40,48},{48,56},{56,64},{64,7... | collective-permute-start | bytes 3145736 | tf_op jit(solution)/shard_map/ppermute | solution.py:275
  17.4 0.7 copy-start.3
  17.4 0.8 copy-start.4
  30.9 11.8 %copy-start.2 = (bf16[512,256]{1,0:T(8,128)(2,1)S(1)}, bf16[512,256]{1,0:T(8,128)(2,1)}, u32[]{:S(2)}) copy-start(bf16[512,256]{1,0:T(8,128)(2,1)} %get-tuple-element.36.top_ref) | copy-start | bytes 786436
  30.9 24.3 %copy-start = (bf16[1024,1024]{1,0:T(8,128)(2,1)S(1)}, bf16[1024,1024]{1,0:T(8,128)(2,1)}, u32[]{:S(2)}) copy-start(bf16[1024,1024]{1,0:T(8,128)(2,1)} %x_ref.1) | copy-start | bytes 6291460
  30.9 24.3 %all-to-all-start = ((bf16[8,48,1536]{2,1,0:T(8,128)(2,1)}), bf16[8,48,1536]{2,1,0:T(8,128)(2,1)S(1)}, u32[]{:S(2)}, u32[]{:S(2)}) async-start(bf16[8,48,1536]{2,1,0:T(8,128)(2,1)} %get-tuple-element.33), calls=%async_computation | async-start | bytes 2359296 | tf_op jit(solution)/shard_map/all_to_all | solution.py:313
  36.4 6.3 %collective-permute-start.3 = (bf16[512,256]{1,0:T(8,128)(2,1)}, bf16[512,256]{1,0:T(8,128)(2,1)S(1)}, u32[]{:S(2)}, u32[]{:S(2)}) collective-permute-start(bf16[512,256]{1,0:T(8,128)(2,1)} %get-tuple-element.38), channel_id=1, source_target_pairs={{0,120},{8,0},{16,8},{24,16},{32,24},{40,32},{48,40},{56,48},{64,5... | collective-permute-start | bytes 786440 | tf_op jit(solution)/shard_map/ppermute | solution.py:312
  42.7 1.0 %copy-start.1 = (f32[512,256]{1,0:T(8,128)S(1)}, f32[512,256]{1,0:T(8,128)}, u32[]{:S(2)}) copy-start(f32[512,256]{1,0:T(8,128)} %get-tuple-element.37.rest_ref) | copy-start | bytes 1572868
  57.6 1.4 %collective-permute-start.4 = (bf16[64,512]{1,0:T(8,128)(2,1)S(1)}, bf16[64,512]{1,0:T(8,128)(2,1)S(1)}, u32[]{:S(2)}, u32[]{:S(2)}) collective-permute-start(bf16[64,512]{1,0:T(8,128)(2,1)S(1)} %get-tuple-element.44), channel_id=1, source_target_pairs={{0,8},{8,0},{16,24},{24,16},{32,40},{40,32},{48,56},{56,48},{64,72... | collective-permute-start | bytes 196616 | tf_op jit(solution)/shard_map/ppermute | solution.py:340
  76.1 2.3 %collective-permute-start.5 = (f32[64,512]{1,0:T(8,128)S(1)}, f32[64,512]{1,0:T(8,128)S(1)}, u32[]{:S(2)}, u32[]{:S(2)}) collective-permute-start(f32[64,512]{1,0:T(8,128)S(1)} %convert_reduce_fusion.mine_ref), channel_id=1, source_target_pairs={{0,8},{8,0},{16,24},{24,16},{32,40},{40,32},{48,56},{56,48},{64,72... | collective-permute-start | bytes 393224 | tf_op jit(solution)/shard_map/ppermute | solution.py:350
